TPU v7x, 128 devices: a whole 4x4x4 slice. The times are simulated.
128 devices in a mesh: row: 8 (over x, core), col: 16 (over y, z).
Axes of the slice: x: 4, y: 4, z: 4, core: 2. Of those that a mesh axis runs over, the one named last changes fastest.
Arguments:
- inputs: bfloat16 [1024, 6144], P('row', 'col'), may hold values from -6 to 6
- upstream: bfloat16 [1024, 6144], P('row', 'col'), may hold values from -6 to 6
- preact: bfloat16 [1024, 24576], P('col', 'row'), may hold values from -6 to 6
- bias_in: float32 [24576], P('row'), may hold values from -3 to 3
- w_in: bfloat16 [6144, 24576], P('col', 'row'), may hold values from -0.078125 to 0.078125
- w_out: bfloat16 [24576, 6144], P('row', 'col'), may hold values from -0.0390625 to 0.0390625
- lengths: int32 [8], replicated, may hold values from 1 to 256, 1024 in all
Outputs:
- grad_inputs: bfloat16 [1024, 6144], P('row', 'col')
- grad_w_in: bfloat16 [6144, 24576], P('col', 'row')
- grad_w_out: bfloat16 [24576, 6144], P('row', 'col')
All inputs are finite; a program needn't handle non-finite values.
Results may differ from a plain program's by a relative error of at most 0.0058.
Values may be sent and summed in bfloat16 or wider, within the bound.
No kernel may reach another device: no remote copies, remote signals or barrier semaphores. Data moves between devices by JAX's collectives and lax.ppermute only.
A program may use at most 128 MiB of HBM per device.

v0:
```python
import jax
import jax.numpy as jnp
from jax import lax
from jax.sharding import PartitionSpec as P

IMAGES = 8


def token_weights(lengths, first_row, count, rows_total):
    ends = jnp.cumsum(lengths)
    starts = ends - lengths
    position = first_row + jnp.arange(count, dtype=jnp.int32)
    member = (position[:, None] >= starts[None, :]) & (position[:, None] < ends[None, :])
    size = jnp.sum(jnp.where(member, lengths[None, :], 0), axis=1).astype(jnp.float32)
    return jnp.sqrt(rows_total / IMAGES / size)


def gelu_parts(pre):
    normal_cdf = 0.5 * (1.0 + lax.erf(pre * 0.7071067811865476))
    density = jnp.exp(-0.5 * pre * pre) * 0.3989422804014327
    return (pre * normal_cdf, normal_cdf + pre * density)


def contract_last(left, right):
    return lax.dot_general(
        left, right, (((1,), (1,)), ((), ())), preferred_element_type=jnp.float32
    )


def contract_first(left, right):
    return lax.dot_general(
        left, right, (((0,), (0,)), ((), ())), preferred_element_type=jnp.float32
    )


def shards(inputs, upstream, preact, bias_in, w_in, w_out, lengths):
    tile_rows = inputs.shape[0]
    rows_total = tile_rows * lax.axis_size("row")
    first_row = lax.axis_index("row") * tile_rows
    weight = token_weights(lengths, first_row, tile_rows, rows_total)
    scaled = (upstream.astype(jnp.float32) * weight[:, None]).astype(jnp.bfloat16)
    inputs_all, scaled_all = (
        lax.all_gather(inputs, "row", axis=0, tiled=True),
        lax.all_gather(scaled, "row", axis=0, tiled=True),
    )
    piece = scaled_all
    back = lax.psum_scatter(contract_last(piece, w_out), "col", scatter_dimension=0, tiled=True)
    pre = preact.astype(jnp.float32) + bias_in[None, :]
    value, slope = gelu_parts(pre)
    act = value.astype(jnp.bfloat16)
    grad_pre = (back * slope).astype(jnp.bfloat16)
    act_all, grad_all = (
        lax.all_gather(act, "col", axis=0, tiled=True),
        lax.all_gather(grad_pre, "col", axis=0, tiled=True),
    )
    factor = rows_total ** (-0.5)
    grad_w_out = (contract_first(act_all, scaled_all) * factor).astype(jnp.bfloat16)
    grad_w_in = (contract_first(inputs_all, grad_all) * factor).astype(jnp.bfloat16)
    piece = grad_all
    grad_inputs = lax.psum_scatter(
        contract_last(piece, w_in), "row", scatter_dimension=0, tiled=True
    ).astype(jnp.bfloat16)
    return (grad_inputs, grad_w_in, grad_w_out)


def solution(mesh):
    placed = (
        P("row", "col"),
        P("row", "col"),
        P("col", "row"),
        P("row"),
        P("col", "row"),
        P("row", "col"),
        P(),
    )
    return jax.shard_map(
        shards,
        mesh=mesh,
        in_specs=placed,
        out_specs=(P("row", "col"), P("col", "row"), P("row", "col")),
        check_vma=False,
    )
```

profile of v0, /device:TPU:24, one launch (start us, length us, event | category | flops | bytes accessed | tf_op | source)
XLA Modules:
  0.0 296.4 jit_solution(15071982755292869556)
XLA Ops:
  7.2 0.0 reduce-scatter.3.cloned.1.call-start
  7.2 1.0 reduce-window.8
  8.2 0.7 bitcast_subtract_fusion
  8.9 0.7 select_reduce_fusion
  9.6 1.0 multiply_convert_fusion.3
  10.6 13.7 %all_gather.12 = bf16[1024,384]{1,0:T(8,128)(2,1)S(1)} all-gather(bf16[128,384]{1,0:T(8,128)(2,1)S(1)} %multiply_convert_fusion.3), channel_id=1, replica_groups=mesh['row'=8,'col'=16] {'row'}, dimensions={0}, use_global_device_ids=true | all-gather | bytes 884736 | tf_op jit(solution)/shard_map/all_gather | solution.py:44
  24.4 6.4 %fusion.7 = f32[1024,3072]{1,0:T(8,128)} fusion(bf16[1024,384]{1,0:T(8,128)(2,1)S(1)} %all_gather.12, bf16[3072,384]{1,0:T(8,128)(2,1)S(1)} %copy-done), kind=kOutput, calls=%fused_computation.18 | convolution fusion | flops 2415919104 | bytes 15728640 | tf_op jit(solution)/shard_map/dot_general | solution.py:25
  30.7 0.0 reduce-scatter.3.cloned.1.call-update
  30.7 0.0 all-gather.3.cloned.1.call-start
  30.8 95.9 %reduce-scatter.3.cloned.1.call-done = f32[64,3072]{1,0:T(8,128)} async-done(((f32[1024,3072]{1,0:T(8,128)}), f32[64,3072]{1,0:T(8,128)}) %reduce-scatter.3.cloned.1.call-update) | async-done | bytes 786448 | tf_op jit(solution)/shard_map/reduce_scatter | solution.py:47
  126.7 2.4 multiply_convert_fusion.2
  129.2 0.0 all-gather.5.cloned.1.call-start
  129.2 0.7 all-gather.5.cloned.1.call-update
  129.9 0.0 reduce-scatter.5.cloned.1.call-start
  130.0 60.6 %all-gather.3.cloned.1.call-done = bf16[1024,3072]{1,0:T(8,128)(2,1)} async-done(((bf16[64,3072]{1,0:T(8,128)(2,1)}), bf16[1024,3072]{1,0:T(8,128)(2,1)}) %all-gather.3.cloned.1.call-update) | async-done | bytes 6291472 | tf_op jit(solution)/shard_map/all_gather | solution.py:54
  190.5 8.1 %fusion.8 = f32[1024,384]{1,0:T(8,128)} fusion(bf16[1024,3072]{1,0:T(8,128)(2,1)} %all-gather.3.cloned.1.call-done, bf16[384,3072]{1,0:T(8,128)(2,1)} %param.11), kind=kOutput, calls=%fused_computation.19 | convolution fusion | flops 2415919104 | bytes 10223616 | tf_op jit(solution)/shard_map/dot_general | solution.py:25
  198.6 0.0 reduce-scatter.5.cloned.1.call-update
  198.7 13.9 %all_gather.14 = bf16[1024,384]{1,0:T(8,128)(2,1)S(1)} all-gather(bf16[128,384]{1,0:T(8,128)(2,1)S(1)} %copy-done.2), channel_id=1, replica_groups=mesh['row'=8,'col'=16] {'row'}, dimensions={0}, use_global_device_ids=true | all-gather | bytes 884736 | tf_op jit(solution)/shard_map/all_gather | solution.py:43
  212.5 7.7 %fusion = bf16[384,3072]{0,1:T(8,128)(2,1)} fusion(bf16[1024,3072]{1,0:T(8,128)(2,1)} %all-gather.3.cloned.1.call-done, bf16[1024,384]{1,0:T(8,128)(2,1)S(1)} %all_gather.14), kind=kOutput, calls=%fused_computation.2 | convolution fusion | flops 2418278400 | bytes 9437184 | tf_op jit(solution)/shard_map/dot_general | solution.py:31
  220.2 4.3 %copy.11 = bf16[384,3072]{1,0:T(8,128)(2,1)} copy(bf16[384,3072]{0,1:T(8,128)(2,1)} %fusion) | data formatting | bytes 4718592
  224.5 29.3 %all-gather.5.cloned.1.call-done = bf16[1024,3072]{1,0:T(8,128)(2,1)} async-done(((bf16[64,3072]{1,0:T(8,128)(2,1)}), bf16[1024,3072]{1,0:T(8,128)(2,1)}) %all-gather.5.cloned.1.call-update) | async-done | bytes 6291472 | tf_op jit(solution)/shard_map/all_gather | solution.py:53
  253.8 7.7 %multiply_convert_fusion = bf16[3072,384]{1,0:T(8,128)(2,1)} fusion(bf16[1024,3072]{1,0:T(8,128)(2,1)} %all-gather.5.cloned.1.call-done, bf16[1024,384]{1,0:T(8,128)(2,1)S(1)} %all_gather.12), kind=kOutput, calls=%fused_computation | convolution fusion | flops 2418278400 | bytes 9437184 | tf_op jit(solution)/shard_map/dot_general | solution.py:31
  261.4 26.9 %reduce-scatter.5.cloned.1.call-done = f32[128,384]{1,0:T(8,128)} async-done(((f32[1024,384]{1,0:T(8,128)}), f32[128,384]{1,0:T(8,128)}) %reduce-scatter.5.cloned.1.call-update) | async-done | bytes 196624 | tf_op jit(solution)/shard_map/reduce_scatter | solution.py:60
  288.3 1.6 convert_element_type.39
  (11 shorter events, 0.1 us)
Async XLA Ops:
  7.2 17.2 %copy-start = (bf16[3072,384]{1,0:T(8,128)(2,1)S(1)}, bf16[3072,384]{1,0:T(8,128)(2,1)}, u32[]{:S(2)}) copy-start(bf16[3072,384]{1,0:T(8,128)(2,1)} %param.12) | copy-start | bytes 7077892
  7.2 119.5 %reduce-scatter.3.cloned.1.call-start = ((), (), s32[]{:S(2)}) async-start(), calls=%async_computation.2 | async-start | bytes 13369344 | tf_op jit(solution)/shard_map/reduce_scatter | solution.py:47
  30.7 96.0 %copy-start.1 = (bf16[64,3072]{1,0:T(8,128)(2,1)S(1)}, bf16[64,3072]{1,0:T(8,128)(2,1)}, u32[]{:S(2)}) copy-start(bf16[64,3072]{1,0:T(8,128)(2,1)} %param.9) | copy-start | bytes 1179652
  30.7 96.0 %copy-start.3 = (f32[3072]{0:T(1024)S(1)}, f32[3072]{0:T(1024)}, u32[]{:S(2)}) copy-start(f32[3072]{0:T(1024)} %param.10) | copy-start | bytes 36868
  30.7 159.8 %all-gather.3.cloned.1.call-start = ((), (), s32[]{:S(2)}) async-start(), calls=%async_computation.3 | async-start | bytes 6684672 | tf_op jit(solution)/shard_map/all_gather | solution.py:54
  129.2 124.6 %all-gather.5.cloned.1.call-start = ((), (), s32[]{:S(2)}) async-start(), calls=%async_computation.5 | async-start | bytes 6684672 | tf_op jit(solution)/shard_map/all_gather | solution.py:53
  129.9 68.8 %copy-start.2 = (bf16[128,384]{1,0:T(8,128)(2,1)S(1)}, bf16[128,384]{1,0:T(8,128)(2,1)}, u32[]{:S(2)}) copy-start(bf16[128,384]{1,0:T(8,128)(2,1)} %param.7) | copy-start | bytes 294916
  129.9 158.4 %reduce-scatter.5.cloned.1.call-start = ((), (), s32[]{:S(2)}) async-start(), calls=%async_computation.4 | async-start | bytes 1769472 | tf_op jit(solution)/shard_map/reduce_scatter | solution.py:60
Sparse Core Ops, SparseCore 0:
  30.9 95.8 reduce-scatter.2
  129.5 61.0 all-gather.2
  192.7 60.9 all-gather.4
  256.0 32.2 reduce-scatter.4
where the time goes:
time: 297 us; the launch traced here: 296 us
  waiting for transfers between devices  213 us (72%)
  matrix products  29.8 us (10%)
  blocking collectives  27.6 us (9%)
  between operations  13.8 us (5%)
  other arithmetic  7.37 us (2%)
  local copies, waits for them, and re-layouts  4.29 us (1%)
    reduce_scatter x1, waiting for transfers between devices, shards(): lax.psum_scatter(contract_last(piece, w_out), 'col', scatter_dimension=0,...  95.9 us
    all_gather x1, waiting for transfers between devices, shards(): lax.all_gather(grad_pre, 'col', axis=0, tiled=True)  60.6 us
    all_gather x1, waiting for transfers between devices, shards(): lax.all_gather(act, 'col', axis=0, tiled=True)  29.3 us
    reduce_scatter x1, waiting for transfers between devices, shards(): lax.psum_scatter(contract_last(piece, w_in), 'row', scatter_dimension=0,...  26.9 us
    dot_general x2, matrix products, contract_first(): lax.dot_general(left, right, (((0,), (0,)), ((), ())), preferred_element_...  15.3 us
    dot_general x2, matrix products, contract_last(): lax.dot_general(left, right, (((1,), (1,)), ((), ())), preferred_element_...  14.5 us
    all_gather x1, blocking collectives, shards(): lax.all_gather(inputs, 'row', axis=0, tiled=True)  13.9 us
    all_gather x1, blocking collectives, shards(): lax.all_gather(scaled, 'row', axis=0, tiled=True)  13.7 us
  transfers between devices with their start and end apart: 4, of which 4 were waited for; matrix products, arithmetic and copies ran while one was open for 9% of the time, Pallas kernels for 0%

commit v1 on v0

v1 whole, which is shorter than its diff:
```python
import functools

import jax
import jax.numpy as jnp
from jax import lax
from jax.experimental import pallas as pl
from jax.experimental.pallas import tpu as pltpu
from jax.sharding import PartitionSpec as P

IMAGES = 8
SIDE = 4
BLOCK = 64
WIDE = 512
SPLIT = 1536
F32, BF16 = jnp.float32, jnp.bfloat16
NT = (((1,), (1,)), ((), ()))
NN = (((1,), (0,)), ((), ()))


def dot(left, right, dims):
    return lax.dot_general(left, right, dims, preferred_element_type=F32)


def gelu_parts(pre):
    normal_cdf = 0.5 * (1.0 + lax.erf(pre * 0.7071067811865476))
    density = jnp.exp(-0.5 * pre * pre) * 0.3989422804014327
    return (pre * normal_cdf, normal_cdf + pre * density)


def move_y(a, by):
    pairs = [(4 * y + z, 4 * ((y + by) % SIDE) + z) for y in range(SIDE) for z in range(SIDE)]
    return lax.ppermute(a, "col", pairs)


def move_z(a, by):
    pairs = [(4 * y + z, 4 * y + (z + by) % SIDE) for y in range(SIDE) for z in range(SIDE)]
    return lax.ppermute(a, "col", pairs)


def move_x(a, by):
    pairs = [(2 * x + c, 2 * ((x + by) % SIDE) + c) for x in range(SIDE) for c in range(2)]
    return lax.ppermute(a, "row", pairs)


def swap_core(a):
    return lax.ppermute(a, "row", [(2 * x + c, 2 * x + 1 - c) for x in range(SIDE) for c in range(2)])


def call(kernel, outs, operands, name, grid=(), in_specs=None, out_specs=None, flops=0, scratch=(), alias=None):
    moved = sum(o.size * o.dtype.itemsize for o in operands) + sum(o.size * o.dtype.itemsize for o in outs)
    return pl.pallas_call(
        kernel,
        out_shape=outs,
        grid=grid,
        in_specs=in_specs,
        out_specs=out_specs,
        scratch_shapes=scratch,
        input_output_aliases=alias or {},
        name=name,
        cost_estimate=pl.CostEstimate(flops=flops, bytes_accessed=moved, transcendentals=0),
        compiler_params=pltpu.CompilerParams(vmem_limit_bytes=48 * 2**20),
    )(*operands)


SMEM = pl.BlockSpec(memory_space=pltpu.SMEM)
VMEM = pl.BlockSpec(memory_space=pltpu.VMEM)


def shape(dims, kind):
    return jax.ShapeDtypeStruct(dims, kind)


def whole(dims):
    return pl.BlockSpec(dims, lambda i: (0, 0))


def gathered_block(place, mine, other, y, z):
    start = pl.multiple_of(((y - place[2]) & 3) * 128 + (z % 2) * BLOCK, BLOCK)
    rows = pl.ds(start, BLOCK)
    return jnp.where(place[3] == z // 2, mine[rows, :], other[rows, :])


def relative(place, y, z):
    return (y - place[0]) & 3, (z - place[1]) & 3


def rows_of(major, minor):
    return pl.ds(pl.multiple_of((major * SIDE + minor) * BLOCK, BLOCK), BLOCK)


def scaled_kernel(place, lengths, mine, other, by_z, by_y, flipped, plain):
    for y in range(SIDE):
        for z in range(SIDE):
            block = gathered_block(place, mine, other, y, z)
            position = (y * SIDE + z) * BLOCK + lax.broadcasted_iota(jnp.int32, block.shape, 0)
            size = jnp.zeros(block.shape, jnp.int32)
            start = 0
            for k in range(IMAGES):
                end = start + lengths[k]
                size = jnp.where((position >= start) & (position < end), lengths[k], size)
                start = end
            weight = jnp.sqrt(128.0 / size.astype(F32))
            block = (block.astype(F32) * weight).astype(BF16)
            dy, dz = relative(place, y, z)
            by_z[rows_of(dz, dy), :] = block
            by_y[rows_of(dy, dz), :] = block
            plain[pl.ds((y * SIDE + z) * BLOCK, BLOCK), :] = block
    flipped[...] = plain[...].T


def inputs_kernel(place, mine, other, by_z, by_y, first, second):
    for y in range(SIDE):
        for z in range(SIDE):
            block = gathered_block(place, mine, other, y, z)
            dy, dz = relative(place, y, z)
            first[rows_of(dz, dy), :] = block
            second[rows_of(dy, dz), :] = block
    by_z[...] = first[...].T
    by_y[...] = second[...].T


def first_kernel(scaled, w, plus, minus):
    both = dot(scaled[384:896, :], w[...], NT).astype(BF16)
    plus[...] = both[:256]
    minus[...] = both[256:]


def second_kernel(scaled, w, from_low, from_high, plus, minus):
    plus[...] = (dot(scaled[256:384, :], w[...], NT) + from_low[...].astype(F32)).astype(BF16)
    minus[...] = (dot(scaled[896:1024, :], w[...], NT) + from_high[...].astype(F32)).astype(BF16)


def third_kernel(scaled, w, low_own, high_own, low_sum, high_sum, own, one, two, three):
    total = dot(scaled[0:256, :], w[...], NT)
    upper = total[:128] + high_own[...].astype(F32) + low_sum[...].astype(F32)
    lower = total[128:] + low_own[...].astype(F32) + high_sum[...].astype(F32)
    own[...] = upper[:64]
    one[...] = upper[64:].astype(BF16)
    two[...] = lower[:64].astype(BF16)
    three[...] = lower[64:].astype(BF16)


def slope_kernel(own, one, two, three, slope, grad):
    back = own[...] + one[...].astype(F32) + two[...].astype(F32) + three[...].astype(F32)
    grad[...] = (back * slope[...]).astype(BF16)


def reduce_group(scaled, w_out, slope, first, width, major, minor):
    steps, skip = width // WIDE, first // WIDE
    depth = scaled.shape[1]
    s_spec = whole(scaled.shape)
    w_spec = pl.BlockSpec((WIDE, depth), lambda i: (i + skip, 0))

    def part(rows, at=0):
        return pl.BlockSpec((rows, WIDE), lambda i: (at, i))

    plus, minus = call(
        first_kernel,
        [shape((256, width), BF16)] * 2,
        (scaled, w_out),
        "back_first",
        (steps,),
        [s_spec, w_spec],
        [part(256)] * 2,
        2 * 512 * depth * width,
    )
    low, high = major(plus, 1), major(minus, -1)
    plus, minus = call(
        second_kernel,
        [shape((128, width), BF16)] * 2,
        (scaled, w_out, low, high),
        "back_second",
        (steps,),
        [s_spec, w_spec, part(128, 1), part(128, 0)],
        [part(128)] * 2,
        2 * 256 * depth * width,
    )
    low_sum, high_sum = major(plus, 1), major(minus, -1)
    own, one, two, three = call(
        third_kernel,
        [shape((64, width), F32)] + [shape((64, width), BF16)] * 3,
        (scaled, w_out, low, high, low_sum, high_sum),
        "back_third",
        (steps,),
        [s_spec, w_spec, part(128, 0), part(128, 1), part(128), part(128)],
        [part(64)] * 4,
        2 * 256 * depth * width,
    )
    one, two, three = minor(one, 1), minor(two, 2), minor(three, 3)
    return call(
        slope_kernel,
        [shape((64, width), BF16)],
        (own, one, two, three, slope),
        "grad_pre",
        (steps,),
        [part(64)] * 4 + [pl.BlockSpec((64, WIDE), lambda i: (0, i + skip))],
        [part(64)],
    )[0]


def gather_group(grad, major, minor):
    near = jnp.concatenate([grad, minor(grad, -1), minor(grad, -2), minor(grad, -3)], axis=0)
    low, high = major(near, 1), major(near, -1)
    return near, high, major(low[:128], 1), major(high[128:], -1), low


def all_rows(pieces):
    return jnp.concatenate([piece[...] for piece in pieces], axis=0)


def piece_specs():
    return [pl.BlockSpec((rows, WIDE), lambda i: (0, i)) for rows in (256, 256, 128, 128, 256)]


def grad_inputs_kernel(one, two, three, four, five, w, total):
    part = dot(all_rows((one, two, three, four, five)), w[...], NT)

    @pl.when(pl.program_id(0) == 0)
    def _():
        total[...] = part

    @pl.when(pl.program_id(0) > 0)
    def _():
        total[...] += part


def grad_inputs_group(pieces, w_in, first):
    width, depth = pieces[0].shape[1], w_in.shape[0]
    skip = first // WIDE
    return call(
        grad_inputs_kernel,
        [shape((1024, depth), F32)],
        (*pieces, w_in),
        "grad_inputs",
        (width // WIDE,),
        piece_specs() + [pl.BlockSpec((depth, WIDE), lambda i: (0, i + skip))],
        [whole((1024, depth))],
        2 * 1024 * depth * width,
    )[0]


def join_kernel(place, by_z, by_y, send, keep):
    for far in range(SIDE):
        for z in range(2):
            for out, core in ((keep, place[3]), (send, 1 - place[3])):
                dy, dz = relative(place, place[2] + far, 2 * core + z)
                block = by_z[rows_of(dz, dy), :] + by_y[rows_of(dy, dz), :]
                out[pl.ds(far * 128 + z * BLOCK, BLOCK), :] = block.astype(out.dtype)


def grad_w_in_kernel(factor, flipped, one, two, three, four, five, *rest):
    rest[-1][...] = (dot(flipped[...], all_rows((one, two, three, four, five)), NN) * factor).astype(BF16)


def grad_w_in_group(flipped, pieces, first, factor, total, so_far):
    width, depth = pieces[0].shape[1], flipped.shape[0]
    skip = first // WIDE
    operands = (flipped, *pieces) + (() if so_far is None else (so_far,))
    return call(
        functools.partial(grad_w_in_kernel, factor),
        [shape((depth, total), BF16)],
        operands,
        "grad_w_in",
        (width // WIDE,),
        [whole(flipped.shape)] + piece_specs() + [pl.BlockSpec(memory_space=pl.ANY)] * (len(operands) - 6),
        [pl.BlockSpec((depth, WIDE), lambda i: (0, i + skip))],
        2 * 1024 * depth * width,
        alias=None if so_far is None else {6: 0},
    )[0]


def grad_w_out_kernel(factor, flipped, act, out):
    out[...] = (dot(flipped[...], act[...], NN) * factor).T.astype(BF16)


def grad_w_out_all(flipped, act, factor):
    depth, width = flipped.shape[0], act.shape[1]
    return call(
        functools.partial(grad_w_out_kernel, factor),
        [shape((width, depth), BF16)],
        (flipped, act),
        "grad_w_out",
        (width // WIDE,),
        [whole(flipped.shape), pl.BlockSpec((1024, WIDE), lambda i: (0, i))],
        [pl.BlockSpec((WIDE, depth), lambda i: (i, 0))],
        2 * 1024 * depth * width,
    )[0]


def row_gather(a):
    mine = jnp.concatenate([a, move_x(a, -1), move_x(a, -2), move_x(a, -3)], axis=0)
    return mine, swap_core(mine)


def shards(inputs, upstream, preact, bias_in, w_in, w_out, lengths):
    col, row = lax.axis_index("col"), lax.axis_index("row")
    place = jnp.stack([col // SIDE, col % SIDE, row // 2, row % 2]).astype(jnp.int32)
    depth, hidden = w_in.shape
    factor = 1024 ** (-0.5)

    up_mine, up_other = row_gather(upstream)
    scaled_z, scaled_y, scaled_flipped = call(
        scaled_kernel,
        [shape((1024, depth), BF16)] * 2 + [shape((depth, 1024), BF16)],
        (place, lengths, up_mine, up_other),
        "scaled",
        in_specs=[SMEM, SMEM, VMEM, VMEM],
        out_specs=[VMEM] * 3,
        scratch=[pltpu.VMEM((1024, depth), BF16)],
    )
    pre = preact.astype(F32) + bias_in[None, :]
    value, slope = gelu_parts(pre)
    act, slope = lax.optimization_barrier((value.astype(BF16), slope))
    act_all = lax.all_gather(act, "col", axis=0, tiled=True)

    grad_z = reduce_group(scaled_z, w_out, slope, 0, SPLIT, move_z, move_y)
    grad_y = reduce_group(scaled_y, w_out, slope, SPLIT, hidden - SPLIT, move_y, move_z)
    pieces_z = gather_group(grad_z, move_z, move_y)
    pieces_y = gather_group(grad_y, move_y, move_z)

    in_mine, in_other = row_gather(inputs)
    in_z, in_y = call(
        inputs_kernel,
        [shape((depth, 1024), BF16)] * 2,
        (place, in_mine, in_other),
        "inputs",
        in_specs=[SMEM, VMEM, VMEM],
        out_specs=[VMEM] * 2,
        scratch=[pltpu.VMEM((1024, depth), BF16)] * 2,
    )

    total_z = grad_inputs_group(pieces_z, w_in, 0)
    total_y = grad_inputs_group(pieces_y, w_in, SPLIT)
    send, keep = call(
        join_kernel,
        [shape((512, depth), BF16), shape((512, depth), F32)],
        (place, total_z, total_y),
        "join",
        in_specs=[SMEM, VMEM, VMEM],
        out_specs=[VMEM] * 2,
    )
    keep = keep + swap_core(send).astype(F32)
    parts = [keep[128 * k : 128 * (k + 1)] for k in range(SIDE)]
    grad_inputs = parts[0]
    for k in range(1, SIDE):
        grad_inputs = grad_inputs + move_x(parts[k].astype(BF16), k).astype(F32)

    grad_w_in = grad_w_in_group(in_z, pieces_z, 0, factor, hidden, None)
    grad_w_in = grad_w_in_group(in_y, pieces_y, SPLIT, factor, hidden, grad_w_in)
    grad_w_out = grad_w_out_all(scaled_flipped, act_all, factor)
    return (grad_inputs.astype(BF16), grad_w_in, grad_w_out)


def solution(mesh):
    placed = (
        P("row", "col"),
        P("row", "col"),
        P("col", "row"),
        P("row"),
        P("col", "row"),
        P("row", "col"),
        P(),
    )
    return jax.shard_map(
        shards,
        mesh=mesh,
        in_specs=placed,
        out_specs=(P("row", "col"), P("col", "row"), P("row", "col")),
        check_vma=False,
    )
```

time: 297 us -> 184 us (0.62)
  waiting for transfers between devices: 213 us -> 73.5 us
  starting transfers between devices: 0.16 us -> 53.8 us
  Pallas kernels: 0 us -> 36.7 us
  matrix products: 29.8 us -> 0 us
  blocking collectives: 27.6 us -> 0 us
  other arithmetic: 7.37 us -> 3.26 us
  local copies, waits for them, and re-layouts: 4.29 us -> 1.22 us
    reduce_scatter x2 -> x0, waiting for transfers between devices: 123 us -> none  [the longest x1 95.9 us: shards(): lax.psum_scatter(contract_last(piece, w_out), 'col', scatter_dimension=0,...]
    all_gather x2 -> x1, waiting for transfers between devices: 89.9 us -> 0.01 us  [shards(): act_all = lax.all_gather(act, 'col', axis=0, tiled=True)]
    ppermute x0 -> x40, waiting for transfers between devices: none -> 73.5 us  [the longest x14 44 us: move_z(): return lax.ppermute(a, 'col', pairs)]
    ppermute x0 -> x40, starting transfers between devices: none -> 53.8 us  [the longest x14 25.4 us: move_z(): return lax.ppermute(a, 'col', pairs)]
    pallas_call x0 -> x16, Pallas kernels: none -> 36.7 us  [call(): pl.pallas_call(kernel, out_shape=outs, grid=grid, in_specs=in_specs, out_...]
    dot_general x4 -> x0, matrix products: 29.8 us -> none  [the longest x2 15.3 us: contract_first(): lax.dot_general(left, right, (((0,), (0,)), ((), ())), preferred_element_...]
    all_gather x2 -> x0, blocking collectives: 27.6 us -> none  [the longest x1 13.9 us: shards(): lax.all_gather(inputs, 'row', axis=0, tiled=True)]
    convert_element_type x3 -> x1, other arithmetic: 4.98 us -> 0.69 us  [shards(): return (grad_inputs.astype(BF16), grad_w_in, grad_w_out)]
  transfers between devices with their start and end apart: 4 -> 41, of which waited for: 4 -> 20; matrix products, arithmetic and copies ran while one was open for 9% -> 1% of each run, Pallas kernels for 0% -> 16%
where the time goes in v1:
time: 184 us; the launch traced here: 183 us
  waiting for transfers between devices  73.5 us (40%)
  starting transfers between devices  53.8 us (29%)
  Pallas kernels  36.7 us (20%)
  between operations  14.4 us (8%)
  other arithmetic  3.26 us (2%)
    ppermute x14, waiting for transfers between devices, move_z(): return lax.ppermute(a, 'col', pairs)  44 us
    pallas_call x16, Pallas kernels, call(): pl.pallas_call(kernel, out_shape=outs, grid=grid, in_specs=in_specs, out_...  36.7 us
    ppermute x14, starting transfers between devices, move_z(): return lax.ppermute(a, 'col', pairs)  25.4 us
    ppermute x14, starting transfers between devices, move_y(): return lax.ppermute(a, 'col', pairs)  16.4 us
    ppermute x9, waiting for transfers between devices, move_x(): return lax.ppermute(a, 'row', pairs)  16.1 us
    ppermute x14, waiting for transfers between devices, move_y(): return lax.ppermute(a, 'col', pairs)  11.6 us
    ppermute x9, starting transfers between devices, move_x(): return lax.ppermute(a, 'row', pairs)  11.2 us
  transfers between devices with their start and end apart: 41, of which 20 were waited for; matrix products, arithmetic and copies ran while one was open for 1% of the time, Pallas kernels for 16%

profile of v1, /device:TPU:24, one launch (start us, length us, event | category | flops | bytes accessed | tf_op | source)
XLA Modules:
  0.0 182.9 jit_solution(16322757982803838252)
XLA Ops:
  7.2 2.3 %fusion.3 = (f32[64,3072]{1,0:T(8,128)S(1)}, bf16[64,3072]{1,0:T(8,128)(2,1)}) fusion(bf16[64,3072]{1,0:T(8,128)(2,1)} %param.9, f32[3072]{0:T(1024)} %param.10), kind=kLoop, calls=%fused_computation.4 | loop fusion | flops 2359296 | bytes 1585152 | tf_op jit(solution)/shard_map/add | solution.py:27
  9.5 2.8 %collective-permute-start = (bf16[128,384]{1,0:T(8,128)(2,1)}, bf16[128,384]{1,0:T(8,128)(2,1)S(1)}, u32[]{:S(2)}, u32[]{:S(2)}) collective-permute-start(bf16[128,384]{1,0:T(8,128)(2,1)} %param.8), channel_id=1, source_target_pairs={{0,96},{16,112},{32,0},{48,16},{64,32},{80,48},{96,64},{112,80},{1... | collective-permute-start | bytes 294920 | tf_op jit(solution)/shard_map/ppermute | solution.py:42
  16.9 2.5 %collective-permute-done.1 = bf16[128,384]{1,0:T(8,128)(2,1)S(1)} collective-permute-done((bf16[128,384]{1,0:T(8,128)(2,1)}, bf16[128,384]{1,0:T(8,128)(2,1)S(1)}, u32[]{:S(2)}, u32[]{:S(2)}) %collective-permute-start.1) | collective-permute-done | bytes 98336 | tf_op jit(solution)/shard_map/ppermute | solution.py:42
  22.4 2.1 %scaled.1 = (bf16[1024,384]{1,0:T(8,128)(2,1)S(1)}, bf16[1024,384]{1,0:T(8,128)(2,1)S(1)}, bf16[384,1024]{1,0:T(8,128)(2,1)S(1)}) custom-call(s32[4]{0:T(128)S(1)} %pad_add_fusion.place, s32[8]{0:T(128)S(1)} %copy-done.3, bf16[512,384]{1,0:T(8,128)(2,1)S(1)} %constant_dynamic-update-slice_fusion.mine, bf16[512,384]{1,0:T(8,128)(2,1)} %collective-permute-done.3.other), custom_call_target="tpu_custom_call" | custom-call | bytes 3145776 | tf_op jit(solution)/shard_map/scaled/pallas_call | solution.py:51
  28.0 2.2 %collective-permute-start.5 = (bf16[256,1536]{1,0:T(8,128)(2,1)S(1)}, bf16[256,1536]{1,0:T(8,128)(2,1)S(1)}, u32[]{:S(2)}, u32[]{:S(2)}) collective-permute-start(bf16[256,1536]{1,0:T(8,128)(2,1)S(1)} %get-tuple-element.30), channel_id=1, source_target_pairs={{0,3},{1,0},{2,1},{3,2},{4,7},{5,4},{6,5},{7,6},{8,11},{9,8},{10,9... | collective-permute-start | bytes 2359304 | tf_op jit(solution)/shard_map/ppermute | solution.py:37
  33.8 17.2 %collective-permute-done.4.from_low.low_own = bf16[256,1536]{1,0:T(8,128)(2,1)S(1)} collective-permute-done((bf16[256,1536]{1,0:T(8,128)(2,1)S(1)}, bf16[256,1536]{1,0:T(8,128)(2,1)S(1)}, u32[]{:S(2)}, u32[]{:S(2)}) %collective-permute-start.4) | collective-permute-done | bytes 786464 | tf_op jit(solution)/shard_map/ppermute | solution.py:37
  54.9 2.1 %collective-permute-start.7 = (bf16[128,1536]{1,0:T(8,128)(2,1)S(1)}, bf16[128,1536]{1,0:T(8,128)(2,1)S(1)}, u32[]{:S(2)}, u32[]{:S(2)}) collective-permute-start(bf16[128,1536]{1,0:T(8,128)(2,1)S(1)} %get-tuple-element.32), channel_id=1, source_target_pairs={{0,3},{1,0},{2,1},{3,2},{4,7},{5,4},{6,5},{7,6},{8,11},{9,8},{10,9... | collective-permute-start | bytes 1179656 | tf_op jit(solution)/shard_map/ppermute | solution.py:37
  62.3 12.5 %collective-permute-done.6.low_sum = bf16[128,1536]{1,0:T(8,128)(2,1)S(1)} collective-permute-done((bf16[128,1536]{1,0:T(8,128)(2,1)S(1)}, bf16[128,1536]{1,0:T(8,128)(2,1)S(1)}, u32[]{:S(2)}, u32[]{:S(2)}) %collective-permute-start.6) | collective-permute-done | bytes 393248 | tf_op jit(solution)/shard_map/ppermute | solution.py:37
  74.8 2.8 %back_third.2 = (f32[64,1536]{1,0:T(8,128)S(1)}, bf16[64,1536]{1,0:T(8,128)(2,1)S(1)}, bf16[64,1536]{1,0:T(8,128)(2,1)S(1)}, bf16[64,1536]{1,0:T(8,128)(2,1)S(1)}) custom-call(bf16[1024,384]{1,0:T(8,128)(2,1)S(1)} %get-tuple-element.28.scaled, bf16[3072,384]{1,0:T(8,128)(2,1)} %w.14, bf16[256,1536]{1,0:T(8,128)(2,1)S(1)} %collective-permute-done.4.from_low.low_own, ...), custom_call_target="tpu_custom_call" | custom-call | flops 301989888 | bytes 6488064 | tf_op jit(solution)/shard_map/back_third/pallas_call | solution.py:51
  80.8 2.8 %back_third.3 = (f32[64,1536]{1,0:T(8,128)S(1)}, bf16[64,1536]{1,0:T(8,128)(2,1)S(1)}, bf16[64,1536]{1,0:T(8,128)(2,1)S(1)}, bf16[64,1536]{1,0:T(8,128)(2,1)S(1)}) custom-call(bf16[1024,384]{1,0:T(8,128)(2,1)S(1)} %get-tuple-element.38.scaled, bf16[3072,384]{1,0:T(8,128)(2,1)} %w.14, bf16[256,1536]{1,0:T(8,128)(2,1)S(1)} %collective-permute-done.18.from_low.low_own, ...), custom_call_target="tpu_custom_call" | custom-call | flops 301989888 | bytes 6488064 | tf_op jit(solution)/shard_map/back_third/pallas_call | solution.py:51
  84.9 3.4 %collective-permute-start.23 = (bf16[64,1536]{1,0:T(8,128)(2,1)S(1)}, bf16[64,1536]{1,0:T(8,128)(2,1)S(1)}, u32[]{:S(2)}, u32[]{:S(2)}) collective-permute-start(bf16[64,1536]{1,0:T(8,128)(2,1)S(1)} %get-tuple-element.45), channel_id=1, source_target_pairs={{0,2},{1,3},{2,0},{3,1},{4,6},{5,7},{6,4},{7,5},{8,10},{9,11},{10,... | collective-permute-start | bytes 589832 | tf_op jit(solution)/shard_map/ppermute | solution.py:37
  89.6 2.7 %collective-permute-start.24 = (bf16[64,1536]{1,0:T(8,128)(2,1)S(1)}, bf16[64,1536]{1,0:T(8,128)(2,1)S(1)}, u32[]{:S(2)}, u32[]{:S(2)}) collective-permute-start(bf16[64,1536]{1,0:T(8,128)(2,1)S(1)} %get-tuple-element.46), channel_id=1, source_target_pairs={{0,3},{1,0},{2,1},{3,2},{4,7},{5,4},{6,5},{7,6},{8,11},{9,8},{10,9... | collective-permute-start | bytes 589832 | tf_op jit(solution)/shard_map/ppermute | solution.py:37
  92.3 2.9 %collective-permute-done.10.three = bf16[64,1536]{1,0:T(8,128)(2,1)S(1)} collective-permute-done((bf16[64,1536]{1,0:T(8,128)(2,1)S(1)}, bf16[64,1536]{1,0:T(8,128)(2,1)S(1)}, u32[]{:S(2)}, u32[]{:S(2)}) %collective-permute-start.10) | collective-permute-done | bytes 196640 | tf_op jit(solution)/shard_map/ppermute | solution.py:32
  98.8 2.8 %collective-permute-start.26 = (bf16[64,1536]{1,0:T(8,128)(2,1)S(1)}, bf16[64,1536]{1,0:T(8,128)(2,1)S(1)}, u32[]{:S(2)}, u32[]{:S(2)}) collective-permute-start(bf16[64,1536]{1,0:T(8,128)(2,1)S(1)} %grad_pre.3), channel_id=1, source_target_pairs={{0,2},{1,3},{2,0},{3,1},{4,6},{5,7},{6,4},{7,5},{8,10},{9,11},{10,... | collective-permute-start | bytes 589832 | tf_op jit(solution)/shard_map/ppermute | solution.py:37
  106.2 2.3 %collective-permute-done.11 = bf16[64,1536]{1,0:T(8,128)(2,1)S(1)} collective-permute-done((bf16[64,1536]{1,0:T(8,128)(2,1)S(1)}, bf16[64,1536]{1,0:T(8,128)(2,1)S(1)}, u32[]{:S(2)}, u32[]{:S(2)}) %collective-permute-start.11) | collective-permute-done | bytes 196640 | tf_op jit(solution)/shard_map/ppermute | solution.py:32
  110.7 4.0 %collective-permute-start.29 = (bf16[256,1536]{1,0:T(8,128)(2,1)S(1)}, bf16[256,1536]{1,0:T(8,128)(2,1)S(1)}, u32[]{:S(2)}, u32[]{:S(2)}) collective-permute-start(bf16[256,1536]{1,0:T(8,128)(2,1)S(1)} %pad_maximum_fusion.1.one), channel_id=1, source_target_pairs={{0,4},{1,5},{2,6},{3,7},{4,8},{5,9},{6,10},{7,11},{8,12},{9,13},{1... | collective-permute-start | bytes 2359304 | tf_op jit(solution)/shard_map/ppermute | solution.py:32
  117.0 13.4 %collective-permute-done.15.five = bf16[256,1536]{1,0:T(8,128)(2,1)S(1)} collective-permute-done((bf16[256,1536]{1,0:T(8,128)(2,1)S(1)}, bf16[256,1536]{1,0:T(8,128)(2,1)S(1)}, u32[]{:S(2)}, u32[]{:S(2)}) %collective-permute-start.15) | collective-permute-done | bytes 786464 | tf_op jit(solution)/shard_map/ppermute | solution.py:37
  130.6 3.3 %collective-permute-start.17 = (bf16[128,1536]{1,0:T(8,128)(2,1)S(1)}, bf16[128,1536]{1,0:T(8,128)(2,1)S(1)}, u32[]{:S(2)}, u32[]{:S(2)}) collective-permute-start(bf16[128,1536]{1,0:T(8,128)(2,1)S(1)} %slice.36), channel_id=1, source_target_pairs={{0,3},{1,0},{2,1},{3,2},{4,7},{5,4},{6,5},{7,6},{8,11},{9,8},{10,9... | collective-permute-start | bytes 1179656 | tf_op jit(solution)/shard_map/ppermute | solution.py:37
  140.5 5.4 %collective-permute-done.38 = bf16[128,384]{1,0:T(8,128)(2,1)S(1)} collective-permute-done((bf16[128,384]{1,0:T(8,128)(2,1)S(1)}, bf16[128,384]{1,0:T(8,128)(2,1)S(1)}, u32[]{:S(2)}, u32[]{:S(2)}) %collective-permute-start.38) | collective-permute-done | bytes 98336 | tf_op jit(solution)/shard_map/ppermute | solution.py:42
  146.1 3.9 %grad_inputs.2.by_z = f32[1024,384]{1,0:T(8,128)S(1)} custom-call(bf16[256,1536]{1,0:T(8,128)(2,1)S(1)} %pad_maximum_fusion.one, bf16[256,1536]{1,0:T(8,128)(2,1)S(1)} %collective-permute-done.14.two, bf16[128,1536]{1,0:T(8,128)(2,1)S(1)} %collective-permute-done.16.three, bf16[128,1536]{1,0:T(8,128)(2,1)S(1)} %collective-permute-done.17.four, ...), custom_call_target="tpu_custom_call" | custom-call | flops 1207959552 | bytes 7077888 | tf_op jit(solution)/shard_map/grad_inputs/pallas_call | solution.py:51
  150.0 3.9 %grad_inputs.3.by_y = f32[1024,384]{1,0:T(8,128)S(1)} custom-call(bf16[256,1536]{1,0:T(8,128)(2,1)S(1)} %pad_maximum_fusion.1.one, bf16[256,1536]{1,0:T(8,128)(2,1)S(1)} %collective-permute-done.28.two, bf16[128,1536]{1,0:T(8,128)(2,1)S(1)} %collective-permute-done.30.three, bf16[128,1536]{1,0:T(8,128)(2,1)S(1)} %collective-permute-done.31.four, ...), custom_call_target="tpu_custom_call" | custom-call | flops 1207959552 | bytes 7077888 | tf_op jit(solution)/shard_map/grad_inputs/pallas_call | solution.py:51
  156.3 2.9 %grad_w_in.2.rest_0_ = bf16[384,3072]{1,0:T(8,128)(2,1)} custom-call(bf16[384,1024]{1,0:T(8,128)(2,1)S(1)} %get-tuple-element.50.flipped, bf16[256,1536]{1,0:T(8,128)(2,1)S(1)} %pad_maximum_fusion.one, bf16[256,1536]{1,0:T(8,128)(2,1)S(1)} %collective-permute-done.14.two, bf16[128,1536]{1,0:T(8,128)(2,1)S(1)} %collective-permute-done.16.three, ...), custom_call_target="tpu_custom_call" | custom-call | flops 1207959552 | bytes 6291456 | tf_op jit(solution)/shard_map/grad_w_in/pallas_call | solution.py:51
  161.7 2.9 %grad_w_in.3 = bf16[384,3072]{1,0:T(8,128)(2,1)} custom-call(bf16[384,1024]{1,0:T(8,128)(2,1)S(1)} %get-tuple-element.49.flipped, bf16[256,1536]{1,0:T(8,128)(2,1)S(1)} %pad_maximum_fusion.1.one, bf16[256,1536]{1,0:T(8,128)(2,1)S(1)} %collective-permute-done.28.two, ...), custom_call_target="tpu_custom_call", output_to_operand_aliasing={{}: (6, {})} | custom-call | flops 1207959552 | bytes 8650752 | tf_op jit(solution)/shard_map/grad_w_in/pallas_call | solution.py:51
  168.6 7.5 %grad_w_out.1 = bf16[3072,384]{1,0:T(8,128)(2,1)} custom-call(bf16[384,1024]{1,0:T(8,128)(2,1)S(1)} %copy-done.2, bf16[1024,3072]{1,0:T(8,128)(2,1)} %all-gather.2.cloned.1.call-done.act), custom_call_target="tpu_custom_call" | custom-call | flops 2415919104 | bytes 9437184 | tf_op jit(solution)/shard_map/grad_w_out/pallas_call | solution.py:51
  (104 shorter events, 58.2 us)
Async XLA Ops:
  7.2 161.4 %all-gather.2.cloned.1.call-start = ((), (), s32[]{:S(2)}) async-start(), calls=%async_computation | async-start | bytes 6684672 | tf_op jit(solution)/shard_map/all_gather | solution.py:314
  26.0 25.0 %collective-permute-start.4 = (bf16[256,1536]{1,0:T(8,128)(2,1)S(1)}, bf16[256,1536]{1,0:T(8,128)(2,1)S(1)}, u32[]{:S(2)}, u32[]{:S(2)}) collective-permute-start(bf16[256,1536]{1,0:T(8,128)(2,1)S(1)} %get-tuple-element.29), channel_id=1, source_target_pairs={{0,1},{1,2},{2,3},{3,0},{4,5},{5,6},{6,7},{7,4},{8,9},{9,10},{10,1... | collective-permute-start | bytes 2359304 | tf_op jit(solution)/shard_map/ppermute | solution.py:37
  28.0 23.9 %collective-permute-start.5 = (bf16[256,1536]{1,0:T(8,128)(2,1)S(1)}, bf16[256,1536]{1,0:T(8,128)(2,1)S(1)}, u32[]{:S(2)}, u32[]{:S(2)}) collective-permute-start(bf16[256,1536]{1,0:T(8,128)(2,1)S(1)} %get-tuple-element.30), channel_id=1, source_target_pairs={{0,3},{1,0},{2,1},{3,2},{4,7},{5,4},{6,5},{7,6},{8,11},{9,8},{10,9... | collective-permute-start | bytes 2359304 | tf_op jit(solution)/shard_map/ppermute | solution.py:37
  31.7 25.3 %collective-permute-start.18 = (bf16[256,1536]{1,0:T(8,128)(2,1)S(1)}, bf16[256,1536]{1,0:T(8,128)(2,1)S(1)}, u32[]{:S(2)}, u32[]{:S(2)}) collective-permute-start(bf16[256,1536]{1,0:T(8,128)(2,1)S(1)} %get-tuple-element.39), channel_id=1, source_target_pairs={{0,4},{1,5},{2,6},{3,7},{4,8},{5,9},{6,10},{7,11},{8,12},{9,13},{1... | collective-permute-start | bytes 2359304 | tf_op jit(solution)/shard_map/ppermute | solution.py:32
  32.0 26.9 %collective-permute-start.19 = (bf16[256,1536]{1,0:T(8,128)(2,1)S(1)}, bf16[256,1536]{1,0:T(8,128)(2,1)S(1)}, u32[]{:S(2)}, u32[]{:S(2)}) collective-permute-start(bf16[256,1536]{1,0:T(8,128)(2,1)S(1)} %get-tuple-element.40), channel_id=1, source_target_pairs={{0,12},{1,13},{2,14},{3,15},{4,0},{5,1},{6,2},{7,3},{8,4},{9,5},{1... | collective-permute-start | bytes 2359304 | tf_op jit(solution)/shard_map/ppermute | solution.py:32
  53.2 21.6 %collective-permute-start.6 = (bf16[128,1536]{1,0:T(8,128)(2,1)S(1)}, bf16[128,1536]{1,0:T(8,128)(2,1)S(1)}, u32[]{:S(2)}, u32[]{:S(2)}) collective-permute-start(bf16[128,1536]{1,0:T(8,128)(2,1)S(1)} %get-tuple-element.31), channel_id=1, source_target_pairs={{0,1},{1,2},{2,3},{3,0},{4,5},{5,6},{6,7},{7,4},{8,9},{9,10},{10,1... | collective-permute-start | bytes 1179656 | tf_op jit(solution)/shard_map/ppermute | solution.py:37
  54.9 19.9 %collective-permute-start.7 = (bf16[128,1536]{1,0:T(8,128)(2,1)S(1)}, bf16[128,1536]{1,0:T(8,128)(2,1)S(1)}, u32[]{:S(2)}, u32[]{:S(2)}) collective-permute-start(bf16[128,1536]{1,0:T(8,128)(2,1)S(1)} %get-tuple-element.32), channel_id=1, source_target_pairs={{0,3},{1,0},{2,1},{3,2},{4,7},{5,4},{6,5},{7,6},{8,11},{9,8},{10,9... | collective-permute-start | bytes 1179656 | tf_op jit(solution)/shard_map/ppermute | solution.py:37
  60.2 20.5 %collective-permute-start.20 = (bf16[128,1536]{1,0:T(8,128)(2,1)S(1)}, bf16[128,1536]{1,0:T(8,128)(2,1)S(1)}, u32[]{:S(2)}, u32[]{:S(2)}) collective-permute-start(bf16[128,1536]{1,0:T(8,128)(2,1)S(1)} %get-tuple-element.41), channel_id=1, source_target_pairs={{0,4},{1,5},{2,6},{3,7},{4,8},{5,9},{6,10},{7,11},{8,12},{9,13},{1... | collective-permute-start | bytes 1179656 | tf_op jit(solution)/shard_map/ppermute | solution.py:32
  60.3 20.5 %collective-permute-start.21 = (bf16[128,1536]{1,0:T(8,128)(2,1)S(1)}, bf16[128,1536]{1,0:T(8,128)(2,1)S(1)}, u32[]{:S(2)}, u32[]{:S(2)}) collective-permute-start(bf16[128,1536]{1,0:T(8,128)(2,1)S(1)} %get-tuple-element.42), channel_id=1, source_target_pairs={{0,12},{1,13},{2,14},{3,15},{4,0},{5,1},{6,2},{7,3},{8,4},{9,5},{1... | collective-permute-start | bytes 1179656 | tf_op jit(solution)/shard_map/ppermute | solution.py:32
  77.6 12.0 %collective-permute-start.8 = (bf16[64,1536]{1,0:T(8,128)(2,1)S(1)}, bf16[64,1536]{1,0:T(8,128)(2,1)S(1)}, u32[]{:S(2)}, u32[]{:S(2)}) collective-permute-start(bf16[64,1536]{1,0:T(8,128)(2,1)S(1)} %get-tuple-element.34), channel_id=1, source_target_pairs={{0,4},{1,5},{2,6},{3,7},{4,8},{5,9},{6,10},{7,11},{8,12},{9,13},{1... | collective-permute-start | bytes 589832 | tf_op jit(solution)/shard_map/ppermute | solution.py:32
  79.2 13.0 %collective-permute-start.9 = (bf16[64,1536]{1,0:T(8,128)(2,1)S(1)}, bf16[64,1536]{1,0:T(8,128)(2,1)S(1)}, u32[]{:S(2)}, u32[]{:S(2)}) collective-permute-start(bf16[64,1536]{1,0:T(8,128)(2,1)S(1)} %get-tuple-element.35), channel_id=1, source_target_pairs={{0,8},{1,9},{2,10},{3,11},{4,12},{5,13},{6,14},{7,15},{8,0},{9,1},... | collective-permute-start | bytes 589832 | tf_op jit(solution)/shard_map/ppermute | solution.py:32
  80.6 14.5 %collective-permute-start.10 = (bf16[64,1536]{1,0:T(8,128)(2,1)S(1)}, bf16[64,1536]{1,0:T(8,128)(2,1)S(1)}, u32[]{:S(2)}, u32[]{:S(2)}) collective-permute-start(bf16[64,1536]{1,0:T(8,128)(2,1)S(1)} %get-tuple-element.36), channel_id=1, source_target_pairs={{0,12},{1,13},{2,14},{3,15},{4,0},{5,1},{6,2},{7,3},{8,4},{9,5},{1... | collective-permute-start | bytes 589832 | tf_op jit(solution)/shard_map/ppermute | solution.py:32
  83.6 14.1 %collective-permute-start.22 = (bf16[64,1536]{1,0:T(8,128)(2,1)S(1)}, bf16[64,1536]{1,0:T(8,128)(2,1)S(1)}, u32[]{:S(2)}, u32[]{:S(2)}) collective-permute-start(bf16[64,1536]{1,0:T(8,128)(2,1)S(1)} %get-tuple-element.44), channel_id=1, source_target_pairs={{0,1},{1,2},{2,3},{3,0},{4,5},{5,6},{6,7},{7,4},{8,9},{9,10},{10,1... | collective-permute-start | bytes 589832 | tf_op jit(solution)/shard_map/ppermute | solution.py:37
  84.9 13.2 %collective-permute-start.23 = (bf16[64,1536]{1,0:T(8,128)(2,1)S(1)}, bf16[64,1536]{1,0:T(8,128)(2,1)S(1)}, u32[]{:S(2)}, u32[]{:S(2)}) collective-permute-start(bf16[64,1536]{1,0:T(8,128)(2,1)S(1)} %get-tuple-element.45), channel_id=1, source_target_pairs={{0,2},{1,3},{2,0},{3,1},{4,6},{5,7},{6,4},{7,5},{8,10},{9,11},{10,... | collective-permute-start | bytes 589832 | tf_op jit(solution)/shard_map/ppermute | solution.py:37
  98.4 12.2 %collective-permute-start.27 = (bf16[64,1536]{1,0:T(8,128)(2,1)S(1)}, bf16[64,1536]{1,0:T(8,128)(2,1)S(1)}, u32[]{:S(2)}, u32[]{:S(2)}) collective-permute-start(bf16[64,1536]{1,0:T(8,128)(2,1)S(1)} %grad_pre.3), channel_id=1, source_target_pairs={{0,1},{1,2},{2,3},{3,0},{4,5},{5,6},{6,7},{7,4},{8,9},{9,10},{10,1... | collective-permute-start | bytes 589832 | tf_op jit(solution)/shard_map/ppermute | solution.py:37
  108.5 22.0 %collective-permute-start.14 = (bf16[256,1536]{1,0:T(8,128)(2,1)S(1)}, bf16[256,1536]{1,0:T(8,128)(2,1)S(1)}, u32[]{:S(2)}, u32[]{:S(2)}) collective-permute-start(bf16[256,1536]{1,0:T(8,128)(2,1)S(1)} %pad_maximum_fusion.one), channel_id=1, source_target_pairs={{0,3},{1,0},{2,1},{3,2},{4,7},{5,4},{6,5},{7,6},{8,11},{9,8},{10,9... | collective-permute-start | bytes 2359304 | tf_op jit(solution)/shard_map/ppermute | solution.py:37
  110.2 20.2 %collective-permute-start.15 = (bf16[256,1536]{1,0:T(8,128)(2,1)S(1)}, bf16[256,1536]{1,0:T(8,128)(2,1)S(1)}, u32[]{:S(2)}, u32[]{:S(2)}) collective-permute-start(bf16[256,1536]{1,0:T(8,128)(2,1)S(1)} %pad_maximum_fusion.one), channel_id=1, source_target_pairs={{0,1},{1,2},{2,3},{3,0},{4,5},{5,6},{6,7},{7,4},{8,9},{9,10},{10,1... | collective-permute-start | bytes 2359304 | tf_op jit(solution)/shard_map/ppermute | solution.py:37
  110.7 23.2 %collective-permute-start.29 = (bf16[256,1536]{1,0:T(8,128)(2,1)S(1)}, bf16[256,1536]{1,0:T(8,128)(2,1)S(1)}, u32[]{:S(2)}, u32[]{:S(2)}) collective-permute-start(bf16[256,1536]{1,0:T(8,128)(2,1)S(1)} %pad_maximum_fusion.1.one), channel_id=1, source_target_pairs={{0,4},{1,5},{2,6},{3,7},{4,8},{5,9},{6,10},{7,11},{8,12},{9,13},{1... | collective-permute-start | bytes 2359304 | tf_op jit(solution)/shard_map/ppermute | solution.py:32
  114.7 21.3 %collective-permute-start.28 = (bf16[256,1536]{1,0:T(8,128)(2,1)S(1)}, bf16[256,1536]{1,0:T(8,128)(2,1)S(1)}, u32[]{:S(2)}, u32[]{:S(2)}) collective-permute-start(bf16[256,1536]{1,0:T(8,128)(2,1)S(1)} %pad_maximum_fusion.1.one), channel_id=1, source_target_pairs={{0,12},{1,13},{2,14},{3,15},{4,0},{5,1},{6,2},{7,3},{8,4},{9,5},{1... | collective-permute-start | bytes 2359304 | tf_op jit(solution)/shard_map/ppermute | solution.py:32
  115.1 21.0 %collective-permute-start.36 = (bf16[128,384]{1,0:T(8,128)(2,1)S(1)}, bf16[128,384]{1,0:T(8,128)(2,1)S(1)}, u32[]{:S(2)}, u32[]{:S(2)}) collective-permute-start(bf16[128,384]{1,0:T(8,128)(2,1)S(1)} %copy-done.4), channel_id=1, source_target_pairs={{0,96},{16,112},{32,0},{48,16},{64,32},{80,48},{96,64},{112,80},{1... | collective-permute-start | bytes 294920 | tf_op jit(solution)/shard_map/ppermute | solution.py:42
  130.5 15.6 %collective-permute-start.16 = (bf16[128,1536]{1,0:T(8,128)(2,1)S(1)}, bf16[128,1536]{1,0:T(8,128)(2,1)S(1)}, u32[]{:S(2)}, u32[]{:S(2)}) collective-permute-start(bf16[128,1536]{1,0:T(8,128)(2,1)S(1)} %slice.35), channel_id=1, source_target_pairs={{0,1},{1,2},{2,3},{3,0},{4,5},{5,6},{6,7},{7,4},{8,9},{9,10},{10,1... | collective-permute-start | bytes 1179656 | tf_op jit(solution)/shard_map/ppermute | solution.py:37
  130.6 15.5 %collective-permute-start.17 = (bf16[128,1536]{1,0:T(8,128)(2,1)S(1)}, bf16[128,1536]{1,0:T(8,128)(2,1)S(1)}, u32[]{:S(2)}, u32[]{:S(2)}) collective-permute-start(bf16[128,1536]{1,0:T(8,128)(2,1)S(1)} %slice.36), channel_id=1, source_target_pairs={{0,3},{1,0},{2,1},{3,2},{4,7},{5,4},{6,5},{7,6},{8,11},{9,8},{10,9... | collective-permute-start | bytes 1179656 | tf_op jit(solution)/shard_map/ppermute | solution.py:37
  135.9 14.0 %collective-permute-start.30 = (bf16[128,1536]{1,0:T(8,128)(2,1)S(1)}, bf16[128,1536]{1,0:T(8,128)(2,1)S(1)}, u32[]{:S(2)}, u32[]{:S(2)}) collective-permute-start(bf16[128,1536]{1,0:T(8,128)(2,1)S(1)} %slice.37), channel_id=1, source_target_pairs={{0,4},{1,5},{2,6},{3,7},{4,8},{5,9},{6,10},{7,11},{8,12},{9,13},{1... | collective-permute-start | bytes 1179656 | tf_op jit(solution)/shard_map/ppermute | solution.py:32
  136.1 13.9 %collective-permute-start.31 = (bf16[128,1536]{1,0:T(8,128)(2,1)S(1)}, bf16[128,1536]{1,0:T(8,128)(2,1)S(1)}, u32[]{:S(2)}, u32[]{:S(2)}) collective-permute-start(bf16[128,1536]{1,0:T(8,128)(2,1)S(1)} %slice.38), channel_id=1, source_target_pairs={{0,12},{1,13},{2,14},{3,15},{4,0},{5,1},{6,2},{7,3},{8,4},{9,5},{1... | collective-permute-start | bytes 1179656 | tf_op jit(solution)/shard_map/ppermute | solution.py:32
  (22 other events, 182.3 us)
Sparse Core Ops, SparseCore 0:
  10.2 85.0 all-gather.1

commit v2 on v0

v2 whole, which is shorter than its diff:
```python
import functools

import jax
import jax.numpy as jnp
from jax import lax
from jax.experimental import pallas as pl
from jax.experimental.pallas import tpu as pltpu
from jax.sharding import PartitionSpec as P

IMAGES = 8
SIDE = 4
BLOCK = 64
WIDE = 512
F32, BF16 = jnp.float32, jnp.bfloat16
NT = (((1,), (1,)), ((), ()))
NN = (((1,), (0,)), ((), ()))


def dot(left, right, dims):
    return lax.dot_general(left, right, dims, preferred_element_type=F32)


def gelu_parts(pre):
    normal_cdf = 0.5 * (1.0 + lax.erf(pre * 0.7071067811865476))
    density = jnp.exp(-0.5 * pre * pre) * 0.3989422804014327
    return (pre * normal_cdf, normal_cdf + pre * density)


def places():
    return [(x, c, y, z) for x in range(SIDE) for c in range(2) for y in range(SIDE) for z in range(SIDE)]


def index(x, c, y, z):
    return (2 * (x % SIDE) + c) * 16 + 4 * (y % SIDE) + z % SIDE


def move(a, by, along_z):
    pairs = [
        (index(x, c, y, z), index(x, c, y, z + by) if c == along_z else index(x, c, y + by, z))
        for x, c, y, z in places()
    ]
    return lax.ppermute(a, ("row", "col"), pairs)


def major(a, by):
    return move(a, by, 0)


def minor(a, by):
    return move(a, by, 1)


def move_x(a, by):
    pairs = [(2 * x + c, 2 * ((x + by) % SIDE) + c) for x in range(SIDE) for c in range(2)]
    return lax.ppermute(a, "row", pairs)


def swap_core(a):
    return lax.ppermute(a, "row", [(2 * x + c, 2 * x + 1 - c) for x in range(SIDE) for c in range(2)])


def call(kernel, outs, operands, name, small=0, order=(), flops=0, scratch=()):
    moved = sum(o.size * o.dtype.itemsize for o in operands) + sum(o.size * o.dtype.itemsize for o in outs)

    def body(*refs):
        kernel(*refs[: len(operands)], *refs[len(operands) + len(order) :])

    return pl.pallas_call(
        body,
        out_shape=outs,
        in_specs=[SMEM] * small + [VMEM] * (len(operands) - small) + [ANY] * len(order),
        out_specs=[VMEM] * len(outs),
        scratch_shapes=scratch,
        name=name,
        cost_estimate=pl.CostEstimate(flops=2 * flops, bytes_accessed=moved, transcendentals=0),
        compiler_params=pltpu.CompilerParams(vmem_limit_bytes=32 * 2**20),
    )(*operands, *order)


def each_block(count, body):
    @pl.loop(0, count // WIDE)
    def _(i):
        body(pl.ds(pl.multiple_of(i * WIDE, WIDE), WIDE))


SMEM = pl.BlockSpec(memory_space=pltpu.SMEM)
VMEM = pl.BlockSpec(memory_space=pltpu.VMEM)
ANY = pl.BlockSpec(memory_space=pl.ANY)


def shape(dims, kind):
    return jax.ShapeDtypeStruct(dims, kind)


def gathered_block(place, mine, other, cols, y, z):
    start = pl.multiple_of(((y - place[2]) & 3) * 128 + (z % 2) * BLOCK, BLOCK)
    rows = pl.ds(start, BLOCK)
    return jnp.where(place[3] == z // 2, mine[rows, cols], other[rows, cols])


def relative(place, y, z):
    dy, dz = (y - place[0]) & 3, (z - place[1]) & 3
    return jnp.where(place[3] == 0, dz, dy), jnp.where(place[3] == 0, dy, dz)


def rows_of(far, near):
    return pl.ds(pl.multiple_of((far * SIDE + near) * BLOCK, BLOCK), BLOCK)


def weight_kernel(lengths, out):
    position = lax.broadcasted_iota(jnp.int32, out.shape, 0)
    size = jnp.zeros(out.shape, jnp.int32)
    start = 0
    for k in range(IMAGES):
        end = start + lengths[k]
        size = jnp.where((position >= start) & (position < end), lengths[k], size)
        start = end
    out[...] = jnp.sqrt(128.0 / size.astype(F32))


def scaled_kernel(place, mine, other, weight, out):
    for y in range(SIDE):
        for z in range(SIDE):
            block = gathered_block(place, mine, other, pl.ds(0, out.shape[1]), y, z)
            here = weight[(y * SIDE + z) * BLOCK : (y * SIDE + z + 1) * BLOCK, :]
            here = jnp.concatenate([here] * (block.shape[1] // 128), axis=1)
            out[rows_of(*relative(place, y, z)), :] = (block.astype(F32) * here).astype(BF16)


def inputs_kernel(place, mine, other, flipped, plain):
    for y in range(SIDE):
        for z in range(SIDE):
            block = gathered_block(place, mine, other, pl.ds(plain.shape[1], plain.shape[1]), y, z)
            plain[rows_of(*relative(place, y, z)), :] = block
    flipped[...] = plain[...].T


def back_kernel(scaled, w, *outs):
    def body(cols):
        total = dot(scaled[...], w[cols, :], NT)
        at = 0
        for out in outs:
            out[:, cols] = total[at : at + out.shape[0]].astype(out.dtype)
            at += out.shape[0]

    each_block(w.shape[0], body)


def back_rows(scaled, w_out, kinds, order=()):
    (rows, depth), hidden = scaled.shape, w_out.shape[0]
    return call(
        back_kernel,
        [shape((count, hidden), kind) for count, kind in kinds],
        (scaled, w_out),
        "back",
        order=order,
        flops=2 * rows * depth * hidden,
    )


def pass_kernel(to_high, to_low, low, high, plus, minus):
    def body(cols):
        plus[:, cols] = (to_high[:, cols] + low[:, cols].astype(F32)).astype(BF16)
        minus[:, cols] = (to_low[:, cols] + high[:, cols].astype(F32)).astype(BF16)

    each_block(plus.shape[1], body)


def sums_kernel(own, low, high, low_sum, high_sum, zero, to_high, plus, minus, to_low):
    def body(cols):
        upper = own[:128, cols] + high[:, cols].astype(F32) + low_sum[:, cols].astype(F32)
        lower = own[128:, cols] + low[:, cols].astype(F32) + high_sum[:, cols].astype(F32)
        zero[:, cols] = upper[:64]
        to_high[:, cols] = upper[64:96]
        plus[:, cols] = jnp.concatenate([upper[96:], lower[:32]], axis=0).astype(BF16)
        minus[:, cols] = lower[32:96].astype(BF16)
        to_low[:, cols] = lower[96:]

    each_block(own.shape[1], body)


def grad_kernel(own, low, high, low_sum, high_sum, slope, grad):
    def body(cols):
        upper = own[:32, cols] + high[32:, cols].astype(F32) + low_sum[:, cols].astype(F32)
        lower = own[32:, cols] + low[:32, cols].astype(F32) + high_sum[:, cols].astype(F32)
        back = jnp.concatenate([upper, lower], axis=0)
        grad[:, cols] = (back * slope[:, cols]).astype(BF16)

    each_block(own.shape[1], body)


def reduce_back(scaled, w_out, order_rest, order_sums):
    hidden = w_out.shape[0]
    half = [(128, BF16)] * 2
    plus, minus = back_rows(scaled[512:768], w_out, half)
    from_low, from_high = major(plus, 1), major(minus, -1)
    beside = jnp.concatenate([scaled[384:512], scaled[768:896]], axis=0)
    plus, minus = back_rows(beside, w_out, half, order_rest)
    low, high = major(plus, 1), major(minus, -1)
    rest = jnp.concatenate([scaled[896:], scaled[:384]], axis=0)
    to_low, own, to_high = back_rows(rest, w_out, [(128, F32), (256, F32), (128, F32)])
    plus, minus = call(pass_kernel, [shape((128, hidden), BF16)] * 2, (to_high, to_low, from_low, from_high), "pass")
    low_sum, high_sum = major(plus, 1), major(minus, -1)
    sums = call(
        sums_kernel,
        [shape((64, hidden), F32), shape((32, hidden), F32)]
        + [shape((64, hidden), BF16)] * 2
        + [shape((32, hidden), F32)],
        (own, low, high, low_sum, high_sum),
        "sums",
        order=order_sums,
    )

    def minor_parts(order):
        zero, to_high, plus, minus, to_low = sums
        low, high = minor(plus, 1), minor(minus, -1)
        plus, minus = call(
            pass_kernel,
            [shape((32, hidden), BF16)] * 2,
            (to_high, to_low, low[32:], high[:32]),
            "pass_minor",
            order=order,
        )
        return zero, low, high, minor(plus, 1), minor(minus, -1)

    return sums, minor_parts


def minor_sides(a):
    return minor(a, 1), minor(a, -1)


def minor_rows(a, low, high):
    return a, high, minor(low[:32], 1), minor(high[32:], -1), low


def stack_kernel(*refs):
    at = 0
    for piece in refs[:-1]:
        refs[-1][at : at + piece.shape[0], :] = piece[...]
        at += piece.shape[0]


def stack(pieces, order=()):
    dims = (sum(p.shape[0] for p in pieces), pieces[0].shape[1])
    return call(stack_kernel, [shape(dims, BF16)], pieces, "stack", order=order)[0]


def grad_inputs_kernel(*refs):
    *pieces, w, out = refs
    at = 0
    for piece in pieces:
        for k in range(0, piece.shape[0], 128):
            out[at : at + 128, :] = dot(piece[k : k + 128, :], w[...], NT)
            at += 128


def grad_inputs_rows(pieces, w_in, name, order=()):
    rows, depth, hidden = sum(p.shape[0] for p in pieces), *w_in.shape
    return call(
        grad_inputs_kernel,
        [shape((rows, depth), F32)],
        (*pieces, w_in),
        name,
        order=order,
        flops=2 * rows * depth * hidden,
    )[0]


def partial_rows(near, far, place, y, z):
    large, small = relative(place, y, z)
    spot = jnp.where(large == 3, 2, jnp.minimum(large, 1))
    return jnp.where(large == 2, far[rows_of(0, small), :], near[rows_of(spot, small), :])


def join_kernel(place, near, far, send, keep):
    for x in range(SIDE):
        for z in range(2):
            for out, core in ((keep, place[3]), (send, 1 - place[3])):
                block = partial_rows(near, far, place, place[2] + x, 2 * core + z)
                out[pl.ds(x * 128 + z * BLOCK, BLOCK), :] = block.astype(out.dtype)


def grad_w_in_kernel(factor, flipped, *refs):
    *pieces, out = refs

    def body(cols):
        rows = jnp.concatenate([piece[:, cols] for piece in pieces], axis=0)
        out[:, cols] = (dot(flipped[...], rows, NN) * factor).astype(BF16)

    each_block(out.shape[1], body)


def grad_w_in_all(flipped, pieces, factor):
    hidden, depth = pieces[0].shape[1], flipped.shape[0]
    return call(
        functools.partial(grad_w_in_kernel, factor),
        [shape((depth, hidden), BF16)],
        (flipped, *pieces),
        "grad_w_in",
        flops=2 * 1024 * depth * hidden,
    )[0]


def flip_kernel(one, two, three, four, five, out):
    def body(cols):
        out[0, cols, :] = jnp.concatenate([one[:, cols], two[:, cols]], axis=0).T
        out[1, cols, :] = jnp.concatenate([three[:, cols], four[:, cols], five[:, cols]], axis=0).T

    each_block(one.shape[1], body)


def flip(rows, order):
    return call(flip_kernel, [shape((2, rows[0].shape[1], 128), BF16)], rows, "flip", order=order)[0]


def grad_w_out_kernel(factor, scaled, one, two, three, four, five, out):
    def body(cols):
        pieces = [p[k, cols, :] for p in (one, two, three, four, five) for k in range(p.shape[0])]
        out[cols, :] = (dot(jnp.concatenate(pieces, axis=1), scaled[...], NN) * factor).astype(BF16)

    each_block(out.shape[0], body)


def grad_w_out_all(scaled, pieces, factor):
    depth, hidden = scaled.shape[1], pieces[0].shape[1]
    return call(
        functools.partial(grad_w_out_kernel, factor),
        [shape((hidden, depth), BF16)],
        (scaled, *pieces),
        "grad_w_out",
        flops=2 * 1024 * depth * hidden,
    )[0]


def beside_kernel(one, two, out):
    depth = one.shape[1]
    out[:, :depth] = one[...]
    out[:, depth:] = two[...]


def row_gather(one, two):
    dims = (one.shape[0], 2 * one.shape[1])
    both = call(beside_kernel, [shape(dims, BF16)], (one, two), "beside")[0]
    mine = stack((both, move_x(both, -1), move_x(both, -2), move_x(both, -3)))
    return mine, swap_core(mine)


def shards(inputs, upstream, preact, bias_in, w_in, w_out, lengths):
    col, row = lax.axis_index("col"), lax.axis_index("row")
    place = jnp.stack([col // SIDE, col % SIDE, row // 2, row % 2]).astype(jnp.int32)
    depth, hidden = w_in.shape
    factor = 1024 ** (-0.5)

    mine, other = row_gather(upstream, inputs)
    weight = call(weight_kernel, [shape((1024, 128), F32)], (lengths,), "weight", small=1)[0]
    pre = preact.astype(F32) + bias_in[None, :]
    value, slope = gelu_parts(pre)
    act, slope = lax.optimization_barrier((value.astype(BF16), slope))
    act_sides = minor_sides(act)
    scaled = call(
        scaled_kernel,
        [shape((1024, depth), BF16)],
        (place, mine, other, weight),
        "scaled",
        small=1,
    )[0]
    act_rows = minor_rows(act, *act_sides)
    sums, minor_parts = reduce_back(scaled, w_out, (), ())
    act_near = flip(act_rows, ())
    act_low, act_high = major(act_near, 1), major(act_near, -1)
    act_pieces = (act_near, act_high, major(act_low[:1], 1), major(act_high[1:], -1), act_low)
    parts = minor_parts(())
    grad = call(grad_kernel, [shape((BLOCK, hidden), BF16)], (*parts, slope), "grad_pre")[0]
    in_flipped = call(
        inputs_kernel,
        [shape((depth, 1024), BF16)],
        (place, mine, other),
        "inputs",
        small=1,
        scratch=[pltpu.VMEM((1024, depth), BF16)],
    )[0]
    grad_w_out = grad_w_out_all(scaled, act_pieces, factor)
    near = stack(minor_rows(grad, *minor_sides(grad)))
    low_a, high_b = major(near[:128], 1), major(near[128:], -1)
    low_b, high_a = major(near[128:], 1), major(near[:128], -1)
    far = major(low_a, 1), major(high_b, -1)
    total_near = grad_inputs_rows((near, high_a, high_b, low_a, low_b), w_in, "grad_inputs_near")
    total_far = grad_inputs_rows(far, w_in, "grad_inputs_far", (total_near, grad_w_out, in_flipped))
    pieces = (near, high_a, high_b, *far, low_a, low_b)
    send, keep = call(
        join_kernel,
        [shape((512, depth), BF16), shape((512, depth), F32)],
        (place, total_near, total_far),
        "join",
        small=1,
    )
    keep = keep + swap_core(send).astype(F32)
    parts = [keep[128 * k : 128 * (k + 1)] for k in range(SIDE)]
    grad_inputs = parts[0]
    for k in range(1, SIDE):
        grad_inputs = grad_inputs + move_x(parts[k].astype(BF16), k).astype(F32)
    grad_w_in = grad_w_in_all(in_flipped, pieces, factor)
    return (grad_inputs.astype(BF16), grad_w_in, grad_w_out)


def solution(mesh):
    placed = (
        P("row", "col"),
        P("row", "col"),
        P("col", "row"),
        P("row"),
        P("col", "row"),
        P("row", "col"),
        P(),
    )
    return jax.shard_map(
        shards,
        mesh=mesh,
        in_specs=placed,
        out_specs=(P("row", "col"), P("col", "row"), P("row", "col")),
        check_vma=False,
    )
```

time: 297 us -> 157 us (0.53)
  waiting for transfers between devices: 213 us -> 67.4 us
  starting transfers between devices: 0.16 us -> 49.9 us
  Pallas kernels: 0 us -> 29.9 us
  matrix products: 29.8 us -> 0 us
  blocking collectives: 27.6 us -> 0 us
  between operations: 13.8 us -> 1.02 us
  other arithmetic: 7.37 us -> 1.31 us
    reduce_scatter x2 -> x0, waiting for transfers between devices: 123 us -> none  [the longest x1 95.9 us: shards(): lax.psum_scatter(contract_last(piece, w_out), 'col', scatter_dimension=0,...]
    all_gather x2 -> x0, waiting for transfers between devices: 89.9 us -> none  [the longest x1 60.6 us: shards(): lax.all_gather(grad_pre, 'col', axis=0, tiled=True)]
    ppermute x0 -> x36, waiting for transfers between devices: none -> 67.4 us  [the longest x28 58.3 us: move(): return lax.ppermute(a, ('row', 'col'), pairs)]
    ppermute x0 -> x36, starting transfers between devices: none -> 49.9 us  [the longest x28 39.2 us: move(): return lax.ppermute(a, ('row', 'col'), pairs)]
    pallas_call x0 -> x19, Pallas kernels: none -> 29.9 us  [call(): pl.pallas_call(body, out_shape=outs, in_specs=[SMEM] * small + [VMEM] * (...]
    dot_general x4 -> x0, matrix products: 29.8 us -> none  [the longest x2 15.3 us: contract_first(): lax.dot_general(left, right, (((0,), (0,)), ((), ())), preferred_element_...]
    all_gather x2 -> x0, blocking collectives: 27.6 us -> none  [the longest x1 13.9 us: shards(): lax.all_gather(inputs, 'row', axis=0, tiled=True)]
    convert_element_type x3 -> x1, other arithmetic: 4.98 us -> 0.69 us  [shards(): return (grad_inputs.astype(BF16), grad_w_in, grad_w_out)]
  transfers between devices with their start and end apart: 4 -> 36, of which waited for: 4 -> 19; matrix products, arithmetic and copies ran while one was open for 9% -> 2% of each run, Pallas kernels for 0% -> 18%
where the time goes in v2:
time: 157 us; the launch traced here: 154 us
  waiting for transfers between devices  67.4 us (43%)
  starting transfers between devices  49.9 us (32%)
  Pallas kernels  29.9 us (19%)
  local copies, waits for them, and re-layouts  4.96 us (3%)
    ppermute x28, waiting for transfers between devices, move(): return lax.ppermute(a, ('row', 'col'), pairs)  58.3 us
    ppermute x28, starting transfers between devices, move(): return lax.ppermute(a, ('row', 'col'), pairs)  39.2 us
    pallas_call x19, Pallas kernels, call(): pl.pallas_call(body, out_shape=outs, in_specs=[SMEM] * small + [VMEM] * (...  29.9 us
    ppermute x6, starting transfers between devices, move_x(): return lax.ppermute(a, 'row', pairs)  10.5 us
    ppermute x6, waiting for transfers between devices, move_x(): return lax.ppermute(a, 'row', pairs)  7.4 us
  transfers between devices with their start and end apart: 36, of which 19 were waited for; matrix products, arithmetic and copies ran while one was open for 2% of the time, Pallas kernels for 18%

profile of v2, /device:TPU:24, one launch (start us, length us, event | category | flops | bytes accessed | tf_op | source)
XLA Modules:
  0.0 154.5 jit_solution(1105260672573739785)
XLA Ops:
  4.0 2.7 %collective-permute-start.1 = (bf16[128,768]{1,0:T(8,128)(2,1)S(1)}, bf16[128,768]{1,0:T(8,128)(2,1)S(1)}, u32[]{:S(2)}, u32[]{:S(2)}) collective-permute-start(bf16[128,768]{1,0:T(8,128)(2,1)S(1)} %beside.1.refs_0_), channel_id=1, source_target_pairs={{0,64},{16,80},{32,96},{48,112},{64,0},{80,16},{96,32},{112,48},{1... | collective-permute-start | bytes 589832 | tf_op jit(solution)/shard_map/ppermute | solution.py:55
  8.2 2.4 %collective-permute-done.2.refs_3_ = bf16[128,768]{1,0:T(8,128)(2,1)S(1)} collective-permute-done((bf16[128,768]{1,0:T(8,128)(2,1)S(1)}, bf16[128,768]{1,0:T(8,128)(2,1)S(1)}, u32[]{:S(2)}, u32[]{:S(2)}) %collective-permute-start.2) | collective-permute-done | bytes 196640 | tf_op jit(solution)/shard_map/ppermute | solution.py:55
  10.5 5.0 %collective-permute-done.1.refs_2_ = bf16[128,768]{1,0:T(8,128)(2,1)S(1)} collective-permute-done((bf16[128,768]{1,0:T(8,128)(2,1)S(1)}, bf16[128,768]{1,0:T(8,128)(2,1)S(1)}, u32[]{:S(2)}, u32[]{:S(2)}) %collective-permute-start.1) | collective-permute-done | bytes 196640 | tf_op jit(solution)/shard_map/ppermute | solution.py:55
  25.2 2.2 %collective-permute-start.7 = (bf16[128,3072]{1,0:T(8,128)(2,1)S(1)}, bf16[128,3072]{1,0:T(8,128)(2,1)S(1)}, u32[]{:S(2)}, u32[]{:S(2)}) collective-permute-start(bf16[128,3072]{1,0:T(8,128)(2,1)S(1)} %get-tuple-element.29), channel_id=1, source_target_pairs={{0,3},{1,0},{2,1},{3,2},{4,7},{5,4},{6,5},{7,6},{8,11},{9,8},{10,9... | collective-permute-start | bytes 2359304 | tf_op jit(solution)/shard_map/ppermute | solution.py:42
  29.7 2.8 %back.3 = (f32[128,3072]{1,0:T(8,128)S(1)}, f32[256,3072]{1,0:T(8,128)S(1)}, f32[128,3072]{1,0:T(8,128)S(1)}) custom-call(bf16[512,384]{1,0:T(8,128)(2,1)S(1)} %pad_maximum_fusion.refs_0_, bf16[3072,384]{1,0:T(8,128)(2,1)S(1)} %copy-done.5), custom_call_target="tpu_custom_call" | custom-call | flops 2415919104 | bytes 9043968 | tf_op jit(solution)/shard_map/back/pallas_call | solution.py:68
  32.5 4.8 %collective-permute-done.6.refs_2_ = bf16[128,3072]{1,0:T(8,128)(2,1)S(1)} collective-permute-done((bf16[128,3072]{1,0:T(8,128)(2,1)S(1)}, bf16[128,3072]{1,0:T(8,128)(2,1)S(1)}, u32[]{:S(2)}, u32[]{:S(2)}) %collective-permute-start.6) | collective-permute-done | bytes 786464 | tf_op jit(solution)/shard_map/ppermute | solution.py:42
  39.8 3.2 %collective-permute-start.9 = (bf16[128,3072]{1,0:T(8,128)(2,1)S(1)}, bf16[128,3072]{1,0:T(8,128)(2,1)S(1)}, u32[]{:S(2)}, u32[]{:S(2)}) collective-permute-start(bf16[128,3072]{1,0:T(8,128)(2,1)S(1)} %get-tuple-element.31), channel_id=1, source_target_pairs={{0,3},{1,0},{2,1},{3,2},{4,7},{5,4},{6,5},{7,6},{8,11},{9,8},{10,9... | collective-permute-start | bytes 2359304 | tf_op jit(solution)/shard_map/ppermute | solution.py:42
  46.4 5.5 %collective-permute-done.26.refs_2_ = bf16[32,3072]{1,0:T(8,128)(2,1)S(1)} collective-permute-done((bf16[32,3072]{1,0:T(8,128)(2,1)S(1)}, bf16[32,3072]{1,0:T(8,128)(2,1)S(1)}, u32[]{:S(2)}, u32[]{:S(2)}) %collective-permute-start.26) | collective-permute-done | bytes 196640 | tf_op jit(solution)/shard_map/ppermute | solution.py:42
  52.6 6.9 %collective-permute-done.27.refs_3_ = bf16[32,3072]{1,0:T(8,128)(2,1)S(1)} collective-permute-done((bf16[32,3072]{1,0:T(8,128)(2,1)S(1)}, bf16[32,3072]{1,0:T(8,128)(2,1)S(1)}, u32[]{:S(2)}, u32[]{:S(2)}) %collective-permute-start.27) | collective-permute-done | bytes 196640 | tf_op jit(solution)/shard_map/ppermute | solution.py:42
  64.1 3.2 %collective-permute-start.28 = (bf16[2,3072,128]{2,1,0:T(8,128)(2,1)S(1)}, bf16[2,3072,128]{2,1,0:T(8,128)(2,1)S(1)}, u32[]{:S(2)}, u32[]{:S(2)}) collective-permute-start(bf16[2,3072,128]{2,1,0:T(8,128)(2,1)S(1)} %flip.1.refs_1_), channel_id=1, source_target_pairs={{0,3},{1,0},{2,1},{3,2},{4,7},{5,4},{6,5},{7,6},{8,11},{9,8},{10,9... | collective-permute-start | bytes 4718600 | tf_op jit(solution)/shard_map/ppermute | solution.py:42
  67.3 6.8 %collective-permute-done.10.refs_1_ = bf16[64,3072]{1,0:T(8,128)(2,1)S(1)} collective-permute-done((bf16[64,3072]{1,0:T(8,128)(2,1)S(1)}, bf16[64,3072]{1,0:T(8,128)(2,1)S(1)}, u32[]{:S(2)}, u32[]{:S(2)}) %collective-permute-start.10) | collective-permute-done | bytes 393248 | tf_op jit(solution)/shard_map/ppermute | solution.py:42
  77.9 5.8 %collective-permute-done.12.refs_3_ = bf16[32,3072]{1,0:T(8,128)(2,1)S(1)} collective-permute-done((bf16[32,3072]{1,0:T(8,128)(2,1)S(1)}, bf16[32,3072]{1,0:T(8,128)(2,1)S(1)}, u32[]{:S(2)}, u32[]{:S(2)}) %collective-permute-start.12) | collective-permute-done | bytes 196640 | tf_op jit(solution)/shard_map/ppermute | solution.py:42
  87.6 5.8 %collective-permute-done.15.refs_4_ = bf16[64,3072]{1,0:T(8,128)(2,1)S(1)} collective-permute-done((bf16[64,3072]{1,0:T(8,128)(2,1)S(1)}, bf16[64,3072]{1,0:T(8,128)(2,1)S(1)}, u32[]{:S(2)}, u32[]{:S(2)}) %collective-permute-start.15) | collective-permute-done | bytes 393248 | tf_op jit(solution)/shard_map/ppermute | solution.py:42
  96.7 3.1 %collective-permute-done.16.refs_2_ = bf16[32,3072]{1,0:T(8,128)(2,1)S(1)} collective-permute-done((bf16[32,3072]{1,0:T(8,128)(2,1)S(1)}, bf16[32,3072]{1,0:T(8,128)(2,1)S(1)}, u32[]{:S(2)}, u32[]{:S(2)}) %collective-permute-start.16) | collective-permute-done | bytes 196640 | tf_op jit(solution)/shard_map/ppermute | solution.py:42
  102.1 3.0 %collective-permute-start.19 = (bf16[128,3072]{1,0:T(8,128)(2,1)S(1)}, bf16[128,3072]{1,0:T(8,128)(2,1)S(1)}, u32[]{:S(2)}, u32[]{:S(2)}) collective-permute-start(bf16[128,3072]{1,0:T(8,128)(2,1)S(1)} %get-tuple-element.45), channel_id=1, source_target_pairs={{0,3},{1,0},{2,1},{3,2},{4,7},{5,4},{6,5},{7,6},{8,11},{9,8},{10,9... | collective-permute-start | bytes 2359304 | tf_op jit(solution)/shard_map/ppermute | solution.py:42
  105.2 3.3 %collective-permute-start.31 = (bf16[1,3072,128]{2,1,0:T(8,128)(2,1)S(1)}, bf16[1,3072,128]{2,1,0:T(8,128)(2,1)S(1)}, u32[]{:S(2)}, u32[]{:S(2)}) collective-permute-start(bf16[1,3072,128]{2,1,0:T(8,128)(2,1)S(1)} %slice.95), channel_id=1, source_target_pairs={{0,3},{1,0},{2,1},{3,2},{4,7},{5,4},{6,5},{7,6},{8,11},{9,8},{10,9... | collective-permute-start | bytes 2359304 | tf_op jit(solution)/shard_map/ppermute | solution.py:42
  109.0 2.7 %collective-permute-start.18 = (bf16[128,3072]{1,0:T(8,128)(2,1)S(1)}, bf16[128,3072]{1,0:T(8,128)(2,1)S(1)}, u32[]{:S(2)}, u32[]{:S(2)}) collective-permute-start(bf16[128,3072]{1,0:T(8,128)(2,1)S(1)} %get-tuple-element.46), channel_id=1, source_target_pairs={{0,3},{1,0},{2,1},{3,2},{4,7},{5,4},{6,5},{7,6},{8,11},{9,8},{10,9... | collective-permute-start | bytes 2359304 | tf_op jit(solution)/shard_map/ppermute | solution.py:42
  114.6 3.7 %collective-permute-start.23 = (bf16[128,3072]{1,0:T(8,128)(2,1)S(1)}, bf16[128,3072]{1,0:T(8,128)(2,1)S(1)}, u32[]{:S(2)}, u32[]{:S(2)}) collective-permute-start(bf16[128,3072]{1,0:T(8,128)(2,1)S(1)} %collective-permute-done.19.refs_2_.refs_3_), channel_id=1, source_target_pairs={{0,3},{1,0},{2,1},{3,2},{4,7},{5,4},{6,5},{7,6},{8,11},{9,8},{10,9... | collective-permute-start | bytes 2359304 | tf_op jit(solution)/shard_map/ppermute | solution.py:42
  118.3 4.7 %collective-permute-done.31.refs_4_ = bf16[1,3072,128]{2,1,0:T(8,128)(2,1)S(1)} collective-permute-done((bf16[1,3072,128]{2,1,0:T(8,128)(2,1)S(1)}, bf16[1,3072,128]{2,1,0:T(8,128)(2,1)S(1)}, u32[]{:S(2)}, u32[]{:S(2)}) %collective-permute-start.31) | collective-permute-done | bytes 786464 | tf_op jit(solution)/shard_map/ppermute | solution.py:42
  123.1 5.7 %grad_w_out.1.refs_4_ = bf16[3072,384]{1,0:T(8,128)(2,1)} custom-call(bf16[1024,384]{1,0:T(8,128)(2,1)S(1)} %scaled.1.refs_0_, bf16[2,3072,128]{2,1,0:T(8,128)(2,1)S(1)} %flip.1.refs_1_, bf16[2,3072,128]{2,1,0:T(8,128)(2,1)S(1)} %collective-permute-done.28.refs_2_, bf16[1,3072,128]{2,1,0:T(8,128)(2,1)S(1)} %collective-permute-done.30.refs_3_, ...), custom_call_target="tpu_custom_call" | custom-call | flops 4831838208 | bytes 9437184 | tf_op jit(solution)/shard_map/grad_w_out/pallas_call | solution.py:68
  128.7 2.7 %collective-permute-done.18.refs_1_.refs_2_ = bf16[128,3072]{1,0:T(8,128)(2,1)S(1)} collective-permute-done((bf16[128,3072]{1,0:T(8,128)(2,1)S(1)}, bf16[128,3072]{1,0:T(8,128)(2,1)S(1)}, u32[]{:S(2)}, u32[]{:S(2)}) %collective-permute-start.18) | collective-permute-done | bytes 786464 | tf_op jit(solution)/shard_map/ppermute | solution.py:42
  131.5 4.2 %grad_inputs_near.1.refs_3_.refs_1_ = f32[768,384]{1,0:T(8,128)S(1)} custom-call(bf16[256,3072]{1,0:T(8,128)(2,1)S(1)} %stack.23.refs_0_.refs_1_, bf16[128,3072]{1,0:T(8,128)(2,1)S(1)} %collective-permute-done.18.refs_1_.refs_2_, bf16[128,3072]{1,0:T(8,128)(2,1)S(1)} %collective-permute-done.19.refs_2_.refs_3_, ...), custom_call_target="tpu_custom_call" | custom-call | flops 3623878656 | bytes 8257536 | tf_op jit(solution)/shard_map/grad_inputs_near/pallas_call | solution.py:68
  135.7 4.2 %collective-permute-done.23.refs_1_.refs_5_ = bf16[128,3072]{1,0:T(8,128)(2,1)S(1)} collective-permute-done((bf16[128,3072]{1,0:T(8,128)(2,1)S(1)}, bf16[128,3072]{1,0:T(8,128)(2,1)S(1)}, u32[]{:S(2)}, u32[]{:S(2)}) %collective-permute-start.23) | collective-permute-done | bytes 786464 | tf_op jit(solution)/shard_map/ppermute | solution.py:42
  148.8 4.9 %grad_w_in.1 = bf16[384,3072]{1,0:T(8,128)(2,1)} custom-call(bf16[384,1024]{1,0:T(8,128)(2,1)S(1)} %inputs.1.refs_5_.refs_0_, bf16[256,3072]{1,0:T(8,128)(2,1)S(1)} %stack.23.refs_0_.refs_1_, bf16[128,3072]{1,0:T(8,128)(2,1)S(1)} %collective-permute-done.18.refs_1_.refs_2_, bf16[128,3072]{1,0:T(8,128)(2,1)S(1)} %collective-permute-done.19.refs_2_.refs_3_, ...), custom_call_target="tpu_custom_call" | custom-call | flops 4831838208 | bytes 9437184 | tf_op jit(solution)/shard_map/grad_w_in/pallas_call | solution.py:68
  (102 shorter events, 54.0 us)
Async XLA Ops:
  4.0 11.6 %collective-permute-start.1 = (bf16[128,768]{1,0:T(8,128)(2,1)S(1)}, bf16[128,768]{1,0:T(8,128)(2,1)S(1)}, u32[]{:S(2)}, u32[]{:S(2)}) collective-permute-start(bf16[128,768]{1,0:T(8,128)(2,1)S(1)} %beside.1.refs_0_), channel_id=1, source_target_pairs={{0,64},{16,80},{32,96},{48,112},{64,0},{80,16},{96,32},{112,48},{1... | collective-permute-start | bytes 589832 | tf_op jit(solution)/shard_map/ppermute | solution.py:55
  16.1 23.6 %collective-permute-start.25 = (bf16[64,3072]{1,0:T(8,128)(2,1)S(1)}, bf16[64,3072]{1,0:T(8,128)(2,1)}, u32[]{:S(2)}, u32[]{:S(2)}) collective-permute-start(bf16[64,3072]{1,0:T(8,128)(2,1)S(1)} %get-tuple-element.40.refs_0_), channel_id=1, source_target_pairs={{0,4},{1,5},{2,6},{3,7},{4,8},{5,9},{6,10},{7,11},{8,12},{9,13},{1... | collective-permute-start | bytes 1179656 | tf_op jit(solution)/shard_map/ppermute | solution.py:42
  16.4 27.5 %collective-permute-start.24 = (bf16[64,3072]{1,0:T(8,128)(2,1)S(1)}, bf16[64,3072]{1,0:T(8,128)(2,1)}, u32[]{:S(2)}, u32[]{:S(2)}) collective-permute-start(bf16[64,3072]{1,0:T(8,128)(2,1)S(1)} %get-tuple-element.40.refs_0_), channel_id=1, source_target_pairs={{0,12},{1,13},{2,14},{3,15},{4,0},{5,1},{6,2},{7,3},{8,4},{9,5},{1... | collective-permute-start | bytes 1179656 | tf_op jit(solution)/shard_map/ppermute | solution.py:42
  23.3 14.1 %collective-permute-start.6 = (bf16[128,3072]{1,0:T(8,128)(2,1)S(1)}, bf16[128,3072]{1,0:T(8,128)(2,1)S(1)}, u32[]{:S(2)}, u32[]{:S(2)}) collective-permute-start(bf16[128,3072]{1,0:T(8,128)(2,1)S(1)} %get-tuple-element.28), channel_id=1, source_target_pairs={{0,1},{1,2},{2,3},{3,0},{4,5},{5,6},{6,7},{7,4},{8,9},{9,10},{10,1... | collective-permute-start | bytes 2359304 | tf_op jit(solution)/shard_map/ppermute | solution.py:42
  25.2 14.1 %collective-permute-start.7 = (bf16[128,3072]{1,0:T(8,128)(2,1)S(1)}, bf16[128,3072]{1,0:T(8,128)(2,1)S(1)}, u32[]{:S(2)}, u32[]{:S(2)}) collective-permute-start(bf16[128,3072]{1,0:T(8,128)(2,1)S(1)} %get-tuple-element.29), channel_id=1, source_target_pairs={{0,3},{1,0},{2,1},{3,2},{4,7},{5,4},{6,5},{7,6},{8,11},{9,8},{10,9... | collective-permute-start | bytes 2359304 | tf_op jit(solution)/shard_map/ppermute | solution.py:42
  29.5 31.9 %collective-permute-start.4 = (bf16[128,3072]{1,0:T(8,128)(2,1)S(1)}, bf16[128,3072]{1,0:T(8,128)(2,1)S(1)}, u32[]{:S(2)}, u32[]{:S(2)}) collective-permute-start(bf16[128,3072]{1,0:T(8,128)(2,1)S(1)} %get-tuple-element.24), channel_id=1, source_target_pairs={{0,1},{1,2},{2,3},{3,0},{4,5},{5,6},{6,7},{7,4},{8,9},{9,10},{10,1... | collective-permute-start | bytes 2359304 | tf_op jit(solution)/shard_map/ppermute | solution.py:42
  37.3 24.1 %collective-permute-start.5 = (bf16[128,3072]{1,0:T(8,128)(2,1)S(1)}, bf16[128,3072]{1,0:T(8,128)(2,1)S(1)}, u32[]{:S(2)}, u32[]{:S(2)}) collective-permute-start(bf16[128,3072]{1,0:T(8,128)(2,1)S(1)} %get-tuple-element.25), channel_id=1, source_target_pairs={{0,3},{1,0},{2,1},{3,2},{4,7},{5,4},{6,5},{7,6},{8,11},{9,8},{10,9... | collective-permute-start | bytes 2359304 | tf_op jit(solution)/shard_map/ppermute | solution.py:42
  39.7 21.8 %collective-permute-start.8 = (bf16[128,3072]{1,0:T(8,128)(2,1)S(1)}, bf16[128,3072]{1,0:T(8,128)(2,1)S(1)}, u32[]{:S(2)}, u32[]{:S(2)}) collective-permute-start(bf16[128,3072]{1,0:T(8,128)(2,1)S(1)} %get-tuple-element.30), channel_id=1, source_target_pairs={{0,1},{1,2},{2,3},{3,0},{4,5},{5,6},{6,7},{7,4},{8,9},{9,10},{10,1... | collective-permute-start | bytes 2359304 | tf_op jit(solution)/shard_map/ppermute | solution.py:42
  39.8 21.7 %collective-permute-start.9 = (bf16[128,3072]{1,0:T(8,128)(2,1)S(1)}, bf16[128,3072]{1,0:T(8,128)(2,1)S(1)}, u32[]{:S(2)}, u32[]{:S(2)}) collective-permute-start(bf16[128,3072]{1,0:T(8,128)(2,1)S(1)} %get-tuple-element.31), channel_id=1, source_target_pairs={{0,3},{1,0},{2,1},{3,2},{4,7},{5,4},{6,5},{7,6},{8,11},{9,8},{10,9... | collective-permute-start | bytes 2359304 | tf_op jit(solution)/shard_map/ppermute | solution.py:42
  61.4 34.1 %collective-permute-start.29 = (bf16[2,3072,128]{2,1,0:T(8,128)(2,1)S(1)}, bf16[2,3072,128]{2,1,0:T(8,128)(2,1)S(1)}, u32[]{:S(2)}, u32[]{:S(2)}) collective-permute-start(bf16[2,3072,128]{2,1,0:T(8,128)(2,1)S(1)} %flip.1.refs_1_), channel_id=1, source_target_pairs={{0,1},{1,2},{2,3},{3,0},{4,5},{5,6},{6,7},{7,4},{8,9},{9,10},{10,1... | collective-permute-start | bytes 4718600 | tf_op jit(solution)/shard_map/ppermute | solution.py:42
  62.0 12.1 %collective-permute-start.10 = (bf16[64,3072]{1,0:T(8,128)(2,1)S(1)}, bf16[64,3072]{1,0:T(8,128)(2,1)S(1)}, u32[]{:S(2)}, u32[]{:S(2)}) collective-permute-start(bf16[64,3072]{1,0:T(8,128)(2,1)S(1)} %get-tuple-element.33), channel_id=1, source_target_pairs={{0,4},{1,5},{2,6},{3,7},{4,8},{5,9},{6,10},{7,11},{8,12},{9,13},{1... | collective-permute-start | bytes 1179656 | tf_op jit(solution)/shard_map/ppermute | solution.py:42
  62.7 13.0 %collective-permute-start.11 = (bf16[64,3072]{1,0:T(8,128)(2,1)S(1)}, bf16[64,3072]{1,0:T(8,128)(2,1)S(1)}, u32[]{:S(2)}, u32[]{:S(2)}) collective-permute-start(bf16[64,3072]{1,0:T(8,128)(2,1)S(1)} %get-tuple-element.34), channel_id=1, source_target_pairs={{0,12},{1,13},{2,14},{3,15},{4,0},{5,1},{6,2},{7,3},{8,4},{9,5},{1... | collective-permute-start | bytes 1179656 | tf_op jit(solution)/shard_map/ppermute | solution.py:42
  64.1 41.0 %collective-permute-start.28 = (bf16[2,3072,128]{2,1,0:T(8,128)(2,1)S(1)}, bf16[2,3072,128]{2,1,0:T(8,128)(2,1)S(1)}, u32[]{:S(2)}, u32[]{:S(2)}) collective-permute-start(bf16[2,3072,128]{2,1,0:T(8,128)(2,1)S(1)} %flip.1.refs_1_), channel_id=1, source_target_pairs={{0,3},{1,0},{2,1},{3,2},{4,7},{5,4},{6,5},{7,6},{8,11},{9,8},{10,9... | collective-permute-start | bytes 4718600 | tf_op jit(solution)/shard_map/ppermute | solution.py:42
  76.2 9.0 %collective-permute-start.13 = (bf16[32,3072]{1,0:T(8,128)(2,1)S(1)}, bf16[32,3072]{1,0:T(8,128)(2,1)S(1)}, u32[]{:S(2)}, u32[]{:S(2)}) collective-permute-start(bf16[32,3072]{1,0:T(8,128)(2,1)S(1)} %get-tuple-element.38), channel_id=1, source_target_pairs={{0,12},{1,13},{2,14},{3,15},{4,0},{5,1},{6,2},{7,3},{8,4},{9,5},{1... | collective-permute-start | bytes 589832 | tf_op jit(solution)/shard_map/ppermute | solution.py:42
  85.5 9.3 %collective-permute-start.14 = (bf16[64,3072]{1,0:T(8,128)(2,1)S(1)}, bf16[64,3072]{1,0:T(8,128)(2,1)S(1)}, u32[]{:S(2)}, u32[]{:S(2)}) collective-permute-start(bf16[64,3072]{1,0:T(8,128)(2,1)S(1)} %grad_pre.1.refs_0_), channel_id=1, source_target_pairs={{0,12},{1,13},{2,14},{3,15},{4,0},{5,1},{6,2},{7,3},{8,4},{9,5},{1... | collective-permute-start | bytes 1179656 | tf_op jit(solution)/shard_map/ppermute | solution.py:42
  95.6 13.5 %collective-permute-start.30 = (bf16[1,3072,128]{2,1,0:T(8,128)(2,1)S(1)}, bf16[1,3072,128]{2,1,0:T(8,128)(2,1)S(1)}, u32[]{:S(2)}, u32[]{:S(2)}) collective-permute-start(bf16[1,3072,128]{2,1,0:T(8,128)(2,1)S(1)} %slice.94), channel_id=1, source_target_pairs={{0,1},{1,2},{2,3},{3,0},{4,5},{5,6},{6,7},{7,4},{8,9},{9,10},{10,1... | collective-permute-start | bytes 2359304 | tf_op jit(solution)/shard_map/ppermute | solution.py:42
  102.1 12.6 %collective-permute-start.19 = (bf16[128,3072]{1,0:T(8,128)(2,1)S(1)}, bf16[128,3072]{1,0:T(8,128)(2,1)S(1)}, u32[]{:S(2)}, u32[]{:S(2)}) collective-permute-start(bf16[128,3072]{1,0:T(8,128)(2,1)S(1)} %get-tuple-element.45), channel_id=1, source_target_pairs={{0,3},{1,0},{2,1},{3,2},{4,7},{5,4},{6,5},{7,6},{8,11},{9,8},{10,9... | collective-permute-start | bytes 2359304 | tf_op jit(solution)/shard_map/ppermute | solution.py:42
  105.1 13.2 %collective-permute-start.20 = (bf16[128,3072]{1,0:T(8,128)(2,1)S(1)}, bf16[128,3072]{1,0:T(8,128)(2,1)S(1)}, u32[]{:S(2)}, u32[]{:S(2)}) collective-permute-start(bf16[128,3072]{1,0:T(8,128)(2,1)S(1)} %get-tuple-element.46), channel_id=1, source_target_pairs={{0,1},{1,2},{2,3},{3,0},{4,5},{5,6},{6,7},{7,4},{8,9},{9,10},{10,1... | collective-permute-start | bytes 2359304 | tf_op jit(solution)/shard_map/ppermute | solution.py:42
  105.2 17.9 %collective-permute-start.31 = (bf16[1,3072,128]{2,1,0:T(8,128)(2,1)S(1)}, bf16[1,3072,128]{2,1,0:T(8,128)(2,1)S(1)}, u32[]{:S(2)}, u32[]{:S(2)}) collective-permute-start(bf16[1,3072,128]{2,1,0:T(8,128)(2,1)S(1)} %slice.95), channel_id=1, source_target_pairs={{0,3},{1,0},{2,1},{3,2},{4,7},{5,4},{6,5},{7,6},{8,11},{9,8},{10,9... | collective-permute-start | bytes 2359304 | tf_op jit(solution)/shard_map/ppermute | solution.py:42
  108.5 20.2 %collective-permute-start.21 = (bf16[128,3072]{1,0:T(8,128)(2,1)S(1)}, bf16[128,3072]{1,0:T(8,128)(2,1)S(1)}, u32[]{:S(2)}, u32[]{:S(2)}) collective-permute-start(bf16[128,3072]{1,0:T(8,128)(2,1)S(1)} %get-tuple-element.45), channel_id=1, source_target_pairs={{0,1},{1,2},{2,3},{3,0},{4,5},{5,6},{6,7},{7,4},{8,9},{9,10},{10,1... | collective-permute-start | bytes 2359304 | tf_op jit(solution)/shard_map/ppermute | solution.py:42
  109.0 22.4 %collective-permute-start.18 = (bf16[128,3072]{1,0:T(8,128)(2,1)S(1)}, bf16[128,3072]{1,0:T(8,128)(2,1)S(1)}, u32[]{:S(2)}, u32[]{:S(2)}) collective-permute-start(bf16[128,3072]{1,0:T(8,128)(2,1)S(1)} %get-tuple-element.46), channel_id=1, source_target_pairs={{0,3},{1,0},{2,1},{3,2},{4,7},{5,4},{6,5},{7,6},{8,11},{9,8},{10,9... | collective-permute-start | bytes 2359304 | tf_op jit(solution)/shard_map/ppermute | solution.py:42
  114.6 25.3 %collective-permute-start.23 = (bf16[128,3072]{1,0:T(8,128)(2,1)S(1)}, bf16[128,3072]{1,0:T(8,128)(2,1)S(1)}, u32[]{:S(2)}, u32[]{:S(2)}) collective-permute-start(bf16[128,3072]{1,0:T(8,128)(2,1)S(1)} %collective-permute-done.19.refs_2_.refs_3_), channel_id=1, source_target_pairs={{0,3},{1,0},{2,1},{3,2},{4,7},{5,4},{6,5},{7,6},{8,11},{9,8},{10,9... | collective-permute-start | bytes 2359304 | tf_op jit(solution)/shard_map/ppermute | solution.py:42
  118.3 21.6 %collective-permute-start.22 = (bf16[128,3072]{1,0:T(8,128)(2,1)S(1)}, bf16[128,3072]{1,0:T(8,128)(2,1)S(1)}, u32[]{:S(2)}, u32[]{:S(2)}) collective-permute-start(bf16[128,3072]{1,0:T(8,128)(2,1)S(1)} %collective-permute-done.20.refs_3_.refs_6_), channel_id=1, source_target_pairs={{0,1},{1,2},{2,3},{3,0},{4,5},{5,6},{6,7},{7,4},{8,9},{9,10},{10,1... | collective-permute-start | bytes 2359304 | tf_op jit(solution)/shard_map/ppermute | solution.py:42
  144.1 9.7 %collective-permute-start.33 = (bf16[128,384]{1,0:T(8,128)(2,1)S(1)}, bf16[128,384]{1,0:T(8,128)(2,1)S(1)}, u32[]{:S(2)}, u32[]{:S(2)}) collective-permute-start(bf16[128,384]{1,0:T(8,128)(2,1)S(1)} %get-tuple-element.52), channel_id=1, source_target_pairs={{0,32},{16,48},{32,64},{48,80},{64,96},{80,112},{96,0},{112,16},{1... | collective-permute-start | bytes 294920 | tf_op jit(solution)/shard_map/ppermute | solution.py:55
  (20 other events, 155.1 us)

commit v3 on v2

--- a/solution.py
+++ b/solution.py
@@ -72,7 +72,7 @@
         out_specs=[VMEM] * len(outs),
         scratch_shapes=scratch,
         name=name,
-        cost_estimate=pl.CostEstimate(flops=2 * flops, bytes_accessed=moved, transcendentals=0),
+        cost_estimate=pl.CostEstimate(flops=0, bytes_accessed=0, transcendentals=0),
         compiler_params=pltpu.CompilerParams(vmem_limit_bytes=32 * 2**20),
     )(*operands, *order)
 
@@ -92,10 +92,10 @@
     return jax.ShapeDtypeStruct(dims, kind)
 
 
-def gathered_block(place, mine, other, cols, y, z):
+def gathered_block(place, mine, other, y, z):
     start = pl.multiple_of(((y - place[2]) & 3) * 128 + (z % 2) * BLOCK, BLOCK)
     rows = pl.ds(start, BLOCK)
-    return jnp.where(place[3] == z // 2, mine[rows, cols], other[rows, cols])
+    return jnp.where(place[3] == z // 2, mine[rows, :], other[rows, :])
 
 
 def relative(place, y, z):
@@ -121,7 +121,7 @@
 def scaled_kernel(place, mine, other, weight, out):
     for y in range(SIDE):
         for z in range(SIDE):
-            block = gathered_block(place, mine, other, pl.ds(0, out.shape[1]), y, z)
+            block = gathered_block(place, mine, other, y, z)
             here = weight[(y * SIDE + z) * BLOCK : (y * SIDE + z + 1) * BLOCK, :]
             here = jnp.concatenate([here] * (block.shape[1] // 128), axis=1)
             out[rows_of(*relative(place, y, z)), :] = (block.astype(F32) * here).astype(BF16)
@@ -130,8 +130,7 @@
 def inputs_kernel(place, mine, other, flipped, plain):
     for y in range(SIDE):
         for z in range(SIDE):
-            block = gathered_block(place, mine, other, pl.ds(plain.shape[1], plain.shape[1]), y, z)
-            plain[rows_of(*relative(place, y, z)), :] = block
+            plain[rows_of(*relative(place, y, z)), :] = gathered_block(place, mine, other, y, z)
     flipped[...] = plain[...].T
 
 
@@ -194,11 +193,11 @@
     half = [(128, BF16)] * 2
     plus, minus = back_rows(scaled[512:768], w_out, half)
     from_low, from_high = major(plus, 1), major(minus, -1)
-    beside = jnp.concatenate([scaled[384:512], scaled[768:896]], axis=0)
-    plus, minus = back_rows(beside, w_out, half, order_rest)
+    rest = jnp.concatenate([scaled[768:], scaled[:512]], axis=0)
+    minus, to_low, own, to_high, plus = back_rows(
+        rest, w_out, [(128, BF16), (128, F32), (256, F32), (128, F32), (128, BF16)], order_rest
+    )
     low, high = major(plus, 1), major(minus, -1)
-    rest = jnp.concatenate([scaled[896:], scaled[:384]], axis=0)
-    to_low, own, to_high = back_rows(rest, w_out, [(128, F32), (256, F32), (128, F32)])
     plus, minus = call(pass_kernel, [shape((128, hidden), BF16)] * 2, (to_high, to_low, from_low, from_high), "pass")
     low_sum, high_sum = major(plus, 1), major(minus, -1)
     sums = call(
@@ -333,17 +332,17 @@
     )[0]
 
 
-def beside_kernel(one, two, out):
-    depth = one.shape[1]
-    out[:, :depth] = one[...]
-    out[:, depth:] = two[...]
-
-
-def row_gather(one, two):
-    dims = (one.shape[0], 2 * one.shape[1])
-    both = call(beside_kernel, [shape(dims, BF16)], (one, two), "beside")[0]
-    mine = stack((both, move_x(both, -1), move_x(both, -2), move_x(both, -3)))
+def row_gather(a):
+    mine = stack((a, move_x(a, -1), move_x(a, -2), move_x(a, -3)))
     return mine, swap_core(mine)
+
+
+def hold_kernel(a, out):
+    out[...] = a[...]
+
+
+def hold(a, order):
+    return call(hold_kernel, [shape(a.shape, a.dtype)], (a,), "hold", order=order)[0]
 
 
 def shards(inputs, upstream, preact, bias_in, w_in, w_out, lengths):
@@ -352,7 +351,7 @@
     depth, hidden = w_in.shape
     factor = 1024 ** (-0.5)
 
-    mine, other = row_gather(upstream, inputs)
+    up_mine, up_other = row_gather(upstream)
     weight = call(weight_kernel, [shape((1024, 128), F32)], (lengths,), "weight", small=1)[0]
     pre = preact.astype(F32) + bias_in[None, :]
     value, slope = gelu_parts(pre)
@@ -361,32 +360,35 @@
     scaled = call(
         scaled_kernel,
         [shape((1024, depth), BF16)],
-        (place, mine, other, weight),
+        (place, up_mine, up_other, weight),
         "scaled",
         small=1,
+        order=act_sides,
     )[0]
     act_rows = minor_rows(act, *act_sides)
-    sums, minor_parts = reduce_back(scaled, w_out, (), ())
-    act_near = flip(act_rows, ())
-    act_low, act_high = major(act_near, 1), major(act_near, -1)
-    act_pieces = (act_near, act_high, major(act_low[:1], 1), major(act_high[1:], -1), act_low)
-    parts = minor_parts(())
-    grad = call(grad_kernel, [shape((BLOCK, hidden), BF16)], (*parts, slope), "grad_pre")[0]
+    in_mine, in_other = row_gather(hold(inputs, (up_mine,)))
     in_flipped = call(
         inputs_kernel,
         [shape((depth, 1024), BF16)],
-        (place, mine, other),
+        (place, in_mine, in_other),
         "inputs",
         small=1,
         scratch=[pltpu.VMEM((1024, depth), BF16)],
     )[0]
+    sums, minor_parts = reduce_back(scaled, w_out, (), act_rows)
+    act_near = flip(act_rows, sums[:1])
+    act_low, act_high = major(act_near, 1), major(act_near, -1)
+    act_pieces = (act_near, act_high, major(act_low[:1], 1), major(act_high[1:], -1), act_low)
+
+    parts = minor_parts((act_near,))
+    grad = call(grad_kernel, [shape((BLOCK, hidden), BF16)], (*parts, slope), "grad_pre", order=(act_low, act_high))[0]
     grad_w_out = grad_w_out_all(scaled, act_pieces, factor)
-    near = stack(minor_rows(grad, *minor_sides(grad)))
+    near = stack(minor_rows(grad, *minor_sides(grad)), (*act_pieces[2:4], in_flipped))
     low_a, high_b = major(near[:128], 1), major(near[128:], -1)
     low_b, high_a = major(near[128:], 1), major(near[:128], -1)
     far = major(low_a, 1), major(high_b, -1)
     total_near = grad_inputs_rows((near, high_a, high_b, low_a, low_b), w_in, "grad_inputs_near")
-    total_far = grad_inputs_rows(far, w_in, "grad_inputs_far", (total_near, grad_w_out, in_flipped))
+    total_far = grad_inputs_rows(far, w_in, "grad_inputs_far", (total_near, grad_w_out))
     pieces = (near, high_a, high_b, *far, low_a, low_b)
     send, keep = call(
         join_kernel,

time: 157 us -> 155 us (0.987); the launches traced: 154 us -> 155 us
  starting transfers between devices: 49.9 us -> 58.8 us
  local copies, waits for them, and re-layouts: 4.96 us -> 0.43 us
  waiting for transfers between devices: 67.4 us -> 64.7 us
  Pallas kernels: 29.9 us -> 27.5 us
    ppermute x28, starting transfers between devices: 39.2 us -> 43.8 us  [move(): return lax.ppermute(a, ('row', 'col'), pairs)]
    ppermute x6 -> x9, starting transfers between devices: 10.5 us -> 14.7 us  [move_x(): return lax.ppermute(a, 'row', pairs)]
    unnamed x16 -> x12, local copies, waits for them, and re-layouts: 2.7 us -> 0.02 us
    pallas_call x19, Pallas kernels: 29.9 us -> 27.5 us  [call(): pl.pallas_call(body, out_shape=outs, in_specs=[SMEM] * small + [VMEM] * (...]
    ppermute x6 -> x9, waiting for transfers between devices: 7.4 us -> 5.45 us  [move_x(): return lax.ppermute(a, 'row', pairs)]
    slice x4, local copies, waits for them, and re-layouts: 1.91 us -> 0.06 us  [minor_rows(): return (a, high, minor(low[:32], 1), minor(high[32:], -1), low)]
  transfers between devices with their start and end apart: 36 -> 40, of which waited for: 19 -> 20; matrix products, arithmetic and copies ran while one was open for 2% -> 1% of each run, Pallas kernels for 18% -> 14%
where the time goes in v3:
time: 155 us
  waiting for transfers between devices  64.7 us (42%)
  starting transfers between devices  58.8 us (38%)
  Pallas kernels  27.5 us (18%)
  other arithmetic  2.3 us (1%)
    ppermute x28, waiting for transfers between devices, move(): return lax.ppermute(a, ('row', 'col'), pairs)  57.5 us
    ppermute x28, starting transfers between devices, move(): return lax.ppermute(a, ('row', 'col'), pairs)  43.8 us
    pallas_call x19, Pallas kernels, call(): pl.pallas_call(body, out_shape=outs, in_specs=[SMEM] * small + [VMEM] * (...  27.5 us
    ppermute x9, starting transfers between devices, move_x(): return lax.ppermute(a, 'row', pairs)  14.7 us
    ppermute x9, waiting for transfers between devices, move_x(): return lax.ppermute(a, 'row', pairs)  5.45 us
  transfers between devices with their start and end apart: 40, of which 20 were waited for; matrix products, arithmetic and copies ran while one was open for 1% of the time, Pallas kernels for 14%

profile of v3, /device:TPU:24, one launch (start us, length us, event | category | flops | bytes accessed | tf_op | source)
XLA Modules:
  0.0 154.7 jit_solution(15973186179792903775)
XLA Ops:
  0.7 3.1 %collective-permute-start.1 = (bf16[128,384]{1,0:T(8,128)(2,1)}, bf16[128,384]{1,0:T(8,128)(2,1)S(1)}, u32[]{:S(2)}, u32[]{:S(2)}) collective-permute-start(bf16[128,384]{1,0:T(8,128)(2,1)} %refs_0_.3), channel_id=1, source_target_pairs={{0,64},{16,80},{32,96},{48,112},{64,0},{80,16},{96,32},{112,48},{1... | collective-permute-start | bytes 294920 | tf_op jit(solution)/shard_map/ppermute | solution.py:55
  12.5 3.7 %collective-permute-done.5.refs_5_.refs_6_.refs_1_ = bf16[64,3072]{1,0:T(8,128)(2,1)S(1)} collective-permute-done((bf16[64,3072]{1,0:T(8,128)(2,1)S(1)}, bf16[64,3072]{1,0:T(8,128)(2,1)S(1)}, u32[]{:S(2)}, u32[]{:S(2)}) %collective-permute-start.5) | collective-permute-done | bytes 393248 | tf_op jit(solution)/shard_map/ppermute | solution.py:42
  23.3 3.6 %back.2 = (bf16[128,3072]{1,0:T(8,128)(2,1)S(1)}, f32[128,3072]{1,0:T(8,128)S(1)}, f32[256,3072]{1,0:T(8,128)S(1)}, f32[128,3072]{1,0:T(8,128)S(1)}, bf16[128,3072]{1,0:T(8,128)(2,1)S(1)}) custom-call(bf16[768,384]{1,0:T(8,128)(2,1)S(1)} %pad_maximum_fusion.refs_0_, bf16[3072,384]{1,0:T(8,128)(2,1)S(1)} %copy-done), custom_call_target="tpu_custom_call" | custom-call | tf_op jit(solution)/shard_map/back/pallas_call | solution.py:68
  27.0 3.2 %collective-permute-start.7 = (bf16[128,3072]{1,0:T(8,128)(2,1)S(1)}, bf16[128,3072]{1,0:T(8,128)(2,1)S(1)}, u32[]{:S(2)}, u32[]{:S(2)}) collective-permute-start(bf16[128,3072]{1,0:T(8,128)(2,1)S(1)} %get-tuple-element.26), channel_id=1, source_target_pairs={{0,3},{1,0},{2,1},{3,2},{4,7},{5,4},{6,5},{7,6},{8,11},{9,8},{10,9... | collective-permute-start | bytes 2359304 | tf_op jit(solution)/shard_map/ppermute | solution.py:42
  37.0 9.0 %collective-permute-done.13.refs_8_.refs_3_ = bf16[32,3072]{1,0:T(8,128)(2,1)S(1)} collective-permute-done((bf16[32,3072]{1,0:T(8,128)(2,1)S(1)}, bf16[32,3072]{1,0:T(8,128)(2,1)S(1)}, u32[]{:S(2)}, u32[]{:S(2)}) %collective-permute-start.13) | collective-permute-done | bytes 196640 | tf_op jit(solution)/shard_map/ppermute | solution.py:42
  48.0 3.6 %collective-permute-done.12.refs_7_.refs_2_ = bf16[32,3072]{1,0:T(8,128)(2,1)S(1)} collective-permute-done((bf16[32,3072]{1,0:T(8,128)(2,1)S(1)}, bf16[32,3072]{1,0:T(8,128)(2,1)S(1)}, u32[]{:S(2)}, u32[]{:S(2)}) %collective-permute-start.12) | collective-permute-done | bytes 196640 | tf_op jit(solution)/shard_map/ppermute | solution.py:42
  53.3 3.4 %collective-permute-start.19 = (bf16[2,3072,128]{2,1,0:T(8,128)(2,1)S(1)}, bf16[2,3072,128]{2,1,0:T(8,128)(2,1)S(1)}, u32[]{:S(2)}, u32[]{:S(2)}) collective-permute-start(bf16[2,3072,128]{2,1,0:T(8,128)(2,1)S(1)} %flip.1.refs_4_.refs_1_), channel_id=1, source_target_pairs={{0,3},{1,0},{2,1},{3,2},{4,7},{5,4},{6,5},{7,6},{8,11},{9,8},{10,9... | collective-permute-start | bytes 4718600 | tf_op jit(solution)/shard_map/ppermute | solution.py:42
  56.7 3.2 %collective-permute-start.14 = (bf16[64,3072]{1,0:T(8,128)(2,1)S(1)}, bf16[64,3072]{1,0:T(8,128)(2,1)S(1)}, u32[]{:S(2)}, u32[]{:S(2)}) collective-permute-start(bf16[64,3072]{1,0:T(8,128)(2,1)S(1)} %get-tuple-element.34), channel_id=1, source_target_pairs={{0,4},{1,5},{2,6},{3,7},{4,8},{5,9},{6,10},{7,11},{8,12},{9,13},{1... | collective-permute-start | bytes 1179656 | tf_op jit(solution)/shard_map/ppermute | solution.py:42
  59.9 9.6 %collective-permute-done.14.refs_1_ = bf16[64,3072]{1,0:T(8,128)(2,1)S(1)} collective-permute-done((bf16[64,3072]{1,0:T(8,128)(2,1)S(1)}, bf16[64,3072]{1,0:T(8,128)(2,1)S(1)}, u32[]{:S(2)}, u32[]{:S(2)}) %collective-permute-start.14) | collective-permute-done | bytes 393248 | tf_op jit(solution)/shard_map/ppermute | solution.py:42
  69.5 3.7 %collective-permute-done.15.refs_2_ = bf16[64,3072]{1,0:T(8,128)(2,1)S(1)} collective-permute-done((bf16[64,3072]{1,0:T(8,128)(2,1)S(1)}, bf16[64,3072]{1,0:T(8,128)(2,1)S(1)}, u32[]{:S(2)}, u32[]{:S(2)}) %collective-permute-start.15) | collective-permute-done | bytes 393248 | tf_op jit(solution)/shard_map/ppermute | solution.py:42
  75.4 5.5 %collective-permute-done.19.refs_7_.refs_2_ = bf16[2,3072,128]{2,1,0:T(8,128)(2,1)S(1)} collective-permute-done((bf16[2,3072,128]{2,1,0:T(8,128)(2,1)S(1)}, bf16[2,3072,128]{2,1,0:T(8,128)(2,1)S(1)}, u32[]{:S(2)}, u32[]{:S(2)}) %collective-permute-start.19) | collective-permute-done | bytes 1572896 | tf_op jit(solution)/shard_map/ppermute | solution.py:42
  81.0 3.8 %collective-permute-start.25 = (bf16[1,3072,128]{2,1,0:T(8,128)(2,1)S(1)}, bf16[1,3072,128]{2,1,0:T(8,128)(2,1)S(1)}, u32[]{:S(2)}, u32[]{:S(2)}) collective-permute-start(bf16[1,3072,128]{2,1,0:T(8,128)(2,1)S(1)} %slice.83), channel_id=1, source_target_pairs={{0,3},{1,0},{2,1},{3,2},{4,7},{5,4},{6,5},{7,6},{8,11},{9,8},{10,9... | collective-permute-start | bytes 2359304 | tf_op jit(solution)/shard_map/ppermute | solution.py:42
  85.6 3.2 %collective-permute-start.27 = (bf16[128,384]{1,0:T(8,128)(2,1)S(1)}, bf16[128,384]{1,0:T(8,128)(2,1)S(1)}, u32[]{:S(2)}, u32[]{:S(2)}) collective-permute-start(bf16[128,384]{1,0:T(8,128)(2,1)S(1)} %hold.1.refs_0_), channel_id=1, source_target_pairs={{0,64},{16,80},{32,96},{48,112},{64,0},{80,16},{96,32},{112,48},{1... | collective-permute-start | bytes 294920 | tf_op jit(solution)/shard_map/ppermute | solution.py:55
  97.2 3.0 %collective-permute-start.22 = (bf16[32,3072]{1,0:T(8,128)(2,1)S(1)}, bf16[32,3072]{1,0:T(8,128)(2,1)S(1)}, u32[]{:S(2)}, u32[]{:S(2)}) collective-permute-start(bf16[32,3072]{1,0:T(8,128)(2,1)S(1)} %slice.80), channel_id=1, source_target_pairs={{0,4},{1,5},{2,6},{3,7},{4,8},{5,9},{6,10},{7,11},{8,12},{9,13},{1... | collective-permute-start | bytes 589832 | tf_op jit(solution)/shard_map/ppermute | solution.py:42
  103.4 3.8 %collective-permute-done.23.refs_3_ = bf16[32,3072]{1,0:T(8,128)(2,1)S(1)} collective-permute-done((bf16[32,3072]{1,0:T(8,128)(2,1)S(1)}, bf16[32,3072]{1,0:T(8,128)(2,1)S(1)}, u32[]{:S(2)}, u32[]{:S(2)}) %collective-permute-start.23) | collective-permute-done | bytes 196640 | tf_op jit(solution)/shard_map/ppermute | solution.py:42
  107.4 3.0 %collective-permute-start.31 = (bf16[128,3072]{1,0:T(8,128)(2,1)S(1)}, bf16[128,3072]{1,0:T(8,128)(2,1)S(1)}, u32[]{:S(2)}, u32[]{:S(2)}) collective-permute-start(bf16[128,3072]{1,0:T(8,128)(2,1)S(1)} %get-tuple-element.45), channel_id=1, source_target_pairs={{0,3},{1,0},{2,1},{3,2},{4,7},{5,4},{6,5},{7,6},{8,11},{9,8},{10,9... | collective-permute-start | bytes 2359304 | tf_op jit(solution)/shard_map/ppermute | solution.py:42
  110.4 3.3 %collective-permute-start.30 = (bf16[128,3072]{1,0:T(8,128)(2,1)S(1)}, bf16[128,3072]{1,0:T(8,128)(2,1)S(1)}, u32[]{:S(2)}, u32[]{:S(2)}) collective-permute-start(bf16[128,3072]{1,0:T(8,128)(2,1)S(1)} %get-tuple-element.46), channel_id=1, source_target_pairs={{0,3},{1,0},{2,1},{3,2},{4,7},{5,4},{6,5},{7,6},{8,11},{9,8},{10,9... | collective-permute-start | bytes 2359304 | tf_op jit(solution)/shard_map/ppermute | solution.py:42
  113.7 6.2 %collective-permute-done.31.refs_2_.refs_3_ = bf16[128,3072]{1,0:T(8,128)(2,1)S(1)} collective-permute-done((bf16[128,3072]{1,0:T(8,128)(2,1)S(1)}, bf16[128,3072]{1,0:T(8,128)(2,1)S(1)}, u32[]{:S(2)}, u32[]{:S(2)}) %collective-permute-start.31) | collective-permute-done | bytes 786464 | tf_op jit(solution)/shard_map/ppermute | solution.py:42
  119.9 3.7 %collective-permute-start.35 = (bf16[128,3072]{1,0:T(8,128)(2,1)S(1)}, bf16[128,3072]{1,0:T(8,128)(2,1)S(1)}, u32[]{:S(2)}, u32[]{:S(2)}) collective-permute-start(bf16[128,3072]{1,0:T(8,128)(2,1)S(1)} %collective-permute-done.31.refs_2_.refs_3_), channel_id=1, source_target_pairs={{0,3},{1,0},{2,1},{3,2},{4,7},{5,4},{6,5},{7,6},{8,11},{9,8},{10,9... | collective-permute-start | bytes 2359304 | tf_op jit(solution)/shard_map/ppermute | solution.py:42
  123.6 5.7 %grad_w_out.1.refs_4_ = bf16[3072,384]{1,0:T(8,128)(2,1)} custom-call(bf16[1024,384]{1,0:T(8,128)(2,1)S(1)} %scaled.1.refs_0_, bf16[2,3072,128]{2,1,0:T(8,128)(2,1)S(1)} %flip.1.refs_4_.refs_1_, bf16[2,3072,128]{2,1,0:T(8,128)(2,1)S(1)} %collective-permute-done.19.refs_7_.refs_2_, bf16[1,3072,128]{2,1,0:T(8,128)(2,1)S(1)} %collective-permute-done.24.refs_5_.refs_3_, ...), custom_call_target="tpu_custom_call" | custom-call | tf_op jit(solution)/shard_map/grad_w_out/pallas_call | solution.py:68
  132.0 4.2 %grad_inputs_near.1.refs_3_.refs_1_ = f32[768,384]{1,0:T(8,128)S(1)} custom-call(bf16[256,3072]{1,0:T(8,128)(2,1)S(1)} %stack.25.refs_0_.refs_1_, bf16[128,3072]{1,0:T(8,128)(2,1)S(1)} %collective-permute-done.30.refs_1_.refs_2_, bf16[128,3072]{1,0:T(8,128)(2,1)S(1)} %collective-permute-done.31.refs_2_.refs_3_, ...), custom_call_target="tpu_custom_call" | custom-call | tf_op jit(solution)/shard_map/grad_inputs_near/pallas_call | solution.py:68
  136.7 3.7 %collective-permute-done.34.refs_0_.refs_4_ = bf16[128,3072]{1,0:T(8,128)(2,1)S(1)} collective-permute-done((bf16[128,3072]{1,0:T(8,128)(2,1)S(1)}, bf16[128,3072]{1,0:T(8,128)(2,1)S(1)}, u32[]{:S(2)}, u32[]{:S(2)}) %collective-permute-start.34) | collective-permute-done | bytes 786464 | tf_op jit(solution)/shard_map/ppermute | solution.py:42
  145.0 3.0 %collective-permute-start.39 = (bf16[128,384]{1,0:T(8,128)(2,1)S(1)}, bf16[128,384]{1,0:T(8,128)(2,1)S(1)}, u32[]{:S(2)}, u32[]{:S(2)}) collective-permute-start(bf16[128,384]{1,0:T(8,128)(2,1)S(1)} %get-tuple-element.52), channel_id=1, source_target_pairs={{0,96},{16,112},{32,0},{48,16},{64,32},{80,48},{96,64},{112,80},{1... | collective-permute-start | bytes 294920 | tf_op jit(solution)/shard_map/ppermute | solution.py:55
  148.4 4.9 %grad_w_in.1 = bf16[384,3072]{1,0:T(8,128)(2,1)} custom-call(bf16[384,1024]{1,0:T(8,128)(2,1)S(1)} %inputs.1.refs_7_.refs_0_, bf16[256,3072]{1,0:T(8,128)(2,1)S(1)} %stack.25.refs_0_.refs_1_, bf16[128,3072]{1,0:T(8,128)(2,1)S(1)} %collective-permute-done.30.refs_1_.refs_2_, bf16[128,3072]{1,0:T(8,128)(2,1)S(1)} %collective-permute-done.31.refs_2_.refs_3_, ...), custom_call_target="tpu_custom_call" | custom-call | tf_op jit(solution)/shard_map/grad_w_in/pallas_call | solution.py:68
  (104 shorter events, 50.6 us)
Async XLA Ops:
  0.7 9.8 %collective-permute-start.1 = (bf16[128,384]{1,0:T(8,128)(2,1)}, bf16[128,384]{1,0:T(8,128)(2,1)S(1)}, u32[]{:S(2)}, u32[]{:S(2)}) collective-permute-start(bf16[128,384]{1,0:T(8,128)(2,1)} %refs_0_.3), channel_id=1, source_target_pairs={{0,64},{16,80},{32,96},{48,112},{64,0},{80,16},{96,32},{112,48},{1... | collective-permute-start | bytes 294920 | tf_op jit(solution)/shard_map/ppermute | solution.py:55
  7.2 9.1 %collective-permute-start.5 = (bf16[64,3072]{1,0:T(8,128)(2,1)S(1)}, bf16[64,3072]{1,0:T(8,128)(2,1)S(1)}, u32[]{:S(2)}, u32[]{:S(2)}) collective-permute-start(bf16[64,3072]{1,0:T(8,128)(2,1)S(1)} %get-tuple-element.23.refs_5_.refs_0_), channel_id=1, source_target_pairs={{0,12},{1,13},{2,14},{3,15},{4,0},{5,1},{6,2},{7,3},{8,4},{9,5},{1... | collective-permute-start | bytes 1179656 | tf_op jit(solution)/shard_map/ppermute | solution.py:42
  19.0 14.1 %collective-permute-start.8 = (bf16[128,3072]{1,0:T(8,128)(2,1)S(1)}, bf16[128,3072]{1,0:T(8,128)(2,1)S(1)}, u32[]{:S(2)}, u32[]{:S(2)}) collective-permute-start(bf16[128,3072]{1,0:T(8,128)(2,1)S(1)} %get-tuple-element.29), channel_id=1, source_target_pairs={{0,1},{1,2},{2,3},{3,0},{4,5},{5,6},{6,7},{7,4},{8,9},{9,10},{10,1... | collective-permute-start | bytes 2359304 | tf_op jit(solution)/shard_map/ppermute | solution.py:42
  21.0 12.1 %collective-permute-start.9 = (bf16[128,3072]{1,0:T(8,128)(2,1)S(1)}, bf16[128,3072]{1,0:T(8,128)(2,1)S(1)}, u32[]{:S(2)}, u32[]{:S(2)}) collective-permute-start(bf16[128,3072]{1,0:T(8,128)(2,1)S(1)} %get-tuple-element.30), channel_id=1, source_target_pairs={{0,3},{1,0},{2,1},{3,2},{4,7},{5,4},{6,5},{7,6},{8,11},{9,8},{10,9... | collective-permute-start | bytes 2359304 | tf_op jit(solution)/shard_map/ppermute | solution.py:42
  27.0 24.7 %collective-permute-start.6 = (bf16[128,3072]{1,0:T(8,128)(2,1)S(1)}, bf16[128,3072]{1,0:T(8,128)(2,1)S(1)}, u32[]{:S(2)}, u32[]{:S(2)}) collective-permute-start(bf16[128,3072]{1,0:T(8,128)(2,1)S(1)} %get-tuple-element.25), channel_id=1, source_target_pairs={{0,1},{1,2},{2,3},{3,0},{4,5},{5,6},{6,7},{7,4},{8,9},{9,10},{10,1... | collective-permute-start | bytes 2359304 | tf_op jit(solution)/shard_map/ppermute | solution.py:42
  27.0 24.7 %collective-permute-start.7 = (bf16[128,3072]{1,0:T(8,128)(2,1)S(1)}, bf16[128,3072]{1,0:T(8,128)(2,1)S(1)}, u32[]{:S(2)}, u32[]{:S(2)}) collective-permute-start(bf16[128,3072]{1,0:T(8,128)(2,1)S(1)} %get-tuple-element.26), channel_id=1, source_target_pairs={{0,3},{1,0},{2,1},{3,2},{4,7},{5,4},{6,5},{7,6},{8,11},{9,8},{10,9... | collective-permute-start | bytes 2359304 | tf_op jit(solution)/shard_map/ppermute | solution.py:42
  33.4 18.6 %collective-permute-start.10 = (bf16[128,3072]{1,0:T(8,128)(2,1)S(1)}, bf16[128,3072]{1,0:T(8,128)(2,1)S(1)}, u32[]{:S(2)}, u32[]{:S(2)}) collective-permute-start(bf16[128,3072]{1,0:T(8,128)(2,1)S(1)} %get-tuple-element.31), channel_id=1, source_target_pairs={{0,1},{1,2},{2,3},{3,0},{4,5},{5,6},{6,7},{7,4},{8,9},{9,10},{10,1... | collective-permute-start | bytes 2359304 | tf_op jit(solution)/shard_map/ppermute | solution.py:42
  35.3 16.7 %collective-permute-start.11 = (bf16[128,3072]{1,0:T(8,128)(2,1)S(1)}, bf16[128,3072]{1,0:T(8,128)(2,1)S(1)}, u32[]{:S(2)}, u32[]{:S(2)}) collective-permute-start(bf16[128,3072]{1,0:T(8,128)(2,1)S(1)} %get-tuple-element.32), channel_id=1, source_target_pairs={{0,3},{1,0},{2,1},{3,2},{4,7},{5,4},{6,5},{7,6},{8,11},{9,8},{10,9... | collective-permute-start | bytes 2359304 | tf_op jit(solution)/shard_map/ppermute | solution.py:42
  36.9 9.1 %collective-permute-start.13 = (bf16[32,3072]{1,0:T(8,128)(2,1)S(1)}, bf16[32,3072]{1,0:T(8,128)(2,1)S(1)}, u32[]{:S(2)}, u32[]{:S(2)}) collective-permute-start(bf16[32,3072]{1,0:T(8,128)(2,1)S(1)} %slice.77), channel_id=1, source_target_pairs={{0,12},{1,13},{2,14},{3,15},{4,0},{5,1},{6,2},{7,3},{8,4},{9,5},{1... | collective-permute-start | bytes 589832 | tf_op jit(solution)/shard_map/ppermute | solution.py:42
  53.3 27.6 %collective-permute-start.19 = (bf16[2,3072,128]{2,1,0:T(8,128)(2,1)S(1)}, bf16[2,3072,128]{2,1,0:T(8,128)(2,1)S(1)}, u32[]{:S(2)}, u32[]{:S(2)}) collective-permute-start(bf16[2,3072,128]{2,1,0:T(8,128)(2,1)S(1)} %flip.1.refs_4_.refs_1_), channel_id=1, source_target_pairs={{0,3},{1,0},{2,1},{3,2},{4,7},{5,4},{6,5},{7,6},{8,11},{9,8},{10,9... | collective-permute-start | bytes 4718600 | tf_op jit(solution)/shard_map/ppermute | solution.py:42
  56.7 28.1 %collective-permute-start.18 = (bf16[2,3072,128]{2,1,0:T(8,128)(2,1)S(1)}, bf16[2,3072,128]{2,1,0:T(8,128)(2,1)S(1)}, u32[]{:S(2)}, u32[]{:S(2)}) collective-permute-start(bf16[2,3072,128]{2,1,0:T(8,128)(2,1)S(1)} %flip.1.refs_4_.refs_1_), channel_id=1, source_target_pairs={{0,1},{1,2},{2,3},{3,0},{4,5},{5,6},{6,7},{7,4},{8,9},{9,10},{10,1... | collective-permute-start | bytes 4718600 | tf_op jit(solution)/shard_map/ppermute | solution.py:42
  56.7 12.8 %collective-permute-start.14 = (bf16[64,3072]{1,0:T(8,128)(2,1)S(1)}, bf16[64,3072]{1,0:T(8,128)(2,1)S(1)}, u32[]{:S(2)}, u32[]{:S(2)}) collective-permute-start(bf16[64,3072]{1,0:T(8,128)(2,1)S(1)} %get-tuple-element.34), channel_id=1, source_target_pairs={{0,4},{1,5},{2,6},{3,7},{4,8},{5,9},{6,10},{7,11},{8,12},{9,13},{1... | collective-permute-start | bytes 1179656 | tf_op jit(solution)/shard_map/ppermute | solution.py:42
  59.9 13.3 %collective-permute-start.15 = (bf16[64,3072]{1,0:T(8,128)(2,1)S(1)}, bf16[64,3072]{1,0:T(8,128)(2,1)S(1)}, u32[]{:S(2)}, u32[]{:S(2)}) collective-permute-start(bf16[64,3072]{1,0:T(8,128)(2,1)S(1)} %get-tuple-element.35), channel_id=1, source_target_pairs={{0,12},{1,13},{2,14},{3,15},{4,0},{5,1},{6,2},{7,3},{8,4},{9,5},{1... | collective-permute-start | bytes 1179656 | tf_op jit(solution)/shard_map/ppermute | solution.py:42
  73.3 12.3 %collective-permute-start.16 = (bf16[32,3072]{1,0:T(8,128)(2,1)S(1)}, bf16[32,3072]{1,0:T(8,128)(2,1)S(1)}, u32[]{:S(2)}, u32[]{:S(2)}) collective-permute-start(bf16[32,3072]{1,0:T(8,128)(2,1)S(1)} %get-tuple-element.38), channel_id=1, source_target_pairs={{0,4},{1,5},{2,6},{3,7},{4,8},{5,9},{6,10},{7,11},{8,12},{9,13},{1... | collective-permute-start | bytes 589832 | tf_op jit(solution)/shard_map/ppermute | solution.py:42
  73.4 15.4 %collective-permute-start.17 = (bf16[32,3072]{1,0:T(8,128)(2,1)S(1)}, bf16[32,3072]{1,0:T(8,128)(2,1)S(1)}, u32[]{:S(2)}, u32[]{:S(2)}) collective-permute-start(bf16[32,3072]{1,0:T(8,128)(2,1)S(1)} %get-tuple-element.39), channel_id=1, source_target_pairs={{0,12},{1,13},{2,14},{3,15},{4,0},{5,1},{6,2},{7,3},{8,4},{9,5},{1... | collective-permute-start | bytes 589832 | tf_op jit(solution)/shard_map/ppermute | solution.py:42
  81.0 26.2 %collective-permute-start.25 = (bf16[1,3072,128]{2,1,0:T(8,128)(2,1)S(1)}, bf16[1,3072,128]{2,1,0:T(8,128)(2,1)S(1)}, u32[]{:S(2)}, u32[]{:S(2)}) collective-permute-start(bf16[1,3072,128]{2,1,0:T(8,128)(2,1)S(1)} %slice.83), channel_id=1, source_target_pairs={{0,3},{1,0},{2,1},{3,2},{4,7},{5,4},{6,5},{7,6},{8,11},{9,8},{10,9... | collective-permute-start | bytes 2359304 | tf_op jit(solution)/shard_map/ppermute | solution.py:42
  84.8 22.4 %collective-permute-start.24 = (bf16[1,3072,128]{2,1,0:T(8,128)(2,1)S(1)}, bf16[1,3072,128]{2,1,0:T(8,128)(2,1)S(1)}, u32[]{:S(2)}, u32[]{:S(2)}) collective-permute-start(bf16[1,3072,128]{2,1,0:T(8,128)(2,1)S(1)} %slice.82), channel_id=1, source_target_pairs={{0,1},{1,2},{2,3},{3,0},{4,5},{5,6},{6,7},{7,4},{8,9},{9,10},{10,1... | collective-permute-start | bytes 2359304 | tf_op jit(solution)/shard_map/ppermute | solution.py:42
  91.0 9.2 %collective-permute-start.20 = (bf16[64,3072]{1,0:T(8,128)(2,1)S(1)}, bf16[64,3072]{1,0:T(8,128)(2,1)S(1)}, u32[]{:S(2)}, u32[]{:S(2)}) collective-permute-start(bf16[64,3072]{1,0:T(8,128)(2,1)S(1)} %grad_pre.1.refs_0_), channel_id=1, source_target_pairs={{0,12},{1,13},{2,14},{3,15},{4,0},{5,1},{6,2},{7,3},{8,4},{9,5},{1... | collective-permute-start | bytes 1179656 | tf_op jit(solution)/shard_map/ppermute | solution.py:42
  107.4 12.5 %collective-permute-start.31 = (bf16[128,3072]{1,0:T(8,128)(2,1)S(1)}, bf16[128,3072]{1,0:T(8,128)(2,1)S(1)}, u32[]{:S(2)}, u32[]{:S(2)}) collective-permute-start(bf16[128,3072]{1,0:T(8,128)(2,1)S(1)} %get-tuple-element.45), channel_id=1, source_target_pairs={{0,3},{1,0},{2,1},{3,2},{4,7},{5,4},{6,5},{7,6},{8,11},{9,8},{10,9... | collective-permute-start | bytes 2359304 | tf_op jit(solution)/shard_map/ppermute | solution.py:42
  110.4 13.2 %collective-permute-start.32 = (bf16[128,3072]{1,0:T(8,128)(2,1)S(1)}, bf16[128,3072]{1,0:T(8,128)(2,1)S(1)}, u32[]{:S(2)}, u32[]{:S(2)}) collective-permute-start(bf16[128,3072]{1,0:T(8,128)(2,1)S(1)} %get-tuple-element.46), channel_id=1, source_target_pairs={{0,1},{1,2},{2,3},{3,0},{4,5},{5,6},{6,7},{7,4},{8,9},{9,10},{10,1... | collective-permute-start | bytes 2359304 | tf_op jit(solution)/shard_map/ppermute | solution.py:42
  110.4 21.6 %collective-permute-start.33 = (bf16[128,3072]{1,0:T(8,128)(2,1)S(1)}, bf16[128,3072]{1,0:T(8,128)(2,1)S(1)}, u32[]{:S(2)}, u32[]{:S(2)}) collective-permute-start(bf16[128,3072]{1,0:T(8,128)(2,1)S(1)} %get-tuple-element.45), channel_id=1, source_target_pairs={{0,1},{1,2},{2,3},{3,0},{4,5},{5,6},{6,7},{7,4},{8,9},{9,10},{10,1... | collective-permute-start | bytes 2359304 | tf_op jit(solution)/shard_map/ppermute | solution.py:42
  110.4 21.6 %collective-permute-start.30 = (bf16[128,3072]{1,0:T(8,128)(2,1)S(1)}, bf16[128,3072]{1,0:T(8,128)(2,1)S(1)}, u32[]{:S(2)}, u32[]{:S(2)}) collective-permute-start(bf16[128,3072]{1,0:T(8,128)(2,1)S(1)} %get-tuple-element.46), channel_id=1, source_target_pairs={{0,3},{1,0},{2,1},{3,2},{4,7},{5,4},{6,5},{7,6},{8,11},{9,8},{10,9... | collective-permute-start | bytes 2359304 | tf_op jit(solution)/shard_map/ppermute | solution.py:42
  119.9 16.9 %collective-permute-start.35 = (bf16[128,3072]{1,0:T(8,128)(2,1)S(1)}, bf16[128,3072]{1,0:T(8,128)(2,1)S(1)}, u32[]{:S(2)}, u32[]{:S(2)}) collective-permute-start(bf16[128,3072]{1,0:T(8,128)(2,1)S(1)} %collective-permute-done.31.refs_2_.refs_3_), channel_id=1, source_target_pairs={{0,3},{1,0},{2,1},{3,2},{4,7},{5,4},{6,5},{7,6},{8,11},{9,8},{10,9... | collective-permute-start | bytes 2359304 | tf_op jit(solution)/shard_map/ppermute | solution.py:42
  123.6 16.8 %collective-permute-start.34 = (bf16[128,3072]{1,0:T(8,128)(2,1)S(1)}, bf16[128,3072]{1,0:T(8,128)(2,1)S(1)}, u32[]{:S(2)}, u32[]{:S(2)}) collective-permute-start(bf16[128,3072]{1,0:T(8,128)(2,1)S(1)} %collective-permute-done.32.refs_3_.refs_6_), channel_id=1, source_target_pairs={{0,1},{1,2},{2,3},{3,0},{4,5},{5,6},{6,7},{7,4},{8,9},{9,10},{10,1... | collective-permute-start | bytes 2359304 | tf_op jit(solution)/shard_map/ppermute | solution.py:42
  (22 other events, 152.5 us)

commit v4 on v3

--- a/solution.py
+++ b/solution.py
@@ -363,7 +363,7 @@
         (place, up_mine, up_other, weight),
         "scaled",
         small=1,
-        order=act_sides,
+        order=act_sides[:1],
     )[0]
     act_rows = minor_rows(act, *act_sides)
     in_mine, in_other = row_gather(hold(inputs, (up_mine,)))

time: 155 us -> 157 us (1.013)
  waiting for transfers between devices: 64.7 us -> 71.3 us
  starting transfers between devices: 58.8 us -> 54.2 us
    ppermute x28, starting transfers between devices: 43.8 us -> 39.7 us  [move(): return lax.ppermute(a, ('row', 'col'), pairs)]
    ppermute x28, waiting for transfers between devices: 57.5 us -> 60.9 us  [move(): return lax.ppermute(a, ('row', 'col'), pairs)]
    ppermute x9, waiting for transfers between devices: 5.45 us -> 8.71 us  [move_x(): return lax.ppermute(a, 'row', pairs)]
  transfers between devices with their start and end apart: 40 -> 40, of which waited for: 20 -> 22; matrix products, arithmetic and copies ran while one was open for 1% -> 1% of each run, Pallas kernels for 14% -> 14%
where the time goes in v4:
time: 157 us
  waiting for transfers between devices  71.3 us (45%)
  starting transfers between devices  54.2 us (35%)
  Pallas kernels  27.6 us (18%)
  other arithmetic  2.3 us (1%)
    ppermute x28, waiting for transfers between devices, move(): return lax.ppermute(a, ('row', 'col'), pairs)  60.9 us
    ppermute x28, starting transfers between devices, move(): return lax.ppermute(a, ('row', 'col'), pairs)  39.7 us
    pallas_call x19, Pallas kernels, call(): pl.pallas_call(body, out_shape=outs, in_specs=[SMEM] * small + [VMEM] * (...  27.6 us
    ppermute x9, starting transfers between devices, move_x(): return lax.ppermute(a, 'row', pairs)  14.3 us
    ppermute x9, waiting for transfers between devices, move_x(): return lax.ppermute(a, 'row', pairs)  8.71 us
  transfers between devices with their start and end apart: 40, of which 22 were waited for; matrix products, arithmetic and copies ran while one was open for 1% of the time, Pallas kernels for 14%

profile of v4, /device:TPU:24, one launch (start us, length us, event | category | flops | bytes accessed | tf_op | source)
XLA Modules:
  0.0 156.8 jit_solution(4503241749463883340)
XLA Ops:
  0.7 3.1 %collective-permute-start.1 = (bf16[128,384]{1,0:T(8,128)(2,1)}, bf16[128,384]{1,0:T(8,128)(2,1)S(1)}, u32[]{:S(2)}, u32[]{:S(2)}) collective-permute-start(bf16[128,384]{1,0:T(8,128)(2,1)} %refs_0_.3), channel_id=1, source_target_pairs={{0,64},{16,80},{32,96},{48,112},{64,0},{80,16},{96,32},{112,48},{1... | collective-permute-start | bytes 294920 | tf_op jit(solution)/shard_map/ppermute | solution.py:55
  22.8 3.6 %back.2 = (bf16[128,3072]{1,0:T(8,128)(2,1)S(1)}, f32[128,3072]{1,0:T(8,128)S(1)}, f32[256,3072]{1,0:T(8,128)S(1)}, f32[128,3072]{1,0:T(8,128)S(1)}, bf16[128,3072]{1,0:T(8,128)(2,1)S(1)}) custom-call(bf16[768,384]{1,0:T(8,128)(2,1)S(1)} %pad_maximum_fusion.refs_0_, bf16[3072,384]{1,0:T(8,128)(2,1)S(1)} %copy-done), custom_call_target="tpu_custom_call" | custom-call | tf_op jit(solution)/shard_map/back/pallas_call | solution.py:68
  26.6 3.2 %collective-permute-start.6 = (bf16[128,3072]{1,0:T(8,128)(2,1)S(1)}, bf16[128,3072]{1,0:T(8,128)(2,1)S(1)}, u32[]{:S(2)}, u32[]{:S(2)}) collective-permute-start(bf16[128,3072]{1,0:T(8,128)(2,1)S(1)} %get-tuple-element.26), channel_id=1, source_target_pairs={{0,3},{1,0},{2,1},{3,2},{4,7},{5,4},{6,5},{7,6},{8,11},{9,8},{10,9... | collective-permute-start | bytes 2359304 | tf_op jit(solution)/shard_map/ppermute | solution.py:42
  31.9 3.0 %collective-permute-done.8.refs_3_ = bf16[128,3072]{1,0:T(8,128)(2,1)S(1)} collective-permute-done((bf16[128,3072]{1,0:T(8,128)(2,1)S(1)}, bf16[128,3072]{1,0:T(8,128)(2,1)S(1)}, u32[]{:S(2)}, u32[]{:S(2)}) %collective-permute-start.8) | collective-permute-done | bytes 786464 | tf_op jit(solution)/shard_map/ppermute | solution.py:42
  35.9 3.2 %collective-permute-start.10 = (bf16[128,3072]{1,0:T(8,128)(2,1)S(1)}, bf16[128,3072]{1,0:T(8,128)(2,1)S(1)}, u32[]{:S(2)}, u32[]{:S(2)}) collective-permute-start(bf16[128,3072]{1,0:T(8,128)(2,1)S(1)} %get-tuple-element.32), channel_id=1, source_target_pairs={{0,3},{1,0},{2,1},{3,2},{4,7},{5,4},{6,5},{7,6},{8,11},{9,8},{10,9... | collective-permute-start | bytes 2359304 | tf_op jit(solution)/shard_map/ppermute | solution.py:42
  39.9 8.3 %collective-permute-done.13.refs_8_.refs_3_ = bf16[32,3072]{1,0:T(8,128)(2,1)S(1)} collective-permute-done((bf16[32,3072]{1,0:T(8,128)(2,1)S(1)}, bf16[32,3072]{1,0:T(8,128)(2,1)S(1)}, u32[]{:S(2)}, u32[]{:S(2)}) %collective-permute-start.13) | collective-permute-done | bytes 196640 | tf_op jit(solution)/shard_map/ppermute | solution.py:42
  48.6 5.3 %collective-permute-done.12.refs_7_.refs_2_ = bf16[32,3072]{1,0:T(8,128)(2,1)S(1)} collective-permute-done((bf16[32,3072]{1,0:T(8,128)(2,1)S(1)}, bf16[32,3072]{1,0:T(8,128)(2,1)S(1)}, u32[]{:S(2)}, u32[]{:S(2)}) %collective-permute-start.12) | collective-permute-done | bytes 196640 | tf_op jit(solution)/shard_map/ppermute | solution.py:42
  55.2 3.7 %collective-permute-start.19 = (bf16[2,3072,128]{2,1,0:T(8,128)(2,1)S(1)}, bf16[2,3072,128]{2,1,0:T(8,128)(2,1)S(1)}, u32[]{:S(2)}, u32[]{:S(2)}) collective-permute-start(bf16[2,3072,128]{2,1,0:T(8,128)(2,1)S(1)} %flip.1.refs_4_.refs_1_), channel_id=1, source_target_pairs={{0,3},{1,0},{2,1},{3,2},{4,7},{5,4},{6,5},{7,6},{8,11},{9,8},{10,9... | collective-permute-start | bytes 4718600 | tf_op jit(solution)/shard_map/ppermute | solution.py:42
  60.9 10.0 %collective-permute-done.14.refs_1_ = bf16[64,3072]{1,0:T(8,128)(2,1)S(1)} collective-permute-done((bf16[64,3072]{1,0:T(8,128)(2,1)S(1)}, bf16[64,3072]{1,0:T(8,128)(2,1)S(1)}, u32[]{:S(2)}, u32[]{:S(2)}) %collective-permute-start.14) | collective-permute-done | bytes 393248 | tf_op jit(solution)/shard_map/ppermute | solution.py:42
  71.0 2.8 %collective-permute-done.15.refs_2_ = bf16[64,3072]{1,0:T(8,128)(2,1)S(1)} collective-permute-done((bf16[64,3072]{1,0:T(8,128)(2,1)S(1)}, bf16[64,3072]{1,0:T(8,128)(2,1)S(1)}, u32[]{:S(2)}, u32[]{:S(2)}) %collective-permute-start.15) | collective-permute-done | bytes 393248 | tf_op jit(solution)/shard_map/ppermute | solution.py:42
  76.0 7.2 %collective-permute-done.19.refs_7_.refs_2_ = bf16[2,3072,128]{2,1,0:T(8,128)(2,1)S(1)} collective-permute-done((bf16[2,3072,128]{2,1,0:T(8,128)(2,1)S(1)}, bf16[2,3072,128]{2,1,0:T(8,128)(2,1)S(1)}, u32[]{:S(2)}, u32[]{:S(2)}) %collective-permute-start.19) | collective-permute-done | bytes 1572896 | tf_op jit(solution)/shard_map/ppermute | solution.py:42
  83.2 3.8 %collective-permute-start.25 = (bf16[1,3072,128]{2,1,0:T(8,128)(2,1)S(1)}, bf16[1,3072,128]{2,1,0:T(8,128)(2,1)S(1)}, u32[]{:S(2)}, u32[]{:S(2)}) collective-permute-start(bf16[1,3072,128]{2,1,0:T(8,128)(2,1)S(1)} %slice.83), channel_id=1, source_target_pairs={{0,3},{1,0},{2,1},{3,2},{4,7},{5,4},{6,5},{7,6},{8,11},{9,8},{10,9... | collective-permute-start | bytes 2359304 | tf_op jit(solution)/shard_map/ppermute | solution.py:42
  87.2 3.1 %collective-permute-start.27 = (bf16[128,384]{1,0:T(8,128)(2,1)S(1)}, bf16[128,384]{1,0:T(8,128)(2,1)S(1)}, u32[]{:S(2)}, u32[]{:S(2)}) collective-permute-start(bf16[128,384]{1,0:T(8,128)(2,1)S(1)} %hold.1.refs_0_), channel_id=1, source_target_pairs={{0,64},{16,80},{32,96},{48,112},{64,0},{80,16},{96,32},{112,48},{1... | collective-permute-start | bytes 294920 | tf_op jit(solution)/shard_map/ppermute | solution.py:55
  104.7 4.3 %collective-permute-done.23.refs_3_ = bf16[32,3072]{1,0:T(8,128)(2,1)S(1)} collective-permute-done((bf16[32,3072]{1,0:T(8,128)(2,1)S(1)}, bf16[32,3072]{1,0:T(8,128)(2,1)S(1)}, u32[]{:S(2)}, u32[]{:S(2)}) %collective-permute-start.23) | collective-permute-done | bytes 196640 | tf_op jit(solution)/shard_map/ppermute | solution.py:42
  109.2 3.3 %collective-permute-start.31 = (bf16[128,3072]{1,0:T(8,128)(2,1)S(1)}, bf16[128,3072]{1,0:T(8,128)(2,1)S(1)}, u32[]{:S(2)}, u32[]{:S(2)}) collective-permute-start(bf16[128,3072]{1,0:T(8,128)(2,1)S(1)} %get-tuple-element.45), channel_id=1, source_target_pairs={{0,3},{1,0},{2,1},{3,2},{4,7},{5,4},{6,5},{7,6},{8,11},{9,8},{10,9... | collective-permute-start | bytes 2359304 | tf_op jit(solution)/shard_map/ppermute | solution.py:42
  112.5 3.3 %collective-permute-start.30 = (bf16[128,3072]{1,0:T(8,128)(2,1)S(1)}, bf16[128,3072]{1,0:T(8,128)(2,1)S(1)}, u32[]{:S(2)}, u32[]{:S(2)}) collective-permute-start(bf16[128,3072]{1,0:T(8,128)(2,1)S(1)} %get-tuple-element.46), channel_id=1, source_target_pairs={{0,3},{1,0},{2,1},{3,2},{4,7},{5,4},{6,5},{7,6},{8,11},{9,8},{10,9... | collective-permute-start | bytes 2359304 | tf_op jit(solution)/shard_map/ppermute | solution.py:42
  115.8 6.2 %collective-permute-done.31.refs_2_.refs_3_ = bf16[128,3072]{1,0:T(8,128)(2,1)S(1)} collective-permute-done((bf16[128,3072]{1,0:T(8,128)(2,1)S(1)}, bf16[128,3072]{1,0:T(8,128)(2,1)S(1)}, u32[]{:S(2)}, u32[]{:S(2)}) %collective-permute-start.31) | collective-permute-done | bytes 786464 | tf_op jit(solution)/shard_map/ppermute | solution.py:42
  122.0 3.7 %collective-permute-start.35 = (bf16[128,3072]{1,0:T(8,128)(2,1)S(1)}, bf16[128,3072]{1,0:T(8,128)(2,1)S(1)}, u32[]{:S(2)}, u32[]{:S(2)}) collective-permute-start(bf16[128,3072]{1,0:T(8,128)(2,1)S(1)} %collective-permute-done.31.refs_2_.refs_3_), channel_id=1, source_target_pairs={{0,3},{1,0},{2,1},{3,2},{4,7},{5,4},{6,5},{7,6},{8,11},{9,8},{10,9... | collective-permute-start | bytes 2359304 | tf_op jit(solution)/shard_map/ppermute | solution.py:42
  125.7 5.7 %grad_w_out.1.refs_4_ = bf16[3072,384]{1,0:T(8,128)(2,1)} custom-call(bf16[1024,384]{1,0:T(8,128)(2,1)S(1)} %scaled.1.refs_0_, bf16[2,3072,128]{2,1,0:T(8,128)(2,1)S(1)} %flip.1.refs_4_.refs_1_, bf16[2,3072,128]{2,1,0:T(8,128)(2,1)S(1)} %collective-permute-done.19.refs_7_.refs_2_, bf16[1,3072,128]{2,1,0:T(8,128)(2,1)S(1)} %collective-permute-done.24.refs_5_.refs_3_, ...), custom_call_target="tpu_custom_call" | custom-call | tf_op jit(solution)/shard_map/grad_w_out/pallas_call | solution.py:68
  131.4 2.8 %collective-permute-done.33.refs_4_.refs_7_ = bf16[128,3072]{1,0:T(8,128)(2,1)S(1)} collective-permute-done((bf16[128,3072]{1,0:T(8,128)(2,1)S(1)}, bf16[128,3072]{1,0:T(8,128)(2,1)S(1)}, u32[]{:S(2)}, u32[]{:S(2)}) %collective-permute-start.33) | collective-permute-done | bytes 786464 | tf_op jit(solution)/shard_map/ppermute | solution.py:42
  134.1 4.2 %grad_inputs_near.1.refs_3_.refs_1_ = f32[768,384]{1,0:T(8,128)S(1)} custom-call(bf16[256,3072]{1,0:T(8,128)(2,1)S(1)} %stack.25.refs_0_.refs_1_, bf16[128,3072]{1,0:T(8,128)(2,1)S(1)} %collective-permute-done.30.refs_1_.refs_2_, bf16[128,3072]{1,0:T(8,128)(2,1)S(1)} %collective-permute-done.31.refs_2_.refs_3_, ...), custom_call_target="tpu_custom_call" | custom-call | tf_op jit(solution)/shard_map/grad_inputs_near/pallas_call | solution.py:68
  138.9 3.7 %collective-permute-done.34.refs_0_.refs_4_ = bf16[128,3072]{1,0:T(8,128)(2,1)S(1)} collective-permute-done((bf16[128,3072]{1,0:T(8,128)(2,1)S(1)}, bf16[128,3072]{1,0:T(8,128)(2,1)S(1)}, u32[]{:S(2)}, u32[]{:S(2)}) %collective-permute-start.34) | collective-permute-done | bytes 786464 | tf_op jit(solution)/shard_map/ppermute | solution.py:42
  146.8 3.2 %collective-permute-start.39 = (bf16[128,384]{1,0:T(8,128)(2,1)S(1)}, bf16[128,384]{1,0:T(8,128)(2,1)S(1)}, u32[]{:S(2)}, u32[]{:S(2)}) collective-permute-start(bf16[128,384]{1,0:T(8,128)(2,1)S(1)} %get-tuple-element.52), channel_id=1, source_target_pairs={{0,96},{16,112},{32,0},{48,16},{64,32},{80,48},{96,64},{112,80},{1... | collective-permute-start | bytes 294920 | tf_op jit(solution)/shard_map/ppermute | solution.py:55
  150.2 4.9 %grad_w_in.1 = bf16[384,3072]{1,0:T(8,128)(2,1)} custom-call(bf16[384,1024]{1,0:T(8,128)(2,1)S(1)} %inputs.1.refs_7_.refs_0_, bf16[256,3072]{1,0:T(8,128)(2,1)S(1)} %stack.25.refs_0_.refs_1_, bf16[128,3072]{1,0:T(8,128)(2,1)S(1)} %collective-permute-done.30.refs_1_.refs_2_, bf16[128,3072]{1,0:T(8,128)(2,1)S(1)} %collective-permute-done.31.refs_2_.refs_3_, ...), custom_call_target="tpu_custom_call" | custom-call | tf_op jit(solution)/shard_map/grad_w_in/pallas_call | solution.py:68
  (104 shorter events, 50.2 us)
Async XLA Ops:
  17.8 14.1 %collective-permute-start.7 = (bf16[128,3072]{1,0:T(8,128)(2,1)S(1)}, bf16[128,3072]{1,0:T(8,128)(2,1)S(1)}, u32[]{:S(2)}, u32[]{:S(2)}) collective-permute-start(bf16[128,3072]{1,0:T(8,128)(2,1)S(1)} %get-tuple-element.29), channel_id=1, source_target_pairs={{0,1},{1,2},{2,3},{3,0},{4,5},{5,6},{6,7},{7,4},{8,9},{9,10},{10,1... | collective-permute-start | bytes 2359304 | tf_op jit(solution)/shard_map/ppermute | solution.py:42
  19.8 15.1 %collective-permute-start.8 = (bf16[128,3072]{1,0:T(8,128)(2,1)S(1)}, bf16[128,3072]{1,0:T(8,128)(2,1)S(1)}, u32[]{:S(2)}, u32[]{:S(2)}) collective-permute-start(bf16[128,3072]{1,0:T(8,128)(2,1)S(1)} %get-tuple-element.30), channel_id=1, source_target_pairs={{0,3},{1,0},{2,1},{3,2},{4,7},{5,4},{6,5},{7,6},{8,11},{9,8},{10,9... | collective-permute-start | bytes 2359304 | tf_op jit(solution)/shard_map/ppermute | solution.py:42
  22.0 17.1 %collective-permute-start.11 = (bf16[64,3072]{1,0:T(8,128)(2,1)S(1)}, bf16[64,3072]{1,0:T(8,128)(2,1)S(1)}, u32[]{:S(2)}, u32[]{:S(2)}) collective-permute-start(bf16[64,3072]{1,0:T(8,128)(2,1)S(1)} %get-tuple-element.23.refs_5_.refs_0_), channel_id=1, source_target_pairs={{0,12},{1,13},{2,14},{3,15},{4,0},{5,1},{6,2},{7,3},{8,4},{9,5},{1... | collective-permute-start | bytes 1179656 | tf_op jit(solution)/shard_map/ppermute | solution.py:42
  26.5 27.4 %collective-permute-start.5 = (bf16[128,3072]{1,0:T(8,128)(2,1)S(1)}, bf16[128,3072]{1,0:T(8,128)(2,1)S(1)}, u32[]{:S(2)}, u32[]{:S(2)}) collective-permute-start(bf16[128,3072]{1,0:T(8,128)(2,1)S(1)} %get-tuple-element.25), channel_id=1, source_target_pairs={{0,1},{1,2},{2,3},{3,0},{4,5},{5,6},{6,7},{7,4},{8,9},{9,10},{10,1... | collective-permute-start | bytes 2359304 | tf_op jit(solution)/shard_map/ppermute | solution.py:42
  26.6 27.3 %collective-permute-start.6 = (bf16[128,3072]{1,0:T(8,128)(2,1)S(1)}, bf16[128,3072]{1,0:T(8,128)(2,1)S(1)}, u32[]{:S(2)}, u32[]{:S(2)}) collective-permute-start(bf16[128,3072]{1,0:T(8,128)(2,1)S(1)} %get-tuple-element.26), channel_id=1, source_target_pairs={{0,3},{1,0},{2,1},{3,2},{4,7},{5,4},{6,5},{7,6},{8,11},{9,8},{10,9... | collective-permute-start | bytes 2359304 | tf_op jit(solution)/shard_map/ppermute | solution.py:42
  35.2 18.7 %collective-permute-start.9 = (bf16[128,3072]{1,0:T(8,128)(2,1)S(1)}, bf16[128,3072]{1,0:T(8,128)(2,1)S(1)}, u32[]{:S(2)}, u32[]{:S(2)}) collective-permute-start(bf16[128,3072]{1,0:T(8,128)(2,1)S(1)} %get-tuple-element.31), channel_id=1, source_target_pairs={{0,1},{1,2},{2,3},{3,0},{4,5},{5,6},{6,7},{7,4},{8,9},{9,10},{10,1... | collective-permute-start | bytes 2359304 | tf_op jit(solution)/shard_map/ppermute | solution.py:42
  35.9 18.1 %collective-permute-start.10 = (bf16[128,3072]{1,0:T(8,128)(2,1)S(1)}, bf16[128,3072]{1,0:T(8,128)(2,1)S(1)}, u32[]{:S(2)}, u32[]{:S(2)}) collective-permute-start(bf16[128,3072]{1,0:T(8,128)(2,1)S(1)} %get-tuple-element.32), channel_id=1, source_target_pairs={{0,3},{1,0},{2,1},{3,2},{4,7},{5,4},{6,5},{7,6},{8,11},{9,8},{10,9... | collective-permute-start | bytes 2359304 | tf_op jit(solution)/shard_map/ppermute | solution.py:42
  39.1 9.1 %collective-permute-start.13 = (bf16[32,3072]{1,0:T(8,128)(2,1)S(1)}, bf16[32,3072]{1,0:T(8,128)(2,1)S(1)}, u32[]{:S(2)}, u32[]{:S(2)}) collective-permute-start(bf16[32,3072]{1,0:T(8,128)(2,1)S(1)} %slice.77), channel_id=1, source_target_pairs={{0,12},{1,13},{2,14},{3,15},{4,0},{5,1},{6,2},{7,3},{8,4},{9,5},{1... | collective-permute-start | bytes 589832 | tf_op jit(solution)/shard_map/ppermute | solution.py:42
  55.2 28.0 %collective-permute-start.19 = (bf16[2,3072,128]{2,1,0:T(8,128)(2,1)S(1)}, bf16[2,3072,128]{2,1,0:T(8,128)(2,1)S(1)}, u32[]{:S(2)}, u32[]{:S(2)}) collective-permute-start(bf16[2,3072,128]{2,1,0:T(8,128)(2,1)S(1)} %flip.1.refs_4_.refs_1_), channel_id=1, source_target_pairs={{0,3},{1,0},{2,1},{3,2},{4,7},{5,4},{6,5},{7,6},{8,11},{9,8},{10,9... | collective-permute-start | bytes 4718600 | tf_op jit(solution)/shard_map/ppermute | solution.py:42
  58.9 28.1 %collective-permute-start.18 = (bf16[2,3072,128]{2,1,0:T(8,128)(2,1)S(1)}, bf16[2,3072,128]{2,1,0:T(8,128)(2,1)S(1)}, u32[]{:S(2)}, u32[]{:S(2)}) collective-permute-start(bf16[2,3072,128]{2,1,0:T(8,128)(2,1)S(1)} %flip.1.refs_4_.refs_1_), channel_id=1, source_target_pairs={{0,1},{1,2},{2,3},{3,0},{4,5},{5,6},{6,7},{7,4},{8,9},{9,10},{10,1... | collective-permute-start | bytes 4718600 | tf_op jit(solution)/shard_map/ppermute | solution.py:42
  58.9 12.1 %collective-permute-start.14 = (bf16[64,3072]{1,0:T(8,128)(2,1)S(1)}, bf16[64,3072]{1,0:T(8,128)(2,1)S(1)}, u32[]{:S(2)}, u32[]{:S(2)}) collective-permute-start(bf16[64,3072]{1,0:T(8,128)(2,1)S(1)} %get-tuple-element.34), channel_id=1, source_target_pairs={{0,4},{1,5},{2,6},{3,7},{4,8},{5,9},{6,10},{7,11},{8,12},{9,13},{1... | collective-permute-start | bytes 1179656 | tf_op jit(solution)/shard_map/ppermute | solution.py:42
  60.5 13.3 %collective-permute-start.15 = (bf16[64,3072]{1,0:T(8,128)(2,1)S(1)}, bf16[64,3072]{1,0:T(8,128)(2,1)S(1)}, u32[]{:S(2)}, u32[]{:S(2)}) collective-permute-start(bf16[64,3072]{1,0:T(8,128)(2,1)S(1)} %get-tuple-element.35), channel_id=1, source_target_pairs={{0,12},{1,13},{2,14},{3,15},{4,0},{5,1},{6,2},{7,3},{8,4},{9,5},{1... | collective-permute-start | bytes 1179656 | tf_op jit(solution)/shard_map/ppermute | solution.py:42
  73.9 13.4 %collective-permute-start.16 = (bf16[32,3072]{1,0:T(8,128)(2,1)S(1)}, bf16[32,3072]{1,0:T(8,128)(2,1)S(1)}, u32[]{:S(2)}, u32[]{:S(2)}) collective-permute-start(bf16[32,3072]{1,0:T(8,128)(2,1)S(1)} %get-tuple-element.38), channel_id=1, source_target_pairs={{0,4},{1,5},{2,6},{3,7},{4,8},{5,9},{6,10},{7,11},{8,12},{9,13},{1... | collective-permute-start | bytes 589832 | tf_op jit(solution)/shard_map/ppermute | solution.py:42
  74.0 16.4 %collective-permute-start.17 = (bf16[32,3072]{1,0:T(8,128)(2,1)S(1)}, bf16[32,3072]{1,0:T(8,128)(2,1)S(1)}, u32[]{:S(2)}, u32[]{:S(2)}) collective-permute-start(bf16[32,3072]{1,0:T(8,128)(2,1)S(1)} %get-tuple-element.39), channel_id=1, source_target_pairs={{0,12},{1,13},{2,14},{3,15},{4,0},{5,1},{6,2},{7,3},{8,4},{9,5},{1... | collective-permute-start | bytes 589832 | tf_op jit(solution)/shard_map/ppermute | solution.py:42
  83.2 25.8 %collective-permute-start.25 = (bf16[1,3072,128]{2,1,0:T(8,128)(2,1)S(1)}, bf16[1,3072,128]{2,1,0:T(8,128)(2,1)S(1)}, u32[]{:S(2)}, u32[]{:S(2)}) collective-permute-start(bf16[1,3072,128]{2,1,0:T(8,128)(2,1)S(1)} %slice.83), channel_id=1, source_target_pairs={{0,3},{1,0},{2,1},{3,2},{4,7},{5,4},{6,5},{7,6},{8,11},{9,8},{10,9... | collective-permute-start | bytes 2359304 | tf_op jit(solution)/shard_map/ppermute | solution.py:42
  87.0 22.0 %collective-permute-start.24 = (bf16[1,3072,128]{2,1,0:T(8,128)(2,1)S(1)}, bf16[1,3072,128]{2,1,0:T(8,128)(2,1)S(1)}, u32[]{:S(2)}, u32[]{:S(2)}) collective-permute-start(bf16[1,3072,128]{2,1,0:T(8,128)(2,1)S(1)} %slice.82), channel_id=1, source_target_pairs={{0,1},{1,2},{2,3},{3,0},{4,5},{5,6},{6,7},{7,4},{8,9},{9,10},{10,1... | collective-permute-start | bytes 2359304 | tf_op jit(solution)/shard_map/ppermute | solution.py:42
  93.0 9.0 %collective-permute-start.20 = (bf16[64,3072]{1,0:T(8,128)(2,1)S(1)}, bf16[64,3072]{1,0:T(8,128)(2,1)S(1)}, u32[]{:S(2)}, u32[]{:S(2)}) collective-permute-start(bf16[64,3072]{1,0:T(8,128)(2,1)S(1)} %grad_pre.1.refs_0_), channel_id=1, source_target_pairs={{0,12},{1,13},{2,14},{3,15},{4,0},{5,1},{6,2},{7,3},{8,4},{9,5},{1... | collective-permute-start | bytes 1179656 | tf_op jit(solution)/shard_map/ppermute | solution.py:42
  109.2 12.8 %collective-permute-start.31 = (bf16[128,3072]{1,0:T(8,128)(2,1)S(1)}, bf16[128,3072]{1,0:T(8,128)(2,1)S(1)}, u32[]{:S(2)}, u32[]{:S(2)}) collective-permute-start(bf16[128,3072]{1,0:T(8,128)(2,1)S(1)} %get-tuple-element.45), channel_id=1, source_target_pairs={{0,3},{1,0},{2,1},{3,2},{4,7},{5,4},{6,5},{7,6},{8,11},{9,8},{10,9... | collective-permute-start | bytes 2359304 | tf_op jit(solution)/shard_map/ppermute | solution.py:42
  112.5 13.2 %collective-permute-start.32 = (bf16[128,3072]{1,0:T(8,128)(2,1)S(1)}, bf16[128,3072]{1,0:T(8,128)(2,1)S(1)}, u32[]{:S(2)}, u32[]{:S(2)}) collective-permute-start(bf16[128,3072]{1,0:T(8,128)(2,1)S(1)} %get-tuple-element.46), channel_id=1, source_target_pairs={{0,1},{1,2},{2,3},{3,0},{4,5},{5,6},{6,7},{7,4},{8,9},{9,10},{10,1... | collective-permute-start | bytes 2359304 | tf_op jit(solution)/shard_map/ppermute | solution.py:42
  112.5 21.6 %collective-permute-start.33 = (bf16[128,3072]{1,0:T(8,128)(2,1)S(1)}, bf16[128,3072]{1,0:T(8,128)(2,1)S(1)}, u32[]{:S(2)}, u32[]{:S(2)}) collective-permute-start(bf16[128,3072]{1,0:T(8,128)(2,1)S(1)} %get-tuple-element.45), channel_id=1, source_target_pairs={{0,1},{1,2},{2,3},{3,0},{4,5},{5,6},{6,7},{7,4},{8,9},{9,10},{10,1... | collective-permute-start | bytes 2359304 | tf_op jit(solution)/shard_map/ppermute | solution.py:42
  112.5 21.6 %collective-permute-start.30 = (bf16[128,3072]{1,0:T(8,128)(2,1)S(1)}, bf16[128,3072]{1,0:T(8,128)(2,1)S(1)}, u32[]{:S(2)}, u32[]{:S(2)}) collective-permute-start(bf16[128,3072]{1,0:T(8,128)(2,1)S(1)} %get-tuple-element.46), channel_id=1, source_target_pairs={{0,3},{1,0},{2,1},{3,2},{4,7},{5,4},{6,5},{7,6},{8,11},{9,8},{10,9... | collective-permute-start | bytes 2359304 | tf_op jit(solution)/shard_map/ppermute | solution.py:42
  122.0 16.9 %collective-permute-start.35 = (bf16[128,3072]{1,0:T(8,128)(2,1)S(1)}, bf16[128,3072]{1,0:T(8,128)(2,1)S(1)}, u32[]{:S(2)}, u32[]{:S(2)}) collective-permute-start(bf16[128,3072]{1,0:T(8,128)(2,1)S(1)} %collective-permute-done.31.refs_2_.refs_3_), channel_id=1, source_target_pairs={{0,3},{1,0},{2,1},{3,2},{4,7},{5,4},{6,5},{7,6},{8,11},{9,8},{10,9... | collective-permute-start | bytes 2359304 | tf_op jit(solution)/shard_map/ppermute | solution.py:42
  125.7 16.8 %collective-permute-start.34 = (bf16[128,3072]{1,0:T(8,128)(2,1)S(1)}, bf16[128,3072]{1,0:T(8,128)(2,1)S(1)}, u32[]{:S(2)}, u32[]{:S(2)}) collective-permute-start(bf16[128,3072]{1,0:T(8,128)(2,1)S(1)} %collective-permute-done.32.refs_3_.refs_6_), channel_id=1, source_target_pairs={{0,1},{1,2},{2,3},{3,0},{4,5},{5,6},{6,7},{7,4},{8,9},{9,10},{10,1... | collective-permute-start | bytes 2359304 | tf_op jit(solution)/shard_map/ppermute | solution.py:42
  146.7 8.4 %collective-permute-start.37 = (bf16[128,384]{1,0:T(8,128)(2,1)S(1)}, bf16[128,384]{1,0:T(8,128)(2,1)S(1)}, u32[]{:S(2)}, u32[]{:S(2)}) collective-permute-start(bf16[128,384]{1,0:T(8,128)(2,1)S(1)} %get-tuple-element.51), channel_id=1, source_target_pairs={{0,32},{16,48},{32,64},{48,80},{64,96},{80,112},{96,0},{112,16},{1... | collective-permute-start | bytes 294920 | tf_op jit(solution)/shard_map/ppermute | solution.py:55
  (22 other events, 148.0 us)

commit v5 on v3

--- a/solution.py
+++ b/solution.py
@@ -77,10 +77,10 @@
     )(*operands, *order)
 
 
-def each_block(count, body):
-    @pl.loop(0, count // WIDE)
+def each_block(count, body, wide=WIDE):
+    @pl.loop(0, count // wide)
     def _(i):
-        body(pl.ds(pl.multiple_of(i * WIDE, WIDE), WIDE))
+        body(pl.ds(pl.multiple_of(i * wide, wide), wide))
 
 
 SMEM = pl.BlockSpec(memory_space=pltpu.SMEM)
@@ -142,7 +142,7 @@
             out[:, cols] = total[at : at + out.shape[0]].astype(out.dtype)
             at += out.shape[0]
 
-    each_block(w.shape[0], body)
+    each_block(w.shape[0], body, 2 * WIDE)
 
 
 def back_rows(scaled, w_out, kinds, order=()):
@@ -287,7 +287,7 @@
         rows = jnp.concatenate([piece[:, cols] for piece in pieces], axis=0)
         out[:, cols] = (dot(flipped[...], rows, NN) * factor).astype(BF16)
 
-    each_block(out.shape[1], body)
+    each_block(out.shape[1], body, 2 * WIDE)
 
 
 def grad_w_in_all(flipped, pieces, factor):
@@ -318,7 +318,7 @@
         pieces = [p[k, cols, :] for p in (one, two, three, four, five) for k in range(p.shape[0])]
         out[cols, :] = (dot(jnp.concatenate(pieces, axis=1), scaled[...], NN) * factor).astype(BF16)
 
-    each_block(out.shape[0], body)
+    each_block(out.shape[0], body, 2 * WIDE)
 
 
 def grad_w_out_all(scaled, pieces, factor):

time: 155 us -> 154 us (level)
  Pallas kernels: 27.5 us -> 25.3 us
  waiting for transfers between devices: 64.7 us -> 66.3 us
    pallas_call x19, Pallas kernels: 27.5 us -> 25.3 us  [call(): pl.pallas_call(body, out_shape=outs, in_specs=[SMEM] * small + [VMEM] * (...]
  transfers between devices with their start and end apart: 40 -> 40, of which waited for: 20 -> 20; matrix products, arithmetic and copies ran while one was open for 1% -> 1% of each run, Pallas kernels for 14% -> 13%
where the time goes in v5:
time: 154 us
  waiting for transfers between devices  66.3 us (43%)
  starting transfers between devices  58.8 us (38%)
  Pallas kernels  25.3 us (16%)
  other arithmetic  2.3 us (1%)
    ppermute x28, waiting for transfers between devices, move(): return lax.ppermute(a, ('row', 'col'), pairs)  58.6 us
    ppermute x28, starting transfers between devices, move(): return lax.ppermute(a, ('row', 'col'), pairs)  43.8 us
    pallas_call x19, Pallas kernels, call(): pl.pallas_call(body, out_shape=outs, in_specs=[SMEM] * small + [VMEM] * (...  25.3 us
    ppermute x9, starting transfers between devices, move_x(): return lax.ppermute(a, 'row', pairs)  14.7 us
    ppermute x9, waiting for transfers between devices, move_x(): return lax.ppermute(a, 'row', pairs)  5.97 us
  transfers between devices with their start and end apart: 40, of which 20 were waited for; matrix products, arithmetic and copies ran while one was open for 1% of the time, Pallas kernels for 13%

profile of v5, /device:TPU:24, one launch (start us, length us, event | category | flops | bytes accessed | tf_op | source)
XLA Modules:
  0.0 154.1 jit_solution(18342883637391176085)
XLA Ops:
  0.7 3.1 %collective-permute-start.1 = (bf16[128,384]{1,0:T(8,128)(2,1)}, bf16[128,384]{1,0:T(8,128)(2,1)S(1)}, u32[]{:S(2)}, u32[]{:S(2)}) collective-permute-start(bf16[128,384]{1,0:T(8,128)(2,1)} %refs_0_.3), channel_id=1, source_target_pairs={{0,64},{16,80},{32,96},{48,112},{64,0},{80,16},{96,32},{112,48},{1... | collective-permute-start | bytes 294920 | tf_op jit(solution)/shard_map/ppermute | solution.py:55
  12.5 3.7 %collective-permute-done.5.refs_5_.refs_6_.refs_1_ = bf16[64,3072]{1,0:T(8,128)(2,1)S(1)} collective-permute-done((bf16[64,3072]{1,0:T(8,128)(2,1)S(1)}, bf16[64,3072]{1,0:T(8,128)(2,1)S(1)}, u32[]{:S(2)}, u32[]{:S(2)}) %collective-permute-start.5) | collective-permute-done | bytes 393248 | tf_op jit(solution)/shard_map/ppermute | solution.py:42
  22.7 3.0 %back.2 = (bf16[128,3072]{1,0:T(8,128)(2,1)S(1)}, f32[128,3072]{1,0:T(8,128)S(1)}, f32[256,3072]{1,0:T(8,128)S(1)}, f32[128,3072]{1,0:T(8,128)S(1)}, bf16[128,3072]{1,0:T(8,128)(2,1)S(1)}) custom-call(bf16[768,384]{1,0:T(8,128)(2,1)S(1)} %pad_maximum_fusion.refs_0_, bf16[3072,384]{1,0:T(8,128)(2,1)S(1)} %copy-done), custom_call_target="tpu_custom_call" | custom-call | tf_op jit(solution)/shard_map/back/pallas_call | solution.py:68
  25.9 3.2 %collective-permute-start.7 = (bf16[128,3072]{1,0:T(8,128)(2,1)S(1)}, bf16[128,3072]{1,0:T(8,128)(2,1)S(1)}, u32[]{:S(2)}, u32[]{:S(2)}) collective-permute-start(bf16[128,3072]{1,0:T(8,128)(2,1)S(1)} %get-tuple-element.26), channel_id=1, source_target_pairs={{0,3},{1,0},{2,1},{3,2},{4,7},{5,4},{6,5},{7,6},{8,11},{9,8},{10,9... | collective-permute-start | bytes 2359304 | tf_op jit(solution)/shard_map/ppermute | solution.py:42
  29.1 3.4 %collective-permute-done.8.refs_2_ = bf16[128,3072]{1,0:T(8,128)(2,1)S(1)} collective-permute-done((bf16[128,3072]{1,0:T(8,128)(2,1)S(1)}, bf16[128,3072]{1,0:T(8,128)(2,1)S(1)}, u32[]{:S(2)}, u32[]{:S(2)}) %collective-permute-start.8) | collective-permute-done | bytes 786464 | tf_op jit(solution)/shard_map/ppermute | solution.py:42
  36.4 9.0 %collective-permute-done.13.refs_8_.refs_3_ = bf16[32,3072]{1,0:T(8,128)(2,1)S(1)} collective-permute-done((bf16[32,3072]{1,0:T(8,128)(2,1)S(1)}, bf16[32,3072]{1,0:T(8,128)(2,1)S(1)}, u32[]{:S(2)}, u32[]{:S(2)}) %collective-permute-start.13) | collective-permute-done | bytes 196640 | tf_op jit(solution)/shard_map/ppermute | solution.py:42
  47.5 3.6 %collective-permute-done.12.refs_7_.refs_2_ = bf16[32,3072]{1,0:T(8,128)(2,1)S(1)} collective-permute-done((bf16[32,3072]{1,0:T(8,128)(2,1)S(1)}, bf16[32,3072]{1,0:T(8,128)(2,1)S(1)}, u32[]{:S(2)}, u32[]{:S(2)}) %collective-permute-start.12) | collective-permute-done | bytes 196640 | tf_op jit(solution)/shard_map/ppermute | solution.py:42
  52.7 3.4 %collective-permute-start.19 = (bf16[2,3072,128]{2,1,0:T(8,128)(2,1)S(1)}, bf16[2,3072,128]{2,1,0:T(8,128)(2,1)S(1)}, u32[]{:S(2)}, u32[]{:S(2)}) collective-permute-start(bf16[2,3072,128]{2,1,0:T(8,128)(2,1)S(1)} %flip.1.refs_4_.refs_1_), channel_id=1, source_target_pairs={{0,3},{1,0},{2,1},{3,2},{4,7},{5,4},{6,5},{7,6},{8,11},{9,8},{10,9... | collective-permute-start | bytes 4718600 | tf_op jit(solution)/shard_map/ppermute | solution.py:42
  56.1 3.2 %collective-permute-start.14 = (bf16[64,3072]{1,0:T(8,128)(2,1)S(1)}, bf16[64,3072]{1,0:T(8,128)(2,1)S(1)}, u32[]{:S(2)}, u32[]{:S(2)}) collective-permute-start(bf16[64,3072]{1,0:T(8,128)(2,1)S(1)} %get-tuple-element.34), channel_id=1, source_target_pairs={{0,4},{1,5},{2,6},{3,7},{4,8},{5,9},{6,10},{7,11},{8,12},{9,13},{1... | collective-permute-start | bytes 1179656 | tf_op jit(solution)/shard_map/ppermute | solution.py:42
  59.3 9.6 %collective-permute-done.14.refs_1_ = bf16[64,3072]{1,0:T(8,128)(2,1)S(1)} collective-permute-done((bf16[64,3072]{1,0:T(8,128)(2,1)S(1)}, bf16[64,3072]{1,0:T(8,128)(2,1)S(1)}, u32[]{:S(2)}, u32[]{:S(2)}) %collective-permute-start.14) | collective-permute-done | bytes 393248 | tf_op jit(solution)/shard_map/ppermute | solution.py:42
  68.9 3.7 %collective-permute-done.15.refs_2_ = bf16[64,3072]{1,0:T(8,128)(2,1)S(1)} collective-permute-done((bf16[64,3072]{1,0:T(8,128)(2,1)S(1)}, bf16[64,3072]{1,0:T(8,128)(2,1)S(1)}, u32[]{:S(2)}, u32[]{:S(2)}) %collective-permute-start.15) | collective-permute-done | bytes 393248 | tf_op jit(solution)/shard_map/ppermute | solution.py:42
  74.8 5.5 %collective-permute-done.19.refs_7_.refs_2_ = bf16[2,3072,128]{2,1,0:T(8,128)(2,1)S(1)} collective-permute-done((bf16[2,3072,128]{2,1,0:T(8,128)(2,1)S(1)}, bf16[2,3072,128]{2,1,0:T(8,128)(2,1)S(1)}, u32[]{:S(2)}, u32[]{:S(2)}) %collective-permute-start.19) | collective-permute-done | bytes 1572896 | tf_op jit(solution)/shard_map/ppermute | solution.py:42
  80.4 3.8 %collective-permute-start.25 = (bf16[1,3072,128]{2,1,0:T(8,128)(2,1)S(1)}, bf16[1,3072,128]{2,1,0:T(8,128)(2,1)S(1)}, u32[]{:S(2)}, u32[]{:S(2)}) collective-permute-start(bf16[1,3072,128]{2,1,0:T(8,128)(2,1)S(1)} %slice.83), channel_id=1, source_target_pairs={{0,3},{1,0},{2,1},{3,2},{4,7},{5,4},{6,5},{7,6},{8,11},{9,8},{10,9... | collective-permute-start | bytes 2359304 | tf_op jit(solution)/shard_map/ppermute | solution.py:42
  85.0 3.2 %collective-permute-start.27 = (bf16[128,384]{1,0:T(8,128)(2,1)S(1)}, bf16[128,384]{1,0:T(8,128)(2,1)S(1)}, u32[]{:S(2)}, u32[]{:S(2)}) collective-permute-start(bf16[128,384]{1,0:T(8,128)(2,1)S(1)} %hold.1.refs_0_), channel_id=1, source_target_pairs={{0,64},{16,80},{32,96},{48,112},{64,0},{80,16},{96,32},{112,48},{1... | collective-permute-start | bytes 294920 | tf_op jit(solution)/shard_map/ppermute | solution.py:55
  102.8 3.8 %collective-permute-done.23.refs_3_ = bf16[32,3072]{1,0:T(8,128)(2,1)S(1)} collective-permute-done((bf16[32,3072]{1,0:T(8,128)(2,1)S(1)}, bf16[32,3072]{1,0:T(8,128)(2,1)S(1)}, u32[]{:S(2)}, u32[]{:S(2)}) %collective-permute-start.23) | collective-permute-done | bytes 196640 | tf_op jit(solution)/shard_map/ppermute | solution.py:42
  106.8 3.0 %collective-permute-start.31 = (bf16[128,3072]{1,0:T(8,128)(2,1)S(1)}, bf16[128,3072]{1,0:T(8,128)(2,1)S(1)}, u32[]{:S(2)}, u32[]{:S(2)}) collective-permute-start(bf16[128,3072]{1,0:T(8,128)(2,1)S(1)} %get-tuple-element.45), channel_id=1, source_target_pairs={{0,3},{1,0},{2,1},{3,2},{4,7},{5,4},{6,5},{7,6},{8,11},{9,8},{10,9... | collective-permute-start | bytes 2359304 | tf_op jit(solution)/shard_map/ppermute | solution.py:42
  109.8 3.3 %collective-permute-start.30 = (bf16[128,3072]{1,0:T(8,128)(2,1)S(1)}, bf16[128,3072]{1,0:T(8,128)(2,1)S(1)}, u32[]{:S(2)}, u32[]{:S(2)}) collective-permute-start(bf16[128,3072]{1,0:T(8,128)(2,1)S(1)} %get-tuple-element.46), channel_id=1, source_target_pairs={{0,3},{1,0},{2,1},{3,2},{4,7},{5,4},{6,5},{7,6},{8,11},{9,8},{10,9... | collective-permute-start | bytes 2359304 | tf_op jit(solution)/shard_map/ppermute | solution.py:42
  113.1 6.2 %collective-permute-done.31.refs_2_.refs_3_ = bf16[128,3072]{1,0:T(8,128)(2,1)S(1)} collective-permute-done((bf16[128,3072]{1,0:T(8,128)(2,1)S(1)}, bf16[128,3072]{1,0:T(8,128)(2,1)S(1)}, u32[]{:S(2)}, u32[]{:S(2)}) %collective-permute-start.31) | collective-permute-done | bytes 786464 | tf_op jit(solution)/shard_map/ppermute | solution.py:42
  119.3 3.7 %collective-permute-start.35 = (bf16[128,3072]{1,0:T(8,128)(2,1)S(1)}, bf16[128,3072]{1,0:T(8,128)(2,1)S(1)}, u32[]{:S(2)}, u32[]{:S(2)}) collective-permute-start(bf16[128,3072]{1,0:T(8,128)(2,1)S(1)} %collective-permute-done.31.refs_2_.refs_3_), channel_id=1, source_target_pairs={{0,3},{1,0},{2,1},{3,2},{4,7},{5,4},{6,5},{7,6},{8,11},{9,8},{10,9... | collective-permute-start | bytes 2359304 | tf_op jit(solution)/shard_map/ppermute | solution.py:42
  123.0 5.1 %grad_w_out.1.refs_4_ = bf16[3072,384]{1,0:T(8,128)(2,1)} custom-call(bf16[1024,384]{1,0:T(8,128)(2,1)S(1)} %scaled.1.refs_0_, bf16[2,3072,128]{2,1,0:T(8,128)(2,1)S(1)} %flip.1.refs_4_.refs_1_, bf16[2,3072,128]{2,1,0:T(8,128)(2,1)S(1)} %collective-permute-done.19.refs_7_.refs_2_, bf16[1,3072,128]{2,1,0:T(8,128)(2,1)S(1)} %collective-permute-done.24.refs_5_.refs_3_, ...), custom_call_target="tpu_custom_call" | custom-call | tf_op jit(solution)/shard_map/grad_w_out/pallas_call | solution.py:68
  128.1 3.3 %collective-permute-done.33.refs_4_.refs_7_ = bf16[128,3072]{1,0:T(8,128)(2,1)S(1)} collective-permute-done((bf16[128,3072]{1,0:T(8,128)(2,1)S(1)}, bf16[128,3072]{1,0:T(8,128)(2,1)S(1)}, u32[]{:S(2)}, u32[]{:S(2)}) %collective-permute-start.33) | collective-permute-done | bytes 786464 | tf_op jit(solution)/shard_map/ppermute | solution.py:42
  131.4 4.2 %grad_inputs_near.1.refs_3_.refs_1_ = f32[768,384]{1,0:T(8,128)S(1)} custom-call(bf16[256,3072]{1,0:T(8,128)(2,1)S(1)} %stack.25.refs_0_.refs_1_, bf16[128,3072]{1,0:T(8,128)(2,1)S(1)} %collective-permute-done.30.refs_1_.refs_2_, bf16[128,3072]{1,0:T(8,128)(2,1)S(1)} %collective-permute-done.31.refs_2_.refs_3_, ...), custom_call_target="tpu_custom_call" | custom-call | tf_op jit(solution)/shard_map/grad_inputs_near/pallas_call | solution.py:68
  136.2 3.7 %collective-permute-done.34.refs_0_.refs_4_ = bf16[128,3072]{1,0:T(8,128)(2,1)S(1)} collective-permute-done((bf16[128,3072]{1,0:T(8,128)(2,1)S(1)}, bf16[128,3072]{1,0:T(8,128)(2,1)S(1)}, u32[]{:S(2)}, u32[]{:S(2)}) %collective-permute-start.34) | collective-permute-done | bytes 786464 | tf_op jit(solution)/shard_map/ppermute | solution.py:42
  147.8 4.4 %grad_w_in.1 = bf16[384,3072]{1,0:T(8,128)(2,1)} custom-call(bf16[384,1024]{1,0:T(8,128)(2,1)S(1)} %inputs.1.refs_7_.refs_0_, bf16[256,3072]{1,0:T(8,128)(2,1)S(1)} %stack.25.refs_0_.refs_1_, bf16[128,3072]{1,0:T(8,128)(2,1)S(1)} %collective-permute-done.30.refs_1_.refs_2_, bf16[128,3072]{1,0:T(8,128)(2,1)S(1)} %collective-permute-done.31.refs_2_.refs_3_, ...), custom_call_target="tpu_custom_call" | custom-call | tf_op jit(solution)/shard_map/grad_w_in/pallas_call | solution.py:68
  (104 shorter events, 50.9 us)
Async XLA Ops:
  0.7 9.8 %collective-permute-start.1 = (bf16[128,384]{1,0:T(8,128)(2,1)}, bf16[128,384]{1,0:T(8,128)(2,1)S(1)}, u32[]{:S(2)}, u32[]{:S(2)}) collective-permute-start(bf16[128,384]{1,0:T(8,128)(2,1)} %refs_0_.3), channel_id=1, source_target_pairs={{0,64},{16,80},{32,96},{48,112},{64,0},{80,16},{96,32},{112,48},{1... | collective-permute-start | bytes 294920 | tf_op jit(solution)/shard_map/ppermute | solution.py:55
  7.2 9.1 %collective-permute-start.5 = (bf16[64,3072]{1,0:T(8,128)(2,1)S(1)}, bf16[64,3072]{1,0:T(8,128)(2,1)S(1)}, u32[]{:S(2)}, u32[]{:S(2)}) collective-permute-start(bf16[64,3072]{1,0:T(8,128)(2,1)S(1)} %get-tuple-element.23.refs_5_.refs_0_), channel_id=1, source_target_pairs={{0,12},{1,13},{2,14},{3,15},{4,0},{5,1},{6,2},{7,3},{8,4},{9,5},{1... | collective-permute-start | bytes 1179656 | tf_op jit(solution)/shard_map/ppermute | solution.py:42
  18.4 14.1 %collective-permute-start.8 = (bf16[128,3072]{1,0:T(8,128)(2,1)S(1)}, bf16[128,3072]{1,0:T(8,128)(2,1)S(1)}, u32[]{:S(2)}, u32[]{:S(2)}) collective-permute-start(bf16[128,3072]{1,0:T(8,128)(2,1)S(1)} %get-tuple-element.29), channel_id=1, source_target_pairs={{0,1},{1,2},{2,3},{3,0},{4,5},{5,6},{6,7},{7,4},{8,9},{9,10},{10,1... | collective-permute-start | bytes 2359304 | tf_op jit(solution)/shard_map/ppermute | solution.py:42
  20.4 12.1 %collective-permute-start.9 = (bf16[128,3072]{1,0:T(8,128)(2,1)S(1)}, bf16[128,3072]{1,0:T(8,128)(2,1)S(1)}, u32[]{:S(2)}, u32[]{:S(2)}) collective-permute-start(bf16[128,3072]{1,0:T(8,128)(2,1)S(1)} %get-tuple-element.30), channel_id=1, source_target_pairs={{0,3},{1,0},{2,1},{3,2},{4,7},{5,4},{6,5},{7,6},{8,11},{9,8},{10,9... | collective-permute-start | bytes 2359304 | tf_op jit(solution)/shard_map/ppermute | solution.py:42
  25.8 25.3 %collective-permute-start.6 = (bf16[128,3072]{1,0:T(8,128)(2,1)S(1)}, bf16[128,3072]{1,0:T(8,128)(2,1)S(1)}, u32[]{:S(2)}, u32[]{:S(2)}) collective-permute-start(bf16[128,3072]{1,0:T(8,128)(2,1)S(1)} %get-tuple-element.25), channel_id=1, source_target_pairs={{0,1},{1,2},{2,3},{3,0},{4,5},{5,6},{6,7},{7,4},{8,9},{9,10},{10,1... | collective-permute-start | bytes 2359304 | tf_op jit(solution)/shard_map/ppermute | solution.py:42
  25.9 25.3 %collective-permute-start.7 = (bf16[128,3072]{1,0:T(8,128)(2,1)S(1)}, bf16[128,3072]{1,0:T(8,128)(2,1)S(1)}, u32[]{:S(2)}, u32[]{:S(2)}) collective-permute-start(bf16[128,3072]{1,0:T(8,128)(2,1)S(1)} %get-tuple-element.26), channel_id=1, source_target_pairs={{0,3},{1,0},{2,1},{3,2},{4,7},{5,4},{6,5},{7,6},{8,11},{9,8},{10,9... | collective-permute-start | bytes 2359304 | tf_op jit(solution)/shard_map/ppermute | solution.py:42
  32.8 18.6 %collective-permute-start.10 = (bf16[128,3072]{1,0:T(8,128)(2,1)S(1)}, bf16[128,3072]{1,0:T(8,128)(2,1)S(1)}, u32[]{:S(2)}, u32[]{:S(2)}) collective-permute-start(bf16[128,3072]{1,0:T(8,128)(2,1)S(1)} %get-tuple-element.31), channel_id=1, source_target_pairs={{0,1},{1,2},{2,3},{3,0},{4,5},{5,6},{6,7},{7,4},{8,9},{9,10},{10,1... | collective-permute-start | bytes 2359304 | tf_op jit(solution)/shard_map/ppermute | solution.py:42
  34.7 16.7 %collective-permute-start.11 = (bf16[128,3072]{1,0:T(8,128)(2,1)S(1)}, bf16[128,3072]{1,0:T(8,128)(2,1)S(1)}, u32[]{:S(2)}, u32[]{:S(2)}) collective-permute-start(bf16[128,3072]{1,0:T(8,128)(2,1)S(1)} %get-tuple-element.32), channel_id=1, source_target_pairs={{0,3},{1,0},{2,1},{3,2},{4,7},{5,4},{6,5},{7,6},{8,11},{9,8},{10,9... | collective-permute-start | bytes 2359304 | tf_op jit(solution)/shard_map/ppermute | solution.py:42
  36.3 9.1 %collective-permute-start.13 = (bf16[32,3072]{1,0:T(8,128)(2,1)S(1)}, bf16[32,3072]{1,0:T(8,128)(2,1)S(1)}, u32[]{:S(2)}, u32[]{:S(2)}) collective-permute-start(bf16[32,3072]{1,0:T(8,128)(2,1)S(1)} %slice.77), channel_id=1, source_target_pairs={{0,12},{1,13},{2,14},{3,15},{4,0},{5,1},{6,2},{7,3},{8,4},{9,5},{1... | collective-permute-start | bytes 589832 | tf_op jit(solution)/shard_map/ppermute | solution.py:42
  52.7 27.6 %collective-permute-start.19 = (bf16[2,3072,128]{2,1,0:T(8,128)(2,1)S(1)}, bf16[2,3072,128]{2,1,0:T(8,128)(2,1)S(1)}, u32[]{:S(2)}, u32[]{:S(2)}) collective-permute-start(bf16[2,3072,128]{2,1,0:T(8,128)(2,1)S(1)} %flip.1.refs_4_.refs_1_), channel_id=1, source_target_pairs={{0,3},{1,0},{2,1},{3,2},{4,7},{5,4},{6,5},{7,6},{8,11},{9,8},{10,9... | collective-permute-start | bytes 4718600 | tf_op jit(solution)/shard_map/ppermute | solution.py:42
  56.1 28.1 %collective-permute-start.18 = (bf16[2,3072,128]{2,1,0:T(8,128)(2,1)S(1)}, bf16[2,3072,128]{2,1,0:T(8,128)(2,1)S(1)}, u32[]{:S(2)}, u32[]{:S(2)}) collective-permute-start(bf16[2,3072,128]{2,1,0:T(8,128)(2,1)S(1)} %flip.1.refs_4_.refs_1_), channel_id=1, source_target_pairs={{0,1},{1,2},{2,3},{3,0},{4,5},{5,6},{6,7},{7,4},{8,9},{9,10},{10,1... | collective-permute-start | bytes 4718600 | tf_op jit(solution)/shard_map/ppermute | solution.py:42
  56.1 12.8 %collective-permute-start.14 = (bf16[64,3072]{1,0:T(8,128)(2,1)S(1)}, bf16[64,3072]{1,0:T(8,128)(2,1)S(1)}, u32[]{:S(2)}, u32[]{:S(2)}) collective-permute-start(bf16[64,3072]{1,0:T(8,128)(2,1)S(1)} %get-tuple-element.34), channel_id=1, source_target_pairs={{0,4},{1,5},{2,6},{3,7},{4,8},{5,9},{6,10},{7,11},{8,12},{9,13},{1... | collective-permute-start | bytes 1179656 | tf_op jit(solution)/shard_map/ppermute | solution.py:42
  59.3 13.3 %collective-permute-start.15 = (bf16[64,3072]{1,0:T(8,128)(2,1)S(1)}, bf16[64,3072]{1,0:T(8,128)(2,1)S(1)}, u32[]{:S(2)}, u32[]{:S(2)}) collective-permute-start(bf16[64,3072]{1,0:T(8,128)(2,1)S(1)} %get-tuple-element.35), channel_id=1, source_target_pairs={{0,12},{1,13},{2,14},{3,15},{4,0},{5,1},{6,2},{7,3},{8,4},{9,5},{1... | collective-permute-start | bytes 1179656 | tf_op jit(solution)/shard_map/ppermute | solution.py:42
  72.7 12.3 %collective-permute-start.16 = (bf16[32,3072]{1,0:T(8,128)(2,1)S(1)}, bf16[32,3072]{1,0:T(8,128)(2,1)S(1)}, u32[]{:S(2)}, u32[]{:S(2)}) collective-permute-start(bf16[32,3072]{1,0:T(8,128)(2,1)S(1)} %get-tuple-element.38), channel_id=1, source_target_pairs={{0,4},{1,5},{2,6},{3,7},{4,8},{5,9},{6,10},{7,11},{8,12},{9,13},{1... | collective-permute-start | bytes 589832 | tf_op jit(solution)/shard_map/ppermute | solution.py:42
  72.8 15.4 %collective-permute-start.17 = (bf16[32,3072]{1,0:T(8,128)(2,1)S(1)}, bf16[32,3072]{1,0:T(8,128)(2,1)S(1)}, u32[]{:S(2)}, u32[]{:S(2)}) collective-permute-start(bf16[32,3072]{1,0:T(8,128)(2,1)S(1)} %get-tuple-element.39), channel_id=1, source_target_pairs={{0,12},{1,13},{2,14},{3,15},{4,0},{5,1},{6,2},{7,3},{8,4},{9,5},{1... | collective-permute-start | bytes 589832 | tf_op jit(solution)/shard_map/ppermute | solution.py:42
  80.4 26.2 %collective-permute-start.25 = (bf16[1,3072,128]{2,1,0:T(8,128)(2,1)S(1)}, bf16[1,3072,128]{2,1,0:T(8,128)(2,1)S(1)}, u32[]{:S(2)}, u32[]{:S(2)}) collective-permute-start(bf16[1,3072,128]{2,1,0:T(8,128)(2,1)S(1)} %slice.83), channel_id=1, source_target_pairs={{0,3},{1,0},{2,1},{3,2},{4,7},{5,4},{6,5},{7,6},{8,11},{9,8},{10,9... | collective-permute-start | bytes 2359304 | tf_op jit(solution)/shard_map/ppermute | solution.py:42
  84.2 22.4 %collective-permute-start.24 = (bf16[1,3072,128]{2,1,0:T(8,128)(2,1)S(1)}, bf16[1,3072,128]{2,1,0:T(8,128)(2,1)S(1)}, u32[]{:S(2)}, u32[]{:S(2)}) collective-permute-start(bf16[1,3072,128]{2,1,0:T(8,128)(2,1)S(1)} %slice.82), channel_id=1, source_target_pairs={{0,1},{1,2},{2,3},{3,0},{4,5},{5,6},{6,7},{7,4},{8,9},{9,10},{10,1... | collective-permute-start | bytes 2359304 | tf_op jit(solution)/shard_map/ppermute | solution.py:42
  90.4 9.2 %collective-permute-start.20 = (bf16[64,3072]{1,0:T(8,128)(2,1)S(1)}, bf16[64,3072]{1,0:T(8,128)(2,1)S(1)}, u32[]{:S(2)}, u32[]{:S(2)}) collective-permute-start(bf16[64,3072]{1,0:T(8,128)(2,1)S(1)} %grad_pre.1.refs_0_), channel_id=1, source_target_pairs={{0,12},{1,13},{2,14},{3,15},{4,0},{5,1},{6,2},{7,3},{8,4},{9,5},{1... | collective-permute-start | bytes 1179656 | tf_op jit(solution)/shard_map/ppermute | solution.py:42
  106.8 12.5 %collective-permute-start.31 = (bf16[128,3072]{1,0:T(8,128)(2,1)S(1)}, bf16[128,3072]{1,0:T(8,128)(2,1)S(1)}, u32[]{:S(2)}, u32[]{:S(2)}) collective-permute-start(bf16[128,3072]{1,0:T(8,128)(2,1)S(1)} %get-tuple-element.45), channel_id=1, source_target_pairs={{0,3},{1,0},{2,1},{3,2},{4,7},{5,4},{6,5},{7,6},{8,11},{9,8},{10,9... | collective-permute-start | bytes 2359304 | tf_op jit(solution)/shard_map/ppermute | solution.py:42
  109.8 13.2 %collective-permute-start.32 = (bf16[128,3072]{1,0:T(8,128)(2,1)S(1)}, bf16[128,3072]{1,0:T(8,128)(2,1)S(1)}, u32[]{:S(2)}, u32[]{:S(2)}) collective-permute-start(bf16[128,3072]{1,0:T(8,128)(2,1)S(1)} %get-tuple-element.46), channel_id=1, source_target_pairs={{0,1},{1,2},{2,3},{3,0},{4,5},{5,6},{6,7},{7,4},{8,9},{9,10},{10,1... | collective-permute-start | bytes 2359304 | tf_op jit(solution)/shard_map/ppermute | solution.py:42
  109.8 21.6 %collective-permute-start.33 = (bf16[128,3072]{1,0:T(8,128)(2,1)S(1)}, bf16[128,3072]{1,0:T(8,128)(2,1)S(1)}, u32[]{:S(2)}, u32[]{:S(2)}) collective-permute-start(bf16[128,3072]{1,0:T(8,128)(2,1)S(1)} %get-tuple-element.45), channel_id=1, source_target_pairs={{0,1},{1,2},{2,3},{3,0},{4,5},{5,6},{6,7},{7,4},{8,9},{9,10},{10,1... | collective-permute-start | bytes 2359304 | tf_op jit(solution)/shard_map/ppermute | solution.py:42
  109.8 21.6 %collective-permute-start.30 = (bf16[128,3072]{1,0:T(8,128)(2,1)S(1)}, bf16[128,3072]{1,0:T(8,128)(2,1)S(1)}, u32[]{:S(2)}, u32[]{:S(2)}) collective-permute-start(bf16[128,3072]{1,0:T(8,128)(2,1)S(1)} %get-tuple-element.46), channel_id=1, source_target_pairs={{0,3},{1,0},{2,1},{3,2},{4,7},{5,4},{6,5},{7,6},{8,11},{9,8},{10,9... | collective-permute-start | bytes 2359304 | tf_op jit(solution)/shard_map/ppermute | solution.py:42
  119.3 16.9 %collective-permute-start.35 = (bf16[128,3072]{1,0:T(8,128)(2,1)S(1)}, bf16[128,3072]{1,0:T(8,128)(2,1)S(1)}, u32[]{:S(2)}, u32[]{:S(2)}) collective-permute-start(bf16[128,3072]{1,0:T(8,128)(2,1)S(1)} %collective-permute-done.31.refs_2_.refs_3_), channel_id=1, source_target_pairs={{0,3},{1,0},{2,1},{3,2},{4,7},{5,4},{6,5},{7,6},{8,11},{9,8},{10,9... | collective-permute-start | bytes 2359304 | tf_op jit(solution)/shard_map/ppermute | solution.py:42
  123.0 16.8 %collective-permute-start.34 = (bf16[128,3072]{1,0:T(8,128)(2,1)S(1)}, bf16[128,3072]{1,0:T(8,128)(2,1)S(1)}, u32[]{:S(2)}, u32[]{:S(2)}) collective-permute-start(bf16[128,3072]{1,0:T(8,128)(2,1)S(1)} %collective-permute-done.32.refs_3_.refs_6_), channel_id=1, source_target_pairs={{0,1},{1,2},{2,3},{3,0},{4,5},{5,6},{6,7},{7,4},{8,9},{9,10},{10,1... | collective-permute-start | bytes 2359304 | tf_op jit(solution)/shard_map/ppermute | solution.py:42
  (22 other events, 151.5 us)
